TPU v7x, 128 devices: a whole 4x4x4 slice. The times are simulated.
128 devices in a mesh: rows: 8 (over x, z_hi), cols: 16 (over y, z_lo, core).
Axes of the slice: x: 4, y: 4, z: 4 (z_hi: 2, z_lo: 2; z = z_hi * 2 + z_lo), core: 2. Of those that a mesh axis runs over, the one named last changes fastest.
Arguments:
- grid_token_states: bfloat16 [64, 256, 512], P('rows', 'cols'), may hold values from -6 to 6
- upstream_gradient: bfloat16 [64, 256, 512], P('rows', 'cols'), may hold values from -6 to 6
- noise_level_step: int32 [1], replicated, may hold values from 0 to 999
- picture_category_label: int32 [1], replicated, may hold values from 0 to 999
- category_gain_offset: bfloat16 [1000, 512], replicated, may hold values from -2 to 2
- noise_level_gain_matrix: bfloat16 [256, 512], replicated, may hold values from -0.375 to 0.375
- attention_input_matrix: bfloat16 [512, 1536], replicated, may hold values from -0.25 to 0.25
- final_projection_matrix: bfloat16 [512, 512], replicated, may hold values from -0.25 to 0.25
- cosine_logit_gain: float32 [8], replicated, may hold values from 2 to 160, as said below
Outputs:
- output: bfloat16 [64, 256, 512], P('rows', 'cols')
- grad_latent: bfloat16 [64, 256, 512], P('rows', 'cols')
- qkv_grad: float32 [512, 1536], replicated
- out_grad: float32 [512, 512], replicated
Inputs may be any that keep to these rules, and one draw needn't show every extreme that they name: `cosine_logit_gain`: per-head score scale.
All inputs are finite; a program needn't handle non-finite values.
Results may differ from a plain program's by a relative error of at most 0.024.
The roundings to bfloat16 on the way count: a program that leaves them out, or rounds other values in their place, can miss the bound.
Values may be sent and summed in bfloat16 or wider, within the bound.
No kernel may reach another device: no remote copies, remote signals or barrier semaphores. Data moves between devices by JAX's collectives and lax.ppermute only.
A program may use at most 192 MiB of HBM per device.

v0:
```python
import math

import jax
import jax.numpy as jnp
from jax import lax
from jax.sharding import PartitionSpec as P

HEADS = 8
HEAD = 64


def with_halo(block, sides, width):
    for axis, dim in sides:
        count = lax.axis_size(axis)
        forward = [(i, i + 1) for i in range(count - 1)]
        backward = [(target, source) for source, target in forward]
        low = lax.ppermute(
            lax.slice_in_dim(block, block.shape[dim] - width, None, axis=dim), axis, forward
        )
        high = lax.ppermute(lax.slice_in_dim(block, 0, width, axis=dim), axis, backward)
        block = jnp.concatenate([low, block, high], axis=dim)
    return block


def passed_along(value, axis, by):
    length = lax.axis_size(axis)
    pairs = [(i, i + by) for i in range(length) if 0 <= i + by < length]
    return lax.ppermute(value, axis, pairs)


def cond_scale(noise_level_step, class_row, noise_level_gain_matrix):
    half_freqs = noise_level_gain_matrix.shape[0] // 2
    steps_idx = jnp.arange(half_freqs, dtype=jnp.float32)
    freq_rates = 2.0 * math.pi * jnp.exp(steps_idx * (math.log(64.0) / half_freqs))
    angles = noise_level_step[0].astype(jnp.float32) * 0.001 * freq_rates
    features = jnp.concatenate([jnp.cos(angles), jnp.sin(angles)]).astype(jnp.bfloat16)
    shifted = jnp.dot(
        features[None, :], noise_level_gain_matrix, preferred_element_type=jnp.float32
    )[0]
    return 1.0 + class_row + shifted


def normalize(content_vector_lines, scale_vec):
    return (
        content_vector_lines
        * lax.rsqrt(
            jnp.mean(content_vector_lines * content_vector_lines, -1, keepdims=True) + 1e-06
        )
        * scale_vec
    )


def key_values(raw_kv):
    half_width = raw_kv.shape[-1] // 2
    lead_shape = raw_kv.shape[:-1]
    key_part = raw_kv[..., :half_width].reshape(lead_shape + (HEADS, HEAD))
    key_part = key_part * lax.rsqrt(jnp.sum(key_part * key_part, -1, keepdims=True) + 1e-06)
    return jnp.concatenate(
        [key_part.reshape(lead_shape + (half_width,)), raw_kv[..., half_width:]], -1
    )


def split_per_attention_group(final_mapped_result, cosine_logit_gain):
    model_width = final_mapped_result.shape[-1] // 3
    lead_shape = final_mapped_result.shape[:-1]
    probe_vector_portion = final_mapped_result[..., :model_width].reshape(
        lead_shape + (HEADS, HEAD)
    )
    probe_vector_portion = probe_vector_portion * lax.rsqrt(
        jnp.sum(probe_vector_portion * probe_vector_portion, -1, keepdims=True) + 1e-06
    )
    probe_vector_portion = probe_vector_portion * cosine_logit_gain[:, None]
    return (
        probe_vector_portion.reshape(lead_shape + (model_width,)),
        key_values(final_mapped_result[..., model_width:]),
    )


def attend(query_in, keys_in, inside):
    nrows, ncols = (query_in.shape[0], query_in.shape[1])
    model_width = query_in.shape[2]
    query_heads = query_in.reshape(nrows, ncols, HEADS, HEAD)
    logits_all = []
    value_all = []
    for row_off in range(7):
        for col_off in range(7):
            window_kv = keys_in[row_off : row_off + nrows, col_off : col_off + ncols].astype(
                jnp.bfloat16
            )
            key_part = window_kv[..., :model_width].reshape(nrows, ncols, HEADS, HEAD)
            value_all.append(window_kv[..., model_width:].reshape(nrows, ncols, HEADS, HEAD))
            logits = jnp.einsum(
                "rchd,rchd->rch", query_heads, key_part, preferred_element_type=jnp.float32
            )
            mask_here = inside[row_off : row_off + nrows, col_off : col_off + ncols]
            logits_all.append(jnp.where(mask_here[:, :, None], logits, -1e30))
    logits_all = jnp.stack(logits_all)
    peak = jnp.max(logits_all, 0, keepdims=True)
    exponent = jnp.exp(logits_all - peak)
    probability = (exponent / jnp.sum(exponent, 0, keepdims=True)).astype(jnp.bfloat16)
    result = jnp.zeros((nrows, ncols, HEADS, HEAD), jnp.float32)
    for offset_idx in range(49):
        result = result + jnp.einsum(
            "rch,rchd->rchd",
            probability[offset_idx],
            value_all[offset_idx],
            preferred_element_type=jnp.float32,
        )
    return result.reshape(nrows, ncols, model_width)


def extend(field_data):
    widened = with_halo(field_data, (("cols", 1),), 3)
    return with_halo(widened, (("rows", 0),), 3)


def send_cols(section, offset):
    return passed_along(section, "cols", offset)


def send_rows(section, offset):
    return passed_along(section, "rows", offset)


def fold_back(grad_ext):
    middle = grad_ext[:, 3:-3]
    from_left = send_cols(grad_ext[:, -3:], 1)
    from_right = send_cols(grad_ext[:, :3], -1)
    middle = middle.at[:, :3].add(from_left).at[:, -3:].add(from_right)
    interior = middle[3:-3]
    from_above = send_rows(middle[-3:], 1)
    from_below = send_rows(middle[:3], -1)
    return interior.at[:3].add(from_above).at[-3:].add(from_below)


def per_device(
    grid_token_states,
    upstream_gradient,
    noise_level_step,
    picture_category_label,
    category_gain_offset,
    noise_level_gain_matrix,
    attention_input_matrix,
    final_projection_matrix,
    cosine_logit_gain,
):
    height, columns = (grid_token_states.shape[0], grid_token_states.shape[1])
    model_width = grid_token_states.shape[2]
    classes = category_gain_offset.shape[0]
    onehot = (jnp.arange(classes, dtype=jnp.int32) == picture_category_label[0]).astype(
        jnp.bfloat16
    )
    class_row = jnp.dot(onehot[None, :], category_gain_offset, preferred_element_type=jnp.float32)[
        0
    ]
    scale_vec = cond_scale(noise_level_step, class_row, noise_level_gain_matrix)
    latent32 = grid_token_states.astype(jnp.float32)
    normed32, norm_back = jax.vjp(
        lambda content_vector_lines: normalize(content_vector_lines, scale_vec), latent32
    )
    normed = normed32.astype(jnp.bfloat16)
    flat_normed = normed.reshape(-1, model_width)
    final_mapped_result = (
        jnp.dot(flat_normed, attention_input_matrix, preferred_element_type=jnp.float32)
        .astype(jnp.bfloat16)
        .reshape(height, columns, 3 * model_width)
    )
    (lone_probe_vector, lone_memory_pair), join_attention_groups = jax.vjp(
        lambda content_vector_lines: split_per_attention_group(
            content_vector_lines, cosine_logit_gain
        ),
        final_mapped_result.astype(jnp.float32),
    )
    queries = lone_probe_vector.astype(jnp.bfloat16)
    extended = extend(lone_memory_pair.astype(jnp.bfloat16))
    row_pos = lax.axis_index("rows") * height - 3 + jnp.arange(height + 6, dtype=jnp.int32)
    col_pos = lax.axis_index("cols") * columns - 3 + jnp.arange(columns + 6, dtype=jnp.int32)
    row_ok = (row_pos >= 0) & (row_pos < height * lax.axis_size("rows"))
    col_ok = (col_pos >= 0) & (col_pos < columns * lax.axis_size("cols"))
    inside = row_ok[:, None] & col_ok[None, :]
    flat_cotangent = upstream_gradient.reshape(-1, model_width)
    grad_attn = jnp.dot(
        flat_cotangent, final_projection_matrix.T, preferred_element_type=jnp.float32
    ).reshape(height, columns, model_width)
    attended32, attn_back = jax.vjp(
        lambda query_in, keys_in: attend(query_in, keys_in, inside),
        queries,
        extended.astype(jnp.float32),
    )
    grad_query, grad_ext = attn_back(grad_attn)
    grad_keys = fold_back(grad_ext)
    grad_proj = join_attention_groups((grad_query.astype(jnp.float32), grad_keys))[0].astype(
        jnp.bfloat16
    )
    attended = attended32.astype(jnp.bfloat16)
    flat_attended = attended.reshape(-1, model_width)
    output = (
        latent32
        + jnp.dot(
            flat_attended, final_projection_matrix, preferred_element_type=jnp.float32
        ).reshape(height, columns, model_width)
    ).astype(jnp.bfloat16)
    flat_grad = grad_proj.reshape(-1, 3 * model_width)
    grad_normed = jnp.dot(
        flat_grad, attention_input_matrix.T, preferred_element_type=jnp.float32
    ).reshape(height, columns, model_width)
    grad_latent = (upstream_gradient.astype(jnp.float32) + norm_back(grad_normed)[0]).astype(
        jnp.bfloat16
    )
    qkv_part = jnp.dot(flat_normed.T, flat_grad, preferred_element_type=jnp.float32)
    out_part = jnp.dot(flat_attended.T, flat_cotangent, preferred_element_type=jnp.float32)
    totals = lax.psum((qkv_part, out_part), ("rows", "cols"))
    tokens_all = height * columns * lax.axis_size("rows") * lax.axis_size("cols")
    factor = 1.0 / math.sqrt(tokens_all)
    return (output, grad_latent, totals[0] * factor, totals[1] * factor)


def solution(mesh):
    placed = (P("rows", "cols", None), P("rows", "cols", None), P(), P(), P(), P(), P(), P(), P())
    return jax.shard_map(
        per_device,
        mesh=mesh,
        in_specs=placed,
        out_specs=(P("rows", "cols", None), P("rows", "cols", None), P(), P()),
        check_vma=False,
    )
```

profile of v0, /device:TPU:1, one launch (start us, length us, event | category | flops | bytes accessed | tf_op | source)
XLA Modules:
  0.0 1024.2 jit_solution(13201852781733114138)
XLA Ops:
  23.0 1.9 mul.237
  27.3 5.1 collective-permute-start
  32.3 1.9 collective-permute-start.1
  41.9 5.9 collective-permute-start.2
  71.1 1.9 reshape.1396
  105.9 1.9 reshape.1344
  142.3 1.9 reshape.1380
  155.1 2.2 reshape.1366
  182.5 2.7 multiply_reduce_fusion.12
  216.4 1.9 reshape.1400
  218.3 5.6 multiply_reduce_fusion.30
  257.1 1.8 reshape.1336
  269.9 4.9 fusion.106
  294.7 5.7 fusion.108
  328.6 1.9 reshape.1436
  356.7 5.5 multiply_reduce_fusion.48
  385.0 6.2 fusion.107
  451.8 2.1 fusion.3
  513.3 4.6 fusion.145
  518.1 5.4 fusion.109
  523.9 11.6 %multiply_reduce_fusion.49 = (f32[8,16,8]{2,1,0:T(8,128)}, bf16[8,16,8,64]{3,2,1,0:T(8,128)(2,1)}) fusion(f32[8,16,8,64]{3,2,1,0:T(8,128)S(1)} %reshape.1292, f32[8]{0:T(128)} %param.25, bf16[8,16,8,64]{3,2,1,0:T(8,128)(2,1)S(1)} %copy-done.46, f32[8,16,8]{2,1,0:T(8,128)} %copy-done.143, bf16[8,16,8,64]{3,2,1,0:T(8,128)(2,1)S(1)} %copy-done.45, ...), kind=kLoop, calls=%fused_computation.372 | loop fusion | flops 13040640 | bytes 7020576 | tf_op jit(solution)/shard_map/transpose(jvp())/reduce_sum | solution.py:69
  535.6 5.4 fusion.127
  548.2 1.9 reshape.1522
  550.1 1.8 reshape.1524
  563.7 4.5 multiply_convert_fusion.12
  624.2 1.9 reshape.1456
  640.7 1.9 reshape.1478
  651.6 1.9 reshape.1492
  654.3 1.9 reshape.1496
  667.9 6.3 multiply_convert_fusion.30
  730.8 6.5 multiply_convert_fusion.48
  740.0 1.9 reshape.1443
  742.6 1.9 reshape.1445
  752.3 1.9 reshape.1451
  754.9 1.9 reshape.1453
  764.7 1.8 reshape.1459
  767.3 1.9 reshape.1461
  793.5 5.8 convert_add_fusion
  801.8 3.3 collective-permute-start.4
  805.5 10.6 %add_convert_fusion.1 = bf16[8,16,8,64]{3,1,2,0:T(8,128)(2,1)} fusion(bf16[8,16,8,64]{3,1,2,0:T(8,128)(2,1)S(1)} %copy-done.107, bf16[8,16,8,64]{3,1,2,0:T(8,128)(2,1)S(1)} %copy-done.106, bf16[8,16,8,64]{3,1,2,0:T(8,128)(2,1)S(1)} %copy-done.105, bf16[8,16,8,64]{3,1,2,0:T(8,128)(2,1)S(1)} %copy-done.101, bf16[8,16,8,64]{3,1,2,0:T(8,128)(2,1)S(1)} %copy-done.104, ...), kind=kLoop, calls=%fused_computation.424 | loop fusion | flops 9633792 | bytes 6754304 | tf_op jit(solution)/shard_map/convert_element_type | solution.py:195
  819.5 2.1 collective-permute-start.5
  824.2 3.0 collective-permute-done.5
  828.4 6.4 collective-permute-start.6
  837.6 6.6 collective-permute-done.7
  849.0 2.0 broadcast_in_dim.683
  853.0 2.3 convolution_bitcast_fusion
  859.0 153.0 %all-reduce.203.cloned.1.call-done = (f32[512,1536]{1,0:T(8,128)}, f32[512,512]{1,0:T(8,128)}) async-done(((f32[512,1536]{1,0:T(8,128)}, f32[512,512]{1,0:T(8,128)}), (f32[512,1536]{1,0:T(8,128)}, f32[512,512]{1,0:T(8,128)})) %all-reduce.203.cloned.1.call-update) | async-done | bytes 4194320 | tf_op jit(solution)/shard_map/psum | solution.py:212
  1012.0 3.9 broadcast_multiply_fusion
  (1417 shorter events, 677.0 us)
Async XLA Ops:
  7.2 1004.8 %all-reduce.203.cloned.1.call-start = ((), (), s32[]{:S(2)}) async-start(), calls=%async_computation | async-start | bytes 8388608 | tf_op jit(solution)/shard_map/psum | solution.py:212
  27.3 13.8 %collective-permute-start = (bf16[8,3,1024]{2,1,0:T(4,128)(2,1)}, bf16[8,3,1024]{2,1,0:T(4,128)(2,1)S(1)}, u32[]{:S(2)}, u32[]{:S(2)}) collective-permute-start(bf16[8,3,1024]{2,1,0:T(4,128)(2,1)} %get-tuple-element.467), channel_id=1, source_target_pairs={{0,1},{1,2},{2,3},{3,4},{4,5},{5,6},{6,7},{7,8},{8,9},{9,10},{10,1... | collective-permute-start | bytes 147464 | tf_op jit(solution)/shard_map/ppermute | solution.py:17
  32.3 8.7 collective-permute-start.1
  41.9 40.6 %collective-permute-start.2 = (bf16[3,22,1024]{2,1,0:T(8,128)(2,1)}, bf16[3,22,1024]{2,1,0:T(8,128)(2,1)}, u32[]{:S(2)}, u32[]{:S(2)}) collective-permute-start(bf16[3,22,1024]{2,1,0:T(8,128)(2,1)} %get-tuple-element.414), channel_id=1, source_target_pairs={{0,16},{16,32},{32,48},{48,64},{64,80},{80,96},{96,112},{1,17},{17... | collective-permute-start | bytes 405512 | tf_op jit(solution)/shard_map/ppermute | solution.py:17
  47.8 34.8 %collective-permute-start.3 = (bf16[3,22,1024]{2,1,0:T(8,128)(2,1)}, bf16[3,22,1024]{2,1,0:T(8,128)(2,1)}, u32[]{:S(2)}, u32[]{:S(2)}) collective-permute-start(bf16[3,22,1024]{2,1,0:T(8,128)(2,1)} %get-tuple-element.415), channel_id=1, source_target_pairs={{16,0},{32,16},{48,32},{64,48},{80,64},{96,80},{112,96},{17,1},{33... | collective-permute-start | bytes 405512 | tf_op jit(solution)/shard_map/ppermute | solution.py:20
  104.7 32.7 %copy-start.85 = (bf16[8,16,8,64]{3,2,1,0:T(8,128)(2,1)}, bf16[8,16,8,64]{3,2,1,0:T(8,128)(2,1)S(1)}, u32[]{:S(2)}) copy-start(bf16[8,16,8,64]{3,2,1,0:T(8,128)(2,1)S(1)} %reshape.1348) | copy-start | bytes 393220
  105.9 30.8 %copy-start.87 = (bf16[8,16,8,64]{3,2,1,0:T(8,128)(2,1)}, bf16[8,16,8,64]{3,2,1,0:T(8,128)(2,1)S(1)}, u32[]{:S(2)}) copy-start(bf16[8,16,8,64]{3,2,1,0:T(8,128)(2,1)S(1)} %reshape.1346) | copy-start | bytes 393220
  141.1 70.4 %copy-start.80 = (bf16[8,16,8,64]{3,2,1,0:T(8,128)(2,1)}, bf16[8,16,8,64]{3,2,1,0:T(8,128)(2,1)S(1)}, u32[]{:S(2)}) copy-start(bf16[8,16,8,64]{3,2,1,0:T(8,128)(2,1)S(1)} %reshape.1384) | copy-start | bytes 393220
  142.3 68.5 %copy-start.81 = (bf16[8,16,8,64]{3,2,1,0:T(8,128)(2,1)}, bf16[8,16,8,64]{3,2,1,0:T(8,128)(2,1)S(1)}, u32[]{:S(2)}) copy-start(bf16[8,16,8,64]{3,2,1,0:T(8,128)(2,1)S(1)} %reshape.1382) | copy-start | bytes 393220
  223.9 29.5 %copy-start.163 = (bf16[8,16,512]{2,1,0:T(8,128)(2,1)S(1)}, bf16[8,16,512]{2,1,0:T(8,128)(2,1)}, u32[]{:S(2)}) copy-start(bf16[8,16,512]{2,1,0:T(8,128)(2,1)} %get-tuple-element.290) | copy-start | bytes 393220
  223.9 30.4 %copy-start.162 = (bf16[8,16,512]{2,1,0:T(8,128)(2,1)S(1)}, bf16[8,16,512]{2,1,0:T(8,128)(2,1)}, u32[]{:S(2)}) copy-start(bf16[8,16,512]{2,1,0:T(8,128)(2,1)} %get-tuple-element.291) | copy-start | bytes 393220
  223.9 31.3 %copy-start.161 = (bf16[8,16,512]{2,1,0:T(8,128)(2,1)S(1)}, bf16[8,16,512]{2,1,0:T(8,128)(2,1)}, u32[]{:S(2)}) copy-start(bf16[8,16,512]{2,1,0:T(8,128)(2,1)} %get-tuple-element.292) | copy-start | bytes 393220
  223.9 32.2 %copy-start.160 = (bf16[8,16,512]{2,1,0:T(8,128)(2,1)S(1)}, bf16[8,16,512]{2,1,0:T(8,128)(2,1)}, u32[]{:S(2)}) copy-start(bf16[8,16,512]{2,1,0:T(8,128)(2,1)} %get-tuple-element.293) | copy-start | bytes 393220
  327.4 29.3 %copy-start.14 = (bf16[8,16,8,64]{3,2,1,0:T(8,128)(2,1)}, bf16[8,16,8,64]{3,2,1,0:T(8,128)(2,1)S(1)}, u32[]{:S(2)}) copy-start(bf16[8,16,8,64]{3,2,1,0:T(8,128)(2,1)S(1)} %reshape.1440) | copy-start | bytes 393220
  405.8 34.3 %copy-start.271 = (f32[8,16,8]{1,2,0:T(8,128)S(1)}, f32[8,16,8]{1,2,0:T(8,128)}, u32[]{:S(2)}) copy-start(f32[8,16,8]{1,2,0:T(8,128)} %copy.980) | copy-start | bytes 12292
  406.5 34.3 %copy-start.272 = (f32[8,16,8]{1,2,0:T(8,128)S(1)}, f32[8,16,8]{1,2,0:T(8,128)}, u32[]{:S(2)}) copy-start(f32[8,16,8]{1,2,0:T(8,128)} %copy.985) | copy-start | bytes 12292
  406.5 34.9 %copy-start.273 = (f32[8,16,8]{1,2,0:T(8,128)S(1)}, f32[8,16,8]{1,2,0:T(8,128)}, u32[]{:S(2)}) copy-start(f32[8,16,8]{1,2,0:T(8,128)} %copy.990) | copy-start | bytes 12292
  408.0 34.0 %copy-start.274 = (f32[8,16,8]{1,2,0:T(8,128)S(1)}, f32[8,16,8]{1,2,0:T(8,128)}, u32[]{:S(2)}) copy-start(f32[8,16,8]{1,2,0:T(8,128)} %copy.995) | copy-start | bytes 12292
  408.7 33.9 %copy-start.275 = (f32[8,16,8]{1,2,0:T(8,128)S(1)}, f32[8,16,8]{1,2,0:T(8,128)}, u32[]{:S(2)}) copy-start(f32[8,16,8]{1,2,0:T(8,128)} %copy.1000) | copy-start | bytes 12292
  408.7 34.6 %copy-start.276 = (f32[8,16,8]{1,2,0:T(8,128)S(1)}, f32[8,16,8]{1,2,0:T(8,128)}, u32[]{:S(2)}) copy-start(f32[8,16,8]{1,2,0:T(8,128)} %copy.1005) | copy-start | bytes 12292
  410.3 33.7 %copy-start.277 = (f32[8,16,8]{1,2,0:T(8,128)S(1)}, f32[8,16,8]{1,2,0:T(8,128)}, u32[]{:S(2)}) copy-start(f32[8,16,8]{1,2,0:T(8,128)} %copy.1010) | copy-start | bytes 12292
  410.9 33.7 %copy-start.278 = (f32[8,16,8]{1,2,0:T(8,128)S(1)}, f32[8,16,8]{1,2,0:T(8,128)}, u32[]{:S(2)}) copy-start(f32[8,16,8]{1,2,0:T(8,128)} %copy.1015) | copy-start | bytes 12292
  410.9 34.3 %copy-start.279 = (f32[8,16,8]{1,2,0:T(8,128)S(1)}, f32[8,16,8]{1,2,0:T(8,128)}, u32[]{:S(2)}) copy-start(f32[8,16,8]{1,2,0:T(8,128)} %copy.1020) | copy-start | bytes 12292
  411.6 34.2 %copy-start.280 = (f32[8,16,8]{1,2,0:T(8,128)S(1)}, f32[8,16,8]{1,2,0:T(8,128)}, u32[]{:S(2)}) copy-start(f32[8,16,8]{1,2,0:T(8,128)} %copy.1025) | copy-start | bytes 12292
  413.2 33.3 %copy-start.281 = (f32[8,16,8]{1,2,0:T(8,128)S(1)}, f32[8,16,8]{1,2,0:T(8,128)}, u32[]{:S(2)}) copy-start(f32[8,16,8]{1,2,0:T(8,128)} %copy.1030) | copy-start | bytes 12292
  413.2 33.9 %copy-start.270 = (f32[8,16,8]{1,2,0:T(8,128)S(1)}, f32[8,16,8]{1,2,0:T(8,128)}, u32[]{:S(2)}) copy-start(f32[8,16,8]{1,2,0:T(8,128)} %copy.1035) | copy-start | bytes 12292
  414.7 33.0 %copy-start.300 = (f32[8,16,8]{1,2,0:T(8,128)S(1)}, f32[8,16,8]{1,2,0:T(8,128)}, u32[]{:S(2)}) copy-start(f32[8,16,8]{1,2,0:T(8,128)} %copy.1040) | copy-start | bytes 12292
  415.4 32.9 %copy-start.269 = (f32[8,16,8]{1,2,0:T(8,128)S(1)}, f32[8,16,8]{1,2,0:T(8,128)}, u32[]{:S(2)}) copy-start(f32[8,16,8]{1,2,0:T(8,128)} %copy.1045) | copy-start | bytes 12292
  415.5 32.9 %copy-start.290 = (f32[8,16,8]{1,2,0:T(8,128)S(1)}, f32[8,16,8]{1,2,0:T(8,128)}, u32[]{:S(2)}) copy-start(f32[8,16,8]{1,2,0:T(8,128)} %copy.845) | copy-start | bytes 12292
  415.5 32.9 %copy-start.291 = (f32[8,16,8]{1,2,0:T(8,128)S(1)}, f32[8,16,8]{1,2,0:T(8,128)}, u32[]{:S(2)}) copy-start(f32[8,16,8]{1,2,0:T(8,128)} %copy.850) | copy-start | bytes 12292
  415.5 32.9 %copy-start.292 = (f32[8,16,8]{1,2,0:T(8,128)S(1)}, f32[8,16,8]{1,2,0:T(8,128)}, u32[]{:S(2)}) copy-start(f32[8,16,8]{1,2,0:T(8,128)} %copy.855) | copy-start | bytes 12292
  415.5 32.9 %copy-start.293 = (f32[8,16,8]{1,2,0:T(8,128)S(1)}, f32[8,16,8]{1,2,0:T(8,128)}, u32[]{:S(2)}) copy-start(f32[8,16,8]{1,2,0:T(8,128)} %copy.860) | copy-start | bytes 12292
  415.5 32.9 %copy-start.294 = (f32[8,16,8]{1,2,0:T(8,128)S(1)}, f32[8,16,8]{1,2,0:T(8,128)}, u32[]{:S(2)}) copy-start(f32[8,16,8]{1,2,0:T(8,128)} %copy.865) | copy-start | bytes 12292
  415.5 32.9 %copy-start.295 = (f32[8,16,8]{1,2,0:T(8,128)S(1)}, f32[8,16,8]{1,2,0:T(8,128)}, u32[]{:S(2)}) copy-start(f32[8,16,8]{1,2,0:T(8,128)} %copy.870) | copy-start | bytes 12292
  415.5 32.9 %copy-start.296 = (f32[8,16,8]{1,2,0:T(8,128)S(1)}, f32[8,16,8]{1,2,0:T(8,128)}, u32[]{:S(2)}) copy-start(f32[8,16,8]{1,2,0:T(8,128)} %copy.875) | copy-start | bytes 12292
  415.5 32.9 %copy-start.297 = (f32[8,16,8]{1,2,0:T(8,128)S(1)}, f32[8,16,8]{1,2,0:T(8,128)}, u32[]{:S(2)}) copy-start(f32[8,16,8]{1,2,0:T(8,128)} %copy.880) | copy-start | bytes 12292
  415.5 32.9 %copy-start.298 = (f32[8,16,8]{1,2,0:T(8,128)S(1)}, f32[8,16,8]{1,2,0:T(8,128)}, u32[]{:S(2)}) copy-start(f32[8,16,8]{1,2,0:T(8,128)} %copy.885) | copy-start | bytes 12292
  415.5 32.9 %copy-start.299 = (f32[8,16,8]{1,2,0:T(8,128)S(1)}, f32[8,16,8]{1,2,0:T(8,128)}, u32[]{:S(2)}) copy-start(f32[8,16,8]{1,2,0:T(8,128)} %copy.890) | copy-start | bytes 12292
  415.6 32.9 %copy-start.301 = (f32[8,16,8]{1,2,0:T(8,128)S(1)}, f32[8,16,8]{1,2,0:T(8,128)}, u32[]{:S(2)}) copy-start(f32[8,16,8]{1,2,0:T(8,128)} %copy.895) | copy-start | bytes 12292
  415.6 32.9 %copy-start.302 = (f32[8,16,8]{1,2,0:T(8,128)S(1)}, f32[8,16,8]{1,2,0:T(8,128)}, u32[]{:S(2)}) copy-start(f32[8,16,8]{1,2,0:T(8,128)} %copy.900) | copy-start | bytes 12292
  415.6 32.9 %copy-start.303 = (f32[8,16,8]{1,2,0:T(8,128)S(1)}, f32[8,16,8]{1,2,0:T(8,128)}, u32[]{:S(2)}) copy-start(f32[8,16,8]{1,2,0:T(8,128)} %copy.905) | copy-start | bytes 12292
  415.6 32.9 %copy-start.304 = (f32[8,16,8]{1,2,0:T(8,128)S(1)}, f32[8,16,8]{1,2,0:T(8,128)}, u32[]{:S(2)}) copy-start(f32[8,16,8]{1,2,0:T(8,128)} %copy.910) | copy-start | bytes 12292
  415.6 32.9 %copy-start.305 = (f32[8,16,8]{1,2,0:T(8,128)S(1)}, f32[8,16,8]{1,2,0:T(8,128)}, u32[]{:S(2)}) copy-start(f32[8,16,8]{1,2,0:T(8,128)} %copy.915) | copy-start | bytes 12292
  415.6 32.9 %copy-start.306 = (f32[8,16,8]{1,2,0:T(8,128)S(1)}, f32[8,16,8]{1,2,0:T(8,128)}, u32[]{:S(2)}) copy-start(f32[8,16,8]{1,2,0:T(8,128)} %copy.920) | copy-start | bytes 12292
  801.8 19.8 %collective-permute-start.4 = (f32[14,3,1024]{2,1,0:T(4,128)}, f32[14,3,1024]{2,1,0:T(4,128)}, u32[]{:S(2)}, u32[]{:S(2)}) collective-permute-start(f32[14,3,1024]{2,1,0:T(4,128)} %get-tuple-element.211), channel_id=1, source_target_pairs={{0,1},{1,2},{2,3},{3,4},{4,5},{5,6},{6,7},{7,8},{8,9},{9,10},{10,1... | collective-permute-start | bytes 516104 | tf_op jit(solution)/shard_map/ppermute | solution.py:28
  819.5 7.7 collective-permute-start.5
  828.4 9.2 collective-permute-start.6
  836.1 8.1 collective-permute-start.7
  (369 other events, 2424.5 us)
Sparse Core Ops, SparseCore 0:
  855.4 156.4 all-reduce.202
where the time goes:
time: 1040 us; the launch traced here: 1020 us
  local copies, waits for them, and re-layouts  639 us (61%)
  other arithmetic  165 us (16%)
  waiting for transfers between devices  163 us (16%)
  starting transfers between devices  27.6 us (3%)
  between operations  20.9 us (2%)
    reshape x126, local copies, waits for them, and re-layouts, attend(): window_kv[..., model_width:].reshape(nrows, ncols, HEADS, HEAD)  196 us
    reshape x98, local copies, waits for them, and re-layouts, attend(): key_part = window_kv[..., :model_width].reshape(nrows, ncols, HEADS, HEAD)  154 us
    psum x1, waiting for transfers between devices, per_device(): totals = lax.psum((qkv_part, out_part), ('rows', 'cols'))  153 us
    dot_general x49, local copies, waits for them, and re-layouts, attend(): jnp.einsum('rchd,rchd->rch', query_heads, key_part, preferred_element_typ...  69.3 us
    dot_general x49, local copies, waits for them, and re-layouts, attend(): jnp.einsum('rch,rchd->rchd', probability[offset_idx], value_all[offset_id...  66.7 us
    unnamed x54, other arithmetic  63.8 us
    convert_element_type x49, local copies, waits for them, and re-layouts, attend(): jnp.einsum('rch,rchd->rchd', probability[offset_idx], value_all[offset_id...  63.3 us
    select_n x49, local copies, waits for them, and re-layouts, attend(): logits_all.append(jnp.where(mask_here[:, :, None], logits, -1e+30))  48.8 us
  transfers between devices with their start and end apart: 9, of which 3 were waited for; matrix products, arithmetic and copies ran while one was open for 6% of the time, Pallas kernels for 0%

commit v1 on v0

v1 whole, which is shorter than its diff:
```python
import functools
import math

import jax
import jax.numpy as jnp
from jax import lax
from jax.experimental import pallas as pl
from jax.experimental.pallas import tpu as pltpu
from jax.sharding import PartitionSpec as P

HEADS = 8
HEAD = 64
BF16 = jnp.bfloat16
F32 = jnp.float32
VMEM_LIMIT = 56 * 1024 * 1024
AXES = ("rows", "cols")
SLOTS = 32
EXT_ROWS = 20
QUERY_ROWS = 14


def mm(a, b):
    return jnp.dot(a, b, preferred_element_type=F32)


def mm_nt(a, b):
    return lax.dot_general(a, b, (((1,), (1,)), ((), ())), preferred_element_type=F32)


def mm_tn(a, b):
    return lax.dot_general(a, b, (((0,), (0,)), ((), ())), preferred_element_type=F32)


def head_sums(product, ones):
    high = product.astype(BF16)
    low = (product - high.astype(F32)).astype(BF16)
    parts = []
    for g in range(2):
        lanes = slice(256 * g, 256 * g + 256)
        parts.append(mm(high[:, lanes], ones) + mm(low[:, lanes], ones))
    return jnp.concatenate(parts, axis=1)


def by_head(block):
    head_of = lax.broadcasted_iota(jnp.int32, block.shape, 1) // HEAD
    zero = jnp.zeros_like(block)
    return jnp.concatenate([jnp.where(head_of == h, block, zero) for h in range(4)], axis=0)


def own_heads(result):
    head_of = lax.broadcasted_iota(jnp.int32, (HEAD, 256), 1) // HEAD
    total = jnp.where(head_of == 0, result[:HEAD], 0.0)
    for h in range(1, 4):
        total = jnp.where(head_of == h, result[HEAD * h : HEAD * (h + 1)], total)
    return total


def main_kernel(
    place_ref, x_ref, du_ref, up_ref, down_ref, left_ref, right_ref, win_ref, wo_ref,
    scale_ref, gain_ref,
    out_ref, dx_ref, send_ref, keep_ref,
    normed_s, du_s, k_s, v_s, q_s, do_s, kraw_s, qraw_s, att_s, dq_s, dk_s, dv_s, kb_s, wb_s, gp_s,
):
    scale = scale_ref[...]
    gain = gain_ref[...]

    def side(ref, row):
        block = ref[16 * (row // 2) : 16 * (row // 2) + 16, :].astype(F32)
        return block[8 * (row % 2) : 8 * (row % 2) + 8]

    def row_of(own, row):
        return jnp.concatenate([own.astype(F32), side(right_ref, row), side(left_ref, row)], axis=0)

    for e in range(EXT_ROWS):
        if e < 6:
            own, row = up_ref[16 * e : 16 * e + 16, :], e
        elif e < 14:
            own, row = x_ref[16 * (e - 6) : 16 * (e - 6) + 16, :], 9 + e - 6
        else:
            own, row = down_ref[16 * (e - 14) : 16 * (e - 14) + 16, :], 25 + e - 14
        x = row_of(own, row)
        r = lax.rsqrt(jnp.mean(x * x, axis=-1, keepdims=True) + 1e-06)
        normed_s[SLOTS * e : SLOTS * (e + 1), :] = (x * r * scale).astype(BF16)
    for f in range(QUERY_ROWS):
        if f < 3:
            own, row = up_ref[16 * (6 + f) : 16 * (7 + f), :], 6 + f
        elif f < 11:
            own, row = du_ref[16 * (f - 3) : 16 * (f - 2), :], 17 + f - 3
        else:
            own, row = down_ref[16 * (6 + f - 11) : 16 * (7 + f - 11), :], 31 + f - 11
        du_s[SLOTS * f : SLOTS * (f + 1), :] = row_of(own, row).astype(BF16)

    same = lax.broadcasted_iota(jnp.int32, (256, 256), 0) // HEAD
    ones = jnp.where(same == lax.broadcasted_iota(jnp.int32, (256, 256), 1) // HEAD, 1.0, 0.0)
    ones = ones.astype(BF16)

    index = lax.broadcasted_iota(jnp.int32, (EXT_ROWS * SLOTS, 128), 0)
    slot = index % SLOTS
    row = index // SLOTS - 6 + place_ref[0]
    col = jnp.where(slot < 24, slot, slot - 32) + place_ref[1]
    inside = (row >= 0) & (row < place_ref[2]) & (col >= 0) & (col < place_ref[3])
    kb_s[...] = jnp.where(inside, 0.0, -1e30)
    index = lax.broadcasted_iota(jnp.int32, (256, 128), 0)
    lane = lax.broadcasted_iota(jnp.int32, (256, 128), 1) % 64
    key_col = jnp.where(index % SLOTS < 24, index % SLOTS, index % SLOTS - 32)
    query_col = jnp.where(lane % SLOTS < 24, lane % SLOTS, lane % SLOTS - 32)
    row_gap = index // SLOTS - lane // SLOTS
    col_gap = key_col - query_col
    near = (row_gap >= 0) & (row_gap <= 6) & (col_gap >= -3) & (col_gap <= 3)
    wb_s[...] = jnp.where(near, 0.0, -1e30)

    for t in range(5):
        rows = slice(128 * t, 128 * t + 128)
        normed = normed_s[rows, :]
        raw = mm(normed, win_ref[:, 512:1024]).astype(BF16)
        kraw_s[rows, :] = raw
        raw = raw.astype(F32)
        k_s[rows, :] = (raw * lax.rsqrt(head_sums(raw * raw, ones) + 1e-06)).astype(BF16)
        v_s[rows, :] = mm(normed, win_ref[:, 1024:1536]).astype(BF16)
    for start, size in ((0, 128), (128, 128), (256, 128), (384, 64)):
        rows = slice(start, start + size)
        raw = mm(normed_s[96 + start : 96 + start + size, :], win_ref[:, 0:512]).astype(BF16)
        qraw_s[rows, :] = raw
        raw = raw.astype(F32)
        q_s[rows, :] = (raw * lax.rsqrt(head_sums(raw * raw, ones) + 1e-06) * gain).astype(BF16)
        do_s[rows, :] = mm_nt(du_s[rows, :], wo_ref[...]).astype(BF16)

    dk_s[...] = jnp.zeros_like(dk_s)
    dv_s[...] = jnp.zeros_like(dv_s)
    for i in range(7):
        keys = slice(64 * i, 64 * i + 256)
        queries = slice(64 * i, 64 * i + 64)
        bias = wb_s[...] + kb_s[keys, :]
        bias = jnp.concatenate([bias, bias], axis=1)
        for g in range(2):
            lanes = slice(256 * g, 256 * g + 256)
            k_t = k_s[keys, lanes]
            v_t = v_s[keys, lanes]
            q_h = by_head(q_s[queries, lanes])
            do_h = by_head(do_s[queries, lanes])
            scores = mm_nt(k_t, q_h) + bias
            weight = jnp.exp(scores - jnp.max(scores, axis=0, keepdims=True))
            weight = weight * (1.0 / jnp.sum(weight, axis=0, keepdims=True))
            prob = weight.astype(BF16)
            dprob = mm_nt(v_t, do_h).astype(BF16).astype(F32)
            mean = jnp.sum(weight * dprob, axis=0, keepdims=True)
            dscore = (weight * (dprob - mean)).astype(BF16)
            low, high = max(2 * i, 6), min(2 * i + 8, 14)
            here = slice((low - 2 * i) * SLOTS, (high - 2 * i) * SLOTS)
            there = slice((low - 6) * SLOTS, (high - 6) * SLOTS)
            dv_s[there, lanes] += mm(prob[here], do_h)
            dk_s[there, lanes] += mm(dscore[here], q_h)
            if 1 <= i <= 5:
                att_s[queries, lanes] = own_heads(mm_tn(prob, v_t)).astype(BF16)
                dq_s[queries, lanes] = own_heads(mm_tn(dscore, k_t)).astype(BF16)

    def own_tokens(ref, first):
        return jnp.concatenate(
            [ref[SLOTS * (first + r) : SLOTS * (first + r) + 16, :] for r in range(8)], axis=0
        )

    att = own_tokens(att_s, 3)
    normed = own_tokens(normed_s, 6)
    x = x_ref[...].astype(F32)
    out_ref[...] = (x + mm(att, wo_ref[...])).astype(BF16)

    def norm_back(raw, grad):
        inv = lax.rsqrt(head_sums(raw * raw, ones) + 1e-06)
        return inv * (grad - raw * (inv * inv) * head_sums(raw * grad, ones))

    dq = norm_back(own_tokens(qraw_s, 3).astype(F32), own_tokens(dq_s, 3).astype(F32) * gain)
    dk = norm_back(own_tokens(kraw_s, 6).astype(F32), own_tokens(dk_s, 0))
    gp_s[:, 0:512] = dq.astype(BF16)
    gp_s[:, 512:1024] = dk.astype(BF16)
    gp_s[:, 1024:1536] = own_tokens(dv_s, 0).astype(BF16)
    dnormed = mm_nt(gp_s[...], win_ref[...]) * scale
    r = lax.rsqrt(jnp.mean(x * x, axis=-1, keepdims=True) + 1e-06)
    along = jnp.mean(dnormed * x, axis=-1, keepdims=True)
    dx = r * dnormed - x * (r * r * r * along)
    dx_ref[...] = (du_ref[...].astype(F32) + dx).astype(BF16)

    for ref in (send_ref, keep_ref):
        ref[:, 0:512] = normed
        ref[:, 1280:1792] = att
    for core in range(2):

        @pl.when(place_ref[4] == core)
        def _():
            for ref, half in ((keep_ref, core), (send_ref, 1 - core)):
                ref[:, 512:1280] = gp_s[:, 768 * half : 768 * half + 768]
                ref[:, 1792:2048] = du_ref[:, 256 * half : 256 * half + 256]


def grads_kernel(factor, keep_ref, got_ref, out_ref):
    def both(first, last):
        return jnp.concatenate([keep_ref[:, first:last], got_ref[:, first:last]], axis=0)

    out_ref[:, 0:768] = (mm_tn(both(0, 512), both(512, 1280)) * factor).astype(BF16)
    out_ref[:, 768:1024] = (mm_tn(both(1280, 1792), both(1792, 2048)) * factor).astype(BF16)


def sum_kernel(rows, parts_ref, out_ref):
    count = parts_ref.shape[0] // rows
    step = max(rows, 16)
    total = parts_ref[0:step, :].astype(F32)
    for i in range(1, count * rows // step):
        total = total + parts_ref[step * i : step * (i + 1), :].astype(F32)
    while total.shape[0] > rows:
        half = total.shape[0] // 2
        total = total[:half] + total[half:]
    block = jnp.concatenate([total] * (step // rows), axis=0).astype(BF16)
    for i in range(count * rows // step):
        out_ref[step * i : step * (i + 1), :] = block


def final_kernel(place_ref, mine_ref, other_ref, qkv_ref, out_ref):
    for core in range(2):

        @pl.when(place_ref[4] == core)
        def _():
            for ref, half in ((mine_ref, core), (other_ref, 1 - core)):
                qkv_ref[:, 768 * half : 768 * half + 768] = ref[:, 0:768].astype(F32)
                out_ref[:, 256 * half : 256 * half + 256] = ref[:, 768:1024].astype(F32)


def call(kernel, outs, scratch=(), flops=0, scalars=0, inputs=0):
    whole = pl.BlockSpec(memory_space=pltpu.VMEM)
    return pl.pallas_call(
        kernel,
        out_shape=outs,
        in_specs=[pl.BlockSpec(memory_space=pltpu.SMEM)] * scalars + [whole] * inputs,
        out_specs=jax.tree.map(lambda _: whole, outs),
        scratch_shapes=list(scratch),
        compiler_params=pltpu.CompilerParams(vmem_limit_bytes=VMEM_LIMIT),
        cost_estimate=pl.CostEstimate(flops=flops, bytes_accessed=4 << 20, transcendentals=0),
    )


def condition(noise_level_step, label, category_gain_offset, noise_level_gain_matrix):
    half_freqs = noise_level_gain_matrix.shape[0] // 2
    steps_idx = jnp.arange(half_freqs, dtype=F32)
    freq_rates = 2.0 * math.pi * jnp.exp(steps_idx * (math.log(64.0) / half_freqs))
    angles = noise_level_step[0].astype(F32) * 0.001 * freq_rates
    features = jnp.concatenate([jnp.cos(angles), jnp.sin(angles)]).astype(BF16)
    shifted = jnp.dot(features[None, :], noise_level_gain_matrix, preferred_element_type=F32)
    class_row = lax.dynamic_slice_in_dim(category_gain_offset, label[0], 1, 0).astype(F32)
    return 1.0 + class_row + shifted


def shifted(value, axis, by):
    count = lax.axis_size(axis)
    pairs = [(i, i + by) for i in range(count) if 0 <= i + by < count]
    return lax.ppermute(value, axis, pairs)


def per_device(
    grid_token_states, upstream_gradient, noise_level_step, picture_category_label,
    category_gain_offset, noise_level_gain_matrix, attention_input_matrix,
    final_projection_matrix, cosine_logit_gain,
):
    x, du = grid_token_states, upstream_gradient
    height, columns, width = x.shape
    n_rows, n_cols = lax.axis_size("rows"), lax.axis_size("cols")
    my_row, my_col = lax.axis_index("rows"), lax.axis_index("cols")

    up = shifted(jnp.concatenate([x[-6:], du[-3:]], axis=0), "rows", 1)
    down = shifted(jnp.concatenate([x[:6], du[:3]], axis=0), "rows", -1)
    scale = condition(
        noise_level_step, picture_category_label, category_gain_offset, noise_level_gain_matrix
    )
    gain = jnp.repeat(cosine_logit_gain, HEAD)[None, :]
    edge = jnp.concatenate([up[:, 8:], x[:, 8:], du[:, 8:], down[:, 8:]], axis=0)
    left = shifted(edge, "cols", 1)
    edge = jnp.concatenate([up[:, :8], x[:, :8], du[:, :8], down[:, :8]], axis=0)
    right = shifted(edge, "cols", -1)

    core = my_col % 2
    place = jnp.stack(
        [my_row * height, my_col * columns, jnp.int32(n_rows * height), jnp.int32(n_cols * columns), core]
    ).astype(jnp.int32)
    tokens = height * columns
    bf = lambda *shape: jax.ShapeDtypeStruct(shape, BF16)
    vm = pltpu.VMEM
    output, grad_latent, send, keep = call(
        main_kernel,
        (bf(tokens, width), bf(tokens, width), bf(tokens, 2048), bf(tokens, 2048)),
        scratch=[
            vm((640, 512), BF16), vm((448, 512), BF16), vm((640, 512), BF16), vm((640, 512), BF16),
            vm((448, 512), BF16), vm((448, 512), BF16), vm((640, 512), BF16), vm((448, 512), BF16),
            vm((448, 512), BF16), vm((448, 512), BF16), vm((256, 512), F32), vm((256, 512), F32),
            vm((640, 128), F32), vm((256, 128), F32), vm((128, 1536), BF16),
        ],
        flops=8 << 30, scalars=1, inputs=10,
    )(
        place, x.reshape(tokens, width), du.reshape(tokens, width), up.reshape(-1, width),
        down.reshape(-1, width), left.reshape(-1, width), right.reshape(-1, width),
        attention_input_matrix, final_projection_matrix, scale, gain,
    )

    swap = [(i, i ^ 1) for i in range(n_cols)]
    got = lax.ppermute(send, "cols", swap)
    factor = 1.0 / math.sqrt(tokens * n_rows * n_cols)
    partial = call(
        functools.partial(grads_kernel, factor), bf(512, 1024), flops=1 << 29, inputs=2
    )(keep, got)

    groups = [
        [r * n_cols + 2 * c + core_ for r in range(n_rows) for c in range(n_cols // 2)]
        for core_ in range(2)
    ]
    members = n_rows * n_cols // 2
    each = 512 // members

    def exchange(value):
        return lax.all_to_all(
            value.reshape(members, each, 1024), AXES, 0, 0, axis_index_groups=groups, tiled=True
        ).reshape(512, 1024)

    summed = call(functools.partial(sum_kernel, each), bf(512, 1024), inputs=1)(exchange(partial))
    mine = exchange(summed)
    other = lax.ppermute(mine, "cols", swap)
    qkv_grad, out_grad = call(
        final_kernel,
        (jax.ShapeDtypeStruct((512, 1536), F32), jax.ShapeDtypeStruct((512, 512), F32)),
        scalars=1, inputs=2,
    )(place, mine, other)
    return output.reshape(x.shape), grad_latent.reshape(x.shape), qkv_grad, out_grad


def solution(mesh):
    placed = (P("rows", "cols", None), P("rows", "cols", None)) + (P(),) * 7
    return jax.shard_map(
        per_device,
        mesh=mesh,
        in_specs=placed,
        out_specs=(P("rows", "cols", None), P("rows", "cols", None), P(), P()),
        check_vma=False,
    )
```

time: 1040 us -> 111 us (0.11); the launches traced: 1020 us -> 110 us
  local copies, waits for them, and re-layouts: 639 us -> 6.69 us
  other arithmetic: 165 us -> 0.17 us
  waiting for transfers between devices: 163 us -> 11.6 us
  blocking collectives: 0 us -> 49.5 us
  Pallas kernels: 0 us -> 22 us
  between operations: 20.9 us -> 2.1 us
  starting transfers between devices: 27.6 us -> 16.9 us
    reshape x227 -> x0, local copies, waits for them, and re-layouts: 352 us -> none  [the longest x126 196 us: attend(): window_kv[..., model_width:].reshape(nrows, ncols, HEADS, HEAD)]
    psum x1 -> x0, waiting for transfers between devices: 153 us -> none  [per_device(): totals = lax.psum((qkv_part, out_part), ('rows', 'cols'))]
    dot_general x98 -> x0, local copies, waits for them, and re-layouts: 136 us -> none  [the longest x49 69.3 us: attend(): jnp.einsum('rchd,rchd->rch', query_heads, key_part, preferred_element_typ...]
    convert_element_type x51 -> x0, local copies, waits for them, and re-layouts: 64.5 us -> none  [the longest x49 63.3 us: attend(): jnp.einsum('rch,rchd->rchd', probability[offset_idx], value_all[offset_id...]
    unnamed x54 -> x0, other arithmetic: 63.8 us -> none
    all_to_all x0 -> x2, blocking collectives: none -> 49.5 us  [exchange(): lax.all_to_all(value.reshape(members, each, 1024), AXES, 0, 0, axis_index...]
    select_n x49 -> x0, local copies, waits for them, and re-layouts: 48.8 us -> none  [attend(): logits_all.append(jnp.where(mask_here[:, :, None], logits, -1e+30))]
    convert_element_type x11 -> x0, other arithmetic: 46.7 us -> none  [the longest x3 17.2 us: attend(): jnp.einsum('rch,rchd->rchd', probability[offset_idx], value_all[offset_id...]
  transfers between devices with their start and end apart: 9 -> 6, of which waited for: 3 -> 4; matrix products, arithmetic and copies ran while one was open for 6% -> 4% of each run, Pallas kernels for 0% -> 0%
where the time goes in v1:
time: 111 us; the launch traced here: 110 us
  blocking collectives  49.5 us (45%)
  Pallas kernels  22 us (20%)
  starting transfers between devices  16.9 us (15%)
  waiting for transfers between devices  11.6 us (10%)
  local copies, waits for them, and re-layouts  6.69 us (6%)
  between operations  2.1 us (2%)
  matrix products  1.44 us (1%)
    all_to_all x2, blocking collectives, exchange(): lax.all_to_all(value.reshape(members, each, 1024), AXES, 0, 0, axis_index...  49.5 us
    ppermute x4, starting transfers between devices, shifted(): return lax.ppermute(value, axis, pairs)  13.9 us
    pallas_call x1, Pallas kernels, per_device(): call(main_kernel, (bf(tokens, width), bf(tokens, width), bf(tokens, 2048)...  13.1 us
    ppermute x4, waiting for transfers between devices, shifted(): return lax.ppermute(value, axis, pairs)  7.24 us
    pallas_call x1, Pallas kernels, per_device(): call(final_kernel, (jax.ShapeDtypeStruct((512, 1536), F32), jax.ShapeDtyp...  3.84 us
    ppermute x1, starting transfers between devices, per_device(): other = lax.ppermute(mine, 'cols', swap)  2.94 us
    pallas_call x1, Pallas kernels, per_device(): call(functools.partial(grads_kernel, factor), bf(512, 1024), flops=1 << 2...  2.64 us
    unnamed x18, local copies, waits for them, and re-layouts  2.51 us
  transfers between devices with their start and end apart: 6, of which 4 were waited for; matrix products, arithmetic and copies ran while one was open for 4% of the time, Pallas kernels for 0%

profile of v1, /device:TPU:1, one launch (start us, length us, event | category | flops | bytes accessed | tf_op | source)
XLA Modules:
  0.0 110.4 jit_solution(16946543804813267746)
XLA Ops:
  0.6 0.0 copy-start
  0.6 0.0 copy-start.6
  0.7 0.9 fusion.5
  1.5 1.0 fusion.4
  2.5 6.3 %collective-permute-start = (bf16[9,16,512]{2,1,0:T(8,128)(2,1)S(1)}, bf16[9,16,512]{2,1,0:T(8,128)(2,1)S(1)}, u32[]{:S(2)}, u32[]{:S(2)}) collective-permute-start(bf16[9,16,512]{2,1,0:T(8,128)(2,1)S(1)} %pad_maximum_fusion.2), channel_id=1, source_target_pairs={{0,16},{16,32},{32,48},{48,64},{64,80},{80,96},{96,112},{1,17},{17... | collective-permute-start | bytes 442376 | tf_op jit(solution)/shard_map/ppermute | solution.py:253
  8.9 1.3 %collective-permute-start.1 = (bf16[9,16,512]{2,1,0:T(8,128)(2,1)S(1)}, bf16[9,16,512]{2,1,0:T(8,128)(2,1)S(1)}, u32[]{:S(2)}, u32[]{:S(2)}) collective-permute-start(bf16[9,16,512]{2,1,0:T(8,128)(2,1)S(1)} %pad_maximum_fusion.3), channel_id=1, source_target_pairs={{16,0},{32,16},{48,32},{64,48},{80,64},{96,80},{112,96},{17,1},{33... | collective-permute-start | bytes 442376 | tf_op jit(solution)/shard_map/ppermute | solution.py:253
  10.2 1.0 fusion.2
  11.8 0.1 sine_convert_fusion
  11.9 0.0 collective-permute-done
  11.9 0.0 copy-start.4
  11.9 4.8 %collective-permute-done.1 = bf16[9,16,512]{2,1,0:T(8,128)(2,1)S(1)} collective-permute-done((bf16[9,16,512]{2,1,0:T(8,128)(2,1)S(1)}, bf16[9,16,512]{2,1,0:T(8,128)(2,1)S(1)}, u32[]{:S(2)}, u32[]{:S(2)}) %collective-permute-start.1) | collective-permute-done | bytes 147488 | tf_op jit(solution)/shard_map/ppermute | solution.py:253
  16.7 0.0 copy-start.5
  16.8 4.4 %collective-permute-start.2 = (bf16[34,8,512]{2,1,0:T(8,128)(2,1)S(1)}, bf16[34,8,512]{2,1,0:T(8,128)(2,1)S(1)}, u32[]{:S(2)}, u32[]{:S(2)}) collective-permute-start(bf16[34,8,512]{2,1,0:T(8,128)(2,1)S(1)} %pad_maximum_fusion), channel_id=1, source_target_pairs={{0,1},{1,2},{2,3},{3,4},{4,5},{5,6},{6,7},{7,8},{8,9},{9,10},{10,1... | collective-permute-start | bytes 835592 | tf_op jit(solution)/shard_map/ppermute | solution.py:253
  21.2 1.9 %collective-permute-start.3 = (bf16[34,8,512]{2,1,0:T(8,128)(2,1)S(1)}, bf16[34,8,512]{2,1,0:T(8,128)(2,1)S(1)}, u32[]{:S(2)}, u32[]{:S(2)}) collective-permute-start(bf16[34,8,512]{2,1,0:T(8,128)(2,1)S(1)} %pad_maximum_fusion.1), channel_id=1, source_target_pairs={{1,0},{2,1},{3,2},{4,3},{5,4},{6,5},{7,6},{8,7},{9,8},{10,9},{11,1... | collective-permute-start | bytes 835592 | tf_op jit(solution)/shard_map/ppermute | solution.py:253
  23.8 0.0 copy-done.6
  23.8 0.1 broadcast_in_dim.4
  23.9 0.7 broadcast_in_dim_reshape.3.gain_ref
  24.6 0.6 stack.15.place_ref
  25.2 0.0 copy-done
  25.2 1.4 %convolution_add_fusion.scale_ref = f32[1,512]{1,0:T(1,128)} fusion(bf16[256,1]{0,1:T(2,128)(2,1)S(1)} %reshape.67, bf16[256,512]{1,0:T(8,128)(2,1)S(1)} %copy-done, bf16[1000,512]{1,0:T(8,128)(2,1)} %param.13, s32[]{:T(128)S(6)} %select_n.11), kind=kOutput, calls=%fused_computation | convolution fusion | flops 263680 | bytes 265732 | tf_op jit(solution)/shard_map/dot_general | solution.py:245
  26.6 0.0 collective-permute-done.2
  26.6 0.0 copy-start.7
  26.6 2.4 %collective-permute-done.3 = bf16[34,8,512]{2,1,0:T(8,128)(2,1)S(1)} collective-permute-done((bf16[34,8,512]{2,1,0:T(8,128)(2,1)S(1)}, bf16[34,8,512]{2,1,0:T(8,128)(2,1)S(1)}, u32[]{:S(2)}, u32[]{:S(2)}) %collective-permute-start.3) | collective-permute-done | bytes 278560 | tf_op jit(solution)/shard_map/ppermute | solution.py:253
  29.1 0.0 copy-start.8
  29.1 0.0 copy-done.4
  29.1 0.0 copy-done.5
  29.1 0.0 copy-done.7
  29.1 0.7 copy-done.8
  29.8 13.1 %shard_map.120 = (bf16[128,512]{1,0:T(8,128)(2,1)}, bf16[128,512]{1,0:T(8,128)(2,1)}, bf16[128,2048]{1,0:T(8,128)(2,1)}, bf16[128,2048]{1,0:T(8,128)(2,1)}) custom-call(s32[5]{0:T(128)} %stack.15.place_ref, bf16[128,512]{1,0:T(8,128)(2,1)} %bitcast.28, bf16[128,512]{1,0:T(8,128)(2,1)} %bitcast.29, bf16[144,512]{1,0:T(8,128)(2,1)} %bitcast.30, ...), custom_call_target="tpu_custom_call" | custom-call | flops 8589934592 | bytes 4194304 | tf_op jit(solution)/shard_map/pallas_call | solution.py:284
  42.9 0.0 collective-permute-start.4
  42.9 2.1 %collective-permute-done.4.got_ref = bf16[128,2048]{1,0:T(8,128)(2,1)S(1)} collective-permute-done((bf16[128,2048]{1,0:T(8,128)(2,1)}, bf16[128,2048]{1,0:T(8,128)(2,1)S(1)}, u32[]{:S(2)}, u32[]{:S(2)}) %collective-permute-start.4) | collective-permute-done | bytes 524320 | tf_op jit(solution)/shard_map/ppermute | solution.py:301
  45.0 0.0 copy-start.3
  45.0 0.8 copy-done.3
  45.8 2.6 %shard_map.121 = bf16[512,1024]{1,0:T(8,128)(2,1)} custom-call(bf16[128,2048]{1,0:T(8,128)(2,1)} %get-tuple-element.12.keep_ref, bf16[128,2048]{1,0:T(8,128)(2,1)} %copy-done.3), custom_call_target="tpu_custom_call" | custom-call | flops 536870912 | bytes 4194304 | tf_op jit(solution)/shard_map/pallas_call | solution.py:303
  48.4 27.9 %all_to_all.10 = bf16[64,8,1024]{2,1,0:T(8,128)(2,1)} all-to-all(bf16[64,8,1024]{2,1,0:T(8,128)(2,1)} %bitcast.25), channel_id=1, replica_groups={{0,2,4,6,8,10,12,14,16,18,20,22,24,26,28,30,32,34,36,38,40,42,44,46,48,..., dimensions={0} | all-to-all | bytes 2097152 | tf_op jit(solution)/shard_map/all_to_all | solution.py:315
  76.4 2.4 %shard_map.122 = bf16[512,1024]{1,0:T(8,128)(2,1)} custom-call(bf16[512,1024]{1,0:T(8,128)(2,1)} %bitcast.26), custom_call_target="tpu_custom_call" | custom-call | bytes 4194304 | tf_op jit(solution)/shard_map/pallas_call | solution.py:319
  78.8 21.5 %all_to_all.11 = bf16[64,8,1024]{2,1,0:T(8,128)(2,1)S(1)} all-to-all(bf16[64,8,1024]{2,1,0:T(8,128)(2,1)} %bitcast.27), channel_id=1, replica_groups={{0,2,4,6,8,10,12,14,16,18,20,22,24,26,28,30,32,34,36,38,40,42,44,46,48,..., dimensions={0} | all-to-all | bytes 2097152 | tf_op jit(solution)/shard_map/all_to_all | solution.py:315
  100.3 0.0 copy-start.1
  100.3 2.9 %collective-permute-start.5 = (bf16[512,1024]{1,0:T(8,128)(2,1)S(1)}, bf16[512,1024]{1,0:T(8,128)(2,1)S(1)}, u32[]{:S(2)}, u32[]{:S(2)}) collective-permute-start(bf16[512,1024]{1,0:T(8,128)(2,1)S(1)} %bitcast.23), channel_id=1, source_target_pairs={{0,1},{1,0},{2,3},{3,2},{4,5},{5,4},{6,7},{7,6},{8,9},{9,8},{10,11... | collective-permute-start | bytes 3145736 | tf_op jit(solution)/shard_map/ppermute | solution.py:321
  103.3 2.3 %collective-permute-done.5.other_ref = bf16[512,1024]{1,0:T(8,128)(2,1)S(1)} collective-permute-done((bf16[512,1024]{1,0:T(8,128)(2,1)S(1)}, bf16[512,1024]{1,0:T(8,128)(2,1)S(1)}, u32[]{:S(2)}, u32[]{:S(2)}) %collective-permute-start.5) | collective-permute-done | bytes 1048608 | tf_op jit(solution)/shard_map/ppermute | solution.py:321
  105.6 0.0 copy-done.1
  105.6 0.0 copy-start.2
  105.6 1.0 copy-done.2
  106.5 3.8 %shard_map.123 = (f32[512,1536]{1,0:T(8,128)}, f32[512,512]{1,0:T(8,128)}) custom-call(s32[5]{0:T(128)} %stack.15.place_ref, bf16[512,1024]{1,0:T(8,128)(2,1)} %bitcast.24, bf16[512,1024]{1,0:T(8,128)(2,1)} %copy-done.2), custom_call_target="tpu_custom_call" | custom-call | bytes 4194304 | tf_op jit(solution)/shard_map/pallas_call | solution.py:322
  (8 shorter events, 0.1 us)
Async XLA Ops:
  0.6 24.6 %copy-start = (bf16[256,512]{1,0:T(8,128)(2,1)S(1)}, bf16[256,512]{1,0:T(8,128)(2,1)}, u32[]{:S(2)}) copy-start(bf16[256,512]{1,0:T(8,128)(2,1)} %param.14) | copy-start | bytes 786436
  0.6 23.2 %copy-start.6 = (f32[8]{0:T(128)S(1)}, f32[8]{0:T(128)}, u32[]{:S(2)}) copy-start(f32[8]{0:T(128)} %param.17) | copy-start | bytes 100
  2.5 9.3 %collective-permute-start = (bf16[9,16,512]{2,1,0:T(8,128)(2,1)S(1)}, bf16[9,16,512]{2,1,0:T(8,128)(2,1)S(1)}, u32[]{:S(2)}, u32[]{:S(2)}) collective-permute-start(bf16[9,16,512]{2,1,0:T(8,128)(2,1)S(1)} %pad_maximum_fusion.2), channel_id=1, source_target_pairs={{0,16},{16,32},{32,48},{48,64},{64,80},{80,96},{96,112},{1,17},{17... | collective-permute-start | bytes 442376 | tf_op jit(solution)/shard_map/ppermute | solution.py:253
  8.9 7.8 %collective-permute-start.1 = (bf16[9,16,512]{2,1,0:T(8,128)(2,1)S(1)}, bf16[9,16,512]{2,1,0:T(8,128)(2,1)S(1)}, u32[]{:S(2)}, u32[]{:S(2)}) collective-permute-start(bf16[9,16,512]{2,1,0:T(8,128)(2,1)S(1)} %pad_maximum_fusion.3), channel_id=1, source_target_pairs={{16,0},{32,16},{48,32},{64,48},{80,64},{96,80},{112,96},{17,1},{33... | collective-permute-start | bytes 442376 | tf_op jit(solution)/shard_map/ppermute | solution.py:253
  11.9 17.2 %copy-start.4 = (bf16[9,16,512]{2,1,0:T(8,128)(2,1)}, bf16[9,16,512]{2,1,0:T(8,128)(2,1)S(1)}, u32[]{:S(2)}) copy-start(bf16[9,16,512]{2,1,0:T(8,128)(2,1)S(1)} %collective-permute-done) | copy-start | bytes 442372
  16.7 12.4 %copy-start.5 = (bf16[9,16,512]{2,1,0:T(8,128)(2,1)}, bf16[9,16,512]{2,1,0:T(8,128)(2,1)S(1)}, u32[]{:S(2)}) copy-start(bf16[9,16,512]{2,1,0:T(8,128)(2,1)S(1)} %collective-permute-done.1) | copy-start | bytes 442372
  16.8 9.9 %collective-permute-start.2 = (bf16[34,8,512]{2,1,0:T(8,128)(2,1)S(1)}, bf16[34,8,512]{2,1,0:T(8,128)(2,1)S(1)}, u32[]{:S(2)}, u32[]{:S(2)}) collective-permute-start(bf16[34,8,512]{2,1,0:T(8,128)(2,1)S(1)} %pad_maximum_fusion), channel_id=1, source_target_pairs={{0,1},{1,2},{2,3},{3,4},{4,5},{5,6},{6,7},{7,8},{8,9},{9,10},{10,1... | collective-permute-start | bytes 835592 | tf_op jit(solution)/shard_map/ppermute | solution.py:253
  21.2 7.9 %collective-permute-start.3 = (bf16[34,8,512]{2,1,0:T(8,128)(2,1)S(1)}, bf16[34,8,512]{2,1,0:T(8,128)(2,1)S(1)}, u32[]{:S(2)}, u32[]{:S(2)}) collective-permute-start(bf16[34,8,512]{2,1,0:T(8,128)(2,1)S(1)} %pad_maximum_fusion.1), channel_id=1, source_target_pairs={{1,0},{2,1},{3,2},{4,3},{5,4},{6,5},{7,6},{8,7},{9,8},{10,9},{11,1... | collective-permute-start | bytes 835592 | tf_op jit(solution)/shard_map/ppermute | solution.py:253
  26.6 2.5 %copy-start.7 = (bf16[34,8,512]{2,1,0:T(8,128)(2,1)}, bf16[34,8,512]{2,1,0:T(8,128)(2,1)S(1)}, u32[]{:S(2)}) copy-start(bf16[34,8,512]{2,1,0:T(8,128)(2,1)S(1)} %collective-permute-done.2) | copy-start | bytes 835588
  29.1 0.7 copy-start.8
  42.9 2.1 %collective-permute-start.4 = (bf16[128,2048]{1,0:T(8,128)(2,1)}, bf16[128,2048]{1,0:T(8,128)(2,1)S(1)}, u32[]{:S(2)}, u32[]{:S(2)}) collective-permute-start(bf16[128,2048]{1,0:T(8,128)(2,1)} %get-tuple-element.13), channel_id=1, source_target_pairs={{0,1},{1,0},{2,3},{3,2},{4,5},{5,4},{6,7},{7,6},{8,9},{9,8},{10,11... | collective-permute-start | bytes 1572872 | tf_op jit(solution)/shard_map/ppermute | solution.py:301
  45.0 0.8 copy-start.3
  100.3 5.2 %copy-start.1 = (bf16[64,8,1024]{2,1,0:T(8,128)(2,1)}, bf16[64,8,1024]{2,1,0:T(8,128)(2,1)S(1)}, u32[]{:S(2)}) copy-start(bf16[64,8,1024]{2,1,0:T(8,128)(2,1)S(1)} %all_to_all.11) | copy-start | bytes 3145732
  100.3 5.2 %collective-permute-start.5 = (bf16[512,1024]{1,0:T(8,128)(2,1)S(1)}, bf16[512,1024]{1,0:T(8,128)(2,1)S(1)}, u32[]{:S(2)}, u32[]{:S(2)}) collective-permute-start(bf16[512,1024]{1,0:T(8,128)(2,1)S(1)} %bitcast.23), channel_id=1, source_target_pairs={{0,1},{1,0},{2,3},{3,2},{4,5},{5,4},{6,7},{7,6},{8,9},{9,8},{10,11... | collective-permute-start | bytes 3145736 | tf_op jit(solution)/shard_map/ppermute | solution.py:321
  105.6 1.0 copy-start.2

commit v2 on v1

v2 whole, which is shorter than its diff:
```python
import functools
import math

import jax
import jax.numpy as jnp
from jax import lax
from jax.experimental import pallas as pl
from jax.experimental.pallas import tpu as pltpu
from jax.sharding import PartitionSpec as P

HEADS = 8
HEAD = 64
BF16 = jnp.bfloat16
F32 = jnp.float32
VMEM_LIMIT = 40 * 1024 * 1024
SMALL_LIMIT = 16 * 1024 * 1024
AXES = ("rows", "cols")
NEAR, FAR = 48, 16


def mm(a, b):
    return jnp.dot(a, b, preferred_element_type=F32)


def mm_nt(a, b):
    return lax.dot_general(a, b, (((1,), (1,)), ((), ())), preferred_element_type=F32)


def mm_tn(a, b):
    return lax.dot_general(a, b, (((0,), (0,)), ((), ())), preferred_element_type=F32)


def head_sums(product, ones):
    high = product.astype(BF16)
    low = (product - high.astype(F32)).astype(BF16)
    parts = []
    for g in range(2):
        lanes = slice(256 * g, 256 * g + 256)
        parts.append(mm(high[:, lanes], ones) + mm(low[:, lanes], ones))
    return jnp.concatenate(parts, axis=1)


def by_head(block):
    head_of = lax.broadcasted_iota(jnp.int32, block.shape, 1) // HEAD
    zero = jnp.zeros_like(block)
    return jnp.concatenate([jnp.where(head_of == h, block, zero) for h in range(4)], axis=0)


def own_heads(result):
    head_of = lax.broadcasted_iota(jnp.int32, (32, 256), 1) // HEAD
    total = result[:32]
    for h in range(1, 4):
        total = jnp.where(head_of == h, result[HEAD * h : HEAD * h + 32], total)
    return total


def head_ones():
    row_head = lax.broadcasted_iota(jnp.int32, (256, 256), 0) // HEAD
    lane_head = lax.broadcasted_iota(jnp.int32, (256, 256), 1) // HEAD
    return jnp.where(row_head == lane_head, 1.0, 0.0).astype(BF16)


def lane_gain(gain_ref):
    head_of = lax.broadcasted_iota(jnp.int32, (1, 512), 1) // HEAD
    gain = jnp.zeros((1, 512), F32)
    for h in range(HEADS):
        gain = jnp.where(head_of == h, gain_ref[h], gain)
    return gain


def block(ref, index):
    return ref[16 * index : 16 * index + 16, :].astype(F32)


def tile(ref, index):
    return block(ref, index // 2)[8 * (index % 2) : 8 * (index % 2) + 8]


def normalize(x, scale):
    return x * lax.rsqrt(jnp.mean(x * x, axis=-1, keepdims=True) + 1e-06) * scale


def unit(raw, ones):
    return raw * lax.rsqrt(head_sums(raw * raw, ones) + 1e-06)


def rows_kernel(x_ref, du_ref, c_ref, d_ref, own_ref):
    even = lax.axis_index("rows") % 2 == 0
    own_ref[0:128, :] = x_ref[...]
    own_ref[128:256, :] = du_ref[...]
    for ref, take_last in ((c_ref, even), (d_ref, jnp.logical_not(even))):

        @pl.when(take_last)
        def _():
            ref[0:96, :] = x_ref[32:128, :]
            ref[96:144, :] = du_ref[80:128, :]

        @pl.when(jnp.logical_not(take_last))
        def _():
            ref[0:96, :] = x_ref[0:96, :]
            ref[96:144, :] = du_ref[0:48, :]


def columns_kernel(own_ref, c_ref, d_ref, far_ref, both_ref):
    even = lax.axis_index("rows") % 2 == 0
    first_core = lax.axis_index("cols") % 2 == 0
    sub = lax.broadcasted_iota(jnp.int32, (8, 512), 0)
    both_ref[0:144, :] = c_ref[...]
    both_ref[144:288, :] = d_ref[...]

    def x_edge(x):
        return jnp.where(first_core, x, pltpu.roll(x, 6, 0))[:8]

    def du_edge(du):
        third = jnp.where(first_core, du[2:3], du[15:16])
        return jnp.where(first_core, pltpu.roll(du, 6, 0), pltpu.roll(du, 9, 0))[:8], third

    tiles = []
    thirds = jnp.zeros((8, 512), F32)
    for row in range(8):
        two, third = du_edge(block(own_ref, 8 + row))
        tiles.append(jnp.where(sub < 6, x_edge(block(own_ref, row)), two))
        thirds = jnp.where(sub == row, third, thirds)
    tiles += [thirds, jnp.zeros((8, 512), F32)]
    for ref in (c_ref, d_ref):
        edges = [du_edge(block(ref, 6 + j)) for j in range(3)]
        for j in range(6):
            rest = edges[j][0] if j < 3 else edges[j - 3][1]
            tiles.append(jnp.where(sub < 6, x_edge(block(ref, j)), rest))
    for i in range(11):
        far_ref[16 * i : 16 * i + 16, :] = jnp.concatenate(tiles[2 * i : 2 * i + 2], 0).astype(BF16)


def near_kernel(
    gain_ref, own_ref, mate_ref, c_ref, d_ref, mate_rows_ref, win_ref, wo_ref, scale_ref,
    k_ref, v_ref, q_ref, do_ref, kraw_ref, qraw_ref, normed_ref,
    own_s, mate_s, du_s,
):
    even = lax.axis_index("rows") % 2 == 0
    first_core = lax.axis_index("cols") % 2 == 0
    scale = scale_ref[...]
    gain = lane_gain(gain_ref)
    ones = head_ones()

    def pick(low, high, above):
        return jnp.where(even, high, low) if above else jnp.where(even, low, high)

    def row_parts(row, first):
        if 0 <= row < 8:
            own, mate = block(own_ref, first + row), block(mate_ref, first + row)
        else:
            above = row < 0
            j = (row + (6 if above else -8)) if first == 0 else 6 + (row + (3 if above else -8))
            own = pick(block(c_ref, j), block(d_ref, j), above)
            mate = pick(block(mate_rows_ref, j), block(mate_rows_ref, 9 + j), above)
        return own, jnp.where(first_core, mate[:8], mate[8:])

    for e in range(20):
        own, mate = row_parts(e - 6, 0)
        own_s[16 * e : 16 * e + 16, :] = normalize(own, scale)
        mate_s[8 * e : 8 * e + 8, :] = normalize(mate, scale)
    normed_ref[...] = own_s[96:224, :].astype(BF16)
    for i in range(7):
        first, second = row_parts(2 * i - 3, 8), row_parts(2 * i - 2, 8)
        pair = jnp.concatenate([first[0], second[0], first[1], second[1]], axis=0)
        du_s[NEAR * i : NEAR * (i + 1), :] = pair.astype(BF16)

    def normed_pairs(first_row, count):
        parts = []
        for n in range(count):
            row = first_row + 2 * n
            parts += [own_s[16 * row : 16 * row + 32, :], mate_s[8 * row : 8 * row + 16, :]]
        return jnp.concatenate(parts, axis=0).astype(BF16)

    for t in range(5):
        rows = slice(96 * t, 96 * t + 96)
        normed = normed_pairs(4 * t, 2)
        raw = mm(normed, win_ref[:, 512:1024]).astype(BF16).astype(F32)
        k_ref[rows, :] = unit(raw, ones).astype(BF16)
        v_ref[rows, :] = mm(normed, win_ref[:, 1024:1536]).astype(BF16)
        for n in range(2):
            at = 2 * t + n - 3
            if 0 <= at < 4:
                kraw_ref[32 * at : 32 * at + 32, :] = raw[48 * n : 48 * n + 32].astype(BF16)
    for first, count in ((0, 2), (2, 2), (4, 2), (6, 1)):
        rows = slice(NEAR * first, NEAR * (first + count))
        normed = normed_pairs(3 + 2 * first, count)
        raw = mm(normed, win_ref[:, 0:512]).astype(BF16).astype(F32)
        q_ref[rows, :] = (unit(raw, ones) * gain).astype(BF16)
        do_ref[rows, :] = mm_nt(du_s[rows, :], wo_ref[...]).astype(BF16)
        for n in range(2 * count):
            at = 2 * first + n - 3
            if 0 <= at < 8:
                here = 48 * (n // 2) + 16 * (n % 2)
                qraw_ref[16 * at : 16 * at + 16, :] = raw[here : here + 16].astype(BF16)


def main_kernel(
    gain_ref, own_ref, far_ref, kn_ref, vn_ref, qn_ref, don_ref, kraw_ref, qraw_ref, normed_ref,
    win_ref, wo_ref, scale_ref,
    out_ref, dx_ref, features_ref, send_ref, keep_ref,
    kf_s, vf_s, qf_s, dof_s, att_s, dq_s, dk_s, dv_s, gp_s,
):
    my_row, my_col = lax.axis_index("rows"), lax.axis_index("cols")
    even = my_row % 2 == 0
    first_core = my_col % 2 == 0
    scale = scale_ref[...]
    gain = lane_gain(gain_ref)
    ones = head_ones()
    sub = lax.broadcasted_iota(jnp.int32, (8, 512), 0)
    edge = jnp.where(first_core, 3, 0)

    def far_du(both, third):
        value = jnp.where(sub == edge, both[6:7], 0.0)
        value = jnp.where(sub == edge + 1, both[7:8], value)
        return jnp.where(sub == edge + 2, third, value)

    def rows_far(first_tile):
        return [tile(far_ref, first_tile + j) for j in range(6)]

    c_tiles, d_tiles = rows_far(10), rows_far(16)
    above = [jnp.where(even, d, c) for c, d in zip(c_tiles, d_tiles)]
    below = [jnp.where(even, c, d) for c, d in zip(c_tiles, d_tiles)]
    middle = [tile(far_ref, j) for j in range(8)]
    thirds = tile(far_ref, 8)
    x_far = jnp.concatenate(above + middle + below, axis=0)
    du_far = [far_du(above[j], above[j + 3][6:7]) for j in range(3)]
    du_far += [far_du(middle[j], thirds[j : j + 1]) for j in range(8)]
    du_far += [far_du(below[j], below[j + 3][6:7]) for j in range(3)]
    normed_far = normalize(x_far, scale)
    normed = normed_far.astype(BF16)
    raw = mm(normed, win_ref[:, 512:1024]).astype(BF16).astype(F32)
    kf_s[...] = unit(raw, ones).astype(BF16)
    vf_s[...] = mm(normed, win_ref[:, 1024:1536]).astype(BF16)
    raw = mm(normed_far[24:136].astype(BF16), win_ref[:, 0:512]).astype(BF16).astype(F32)
    qf_s[...] = (unit(raw, ones) * gain).astype(BF16)
    dof_s[...] = mm_nt(jnp.concatenate(du_far, axis=0).astype(BF16), wo_ref[...]).astype(BF16)

    mate_base = jnp.where(first_core, 16, -8)
    far_base = jnp.where(first_core, -6, 16)

    def places(index, near):
        in_near = index < near
        pair = jnp.where(in_near, index // NEAR, 0)
        j = jnp.where(in_near, index % NEAR, index - near)
        mine = in_near & (j < 32)
        eights = jnp.where(in_near, j - 32, j)
        row = jnp.where(mine, 2 * pair + j // 16, 2 * pair + eights // 8)
        slot = eights % 8
        far_col = jnp.where(slot < 6, far_base + slot, 1000)
        return row, jnp.where(mine, j % 16, jnp.where(in_near, mate_base + slot, far_col))

    key_row, key_col = places(lax.broadcasted_iota(jnp.int32, (256, 128), 0), 4 * NEAR)
    query_row, query_col = places(lax.broadcasted_iota(jnp.int32, (256, 128), 1) % 64, NEAR)
    row_gap, col_gap = key_row - query_row, key_col - query_col
    near = (row_gap >= 0) & (row_gap <= 6) & (col_gap >= -3) & (col_gap <= 3) & (key_col < 1000)
    image_col = key_col + 16 * my_col
    near = near & (image_col >= 0) & (image_col < 16 * lax.axis_size("cols"))
    bias_near = jnp.where(near, 0.0, -1e30)

    dk_s[...] = jnp.zeros_like(dk_s)
    dv_s[...] = jnp.zeros_like(dv_s)
    for i in range(7):
        image_row = key_row + (8 * my_row - 6 + 2 * i)
        inside = (image_row >= 0) & (image_row < 8 * lax.axis_size("rows"))
        bias = jnp.where(inside, bias_near, -1e30)
        bias = jnp.concatenate([bias, bias], axis=1)
        blocks = range(max(i, 3), min(i + 4, 7))
        there = slice(32 * (blocks[0] - 3), 32 * (blocks[-1] - 2))

        def own_keys(value):
            parts = [value[NEAR * (b - i) : NEAR * (b - i) + 32] for b in blocks]
            return jnp.concatenate(parts, axis=0)

        for g in range(2):
            lanes = slice(256 * g, 256 * g + 256)

            def keys(near_ref, far_ref):
                parts = [near_ref[NEAR * i : NEAR * (i + 4), lanes], far_ref[FAR * i : FAR * (i + 4), lanes]]
                return jnp.concatenate(parts, axis=0)

            def queries(near_ref, far_ref):
                parts = [near_ref[NEAR * i : NEAR * (i + 1), lanes], far_ref[FAR * i : FAR * (i + 1), lanes]]
                return by_head(jnp.concatenate(parts, axis=0))

            k_t, v_t = keys(kn_ref, kf_s), keys(vn_ref, vf_s)
            q_h, do_h = queries(qn_ref, qf_s), queries(don_ref, dof_s)
            scores = mm_nt(k_t, q_h) + bias
            weight = jnp.exp(scores - jnp.max(scores, axis=0, keepdims=True))
            weight = weight * (1.0 / jnp.sum(weight, axis=0, keepdims=True))
            prob = weight.astype(BF16)
            dprob = mm_nt(v_t, do_h).astype(BF16).astype(F32)
            mean = jnp.sum(weight * dprob, axis=0, keepdims=True)
            dscore = (weight * (dprob - mean)).astype(BF16)
            dv_s[there, lanes] += mm(own_keys(prob), do_h)
            dk_s[there, lanes] += mm(own_keys(dscore), q_h)
            if 1 <= i <= 5:
                att = own_heads(mm_tn(prob, v_t)).astype(BF16)
                dq = own_heads(mm_tn(dscore, k_t)).astype(BF16)
                for n in range(2):
                    at = 2 * i + n - 3
                    if 0 <= at < 8:
                        att_s[16 * at : 16 * at + 16, lanes] = att[16 * n : 16 * n + 16]
                        dq_s[16 * at : 16 * at + 16, lanes] = dq[16 * n : 16 * n + 16]

    att = att_s[...]
    normed = normed_ref[...]
    x = own_ref[0:128, :].astype(F32)
    out_ref[...] = (x + mm(att, wo_ref[...])).astype(BF16)

    def norm_back(raw, grad):
        inv = lax.rsqrt(head_sums(raw * raw, ones) + 1e-06)
        return inv * (grad - raw * (inv * inv) * head_sums(raw * grad, ones))

    dq = norm_back(qraw_ref[...].astype(F32), dq_s[...].astype(F32) * gain)
    dk = norm_back(kraw_ref[...].astype(F32), dk_s[...])
    gp_s[:, 0:512] = dq.astype(BF16)
    gp_s[:, 512:1024] = dk.astype(BF16)
    gp_s[:, 1024:1536] = dv_s[...].astype(BF16)
    dnormed = mm_nt(gp_s[...], win_ref[...]) * scale
    r = lax.rsqrt(jnp.mean(x * x, axis=-1, keepdims=True) + 1e-06)
    along = jnp.mean(dnormed * x, axis=-1, keepdims=True)
    dx = r * dnormed - x * (r * r * r * along)
    dx_ref[...] = (own_ref[128:256, :].astype(F32) + dx).astype(BF16)

    features_ref[0:512, :] = jnp.transpose(normed)
    features_ref[512:1024, :] = jnp.transpose(att)
    for core in range(2):

        @pl.when(my_col % 2 == core)
        def _():
            for ref, half in ((keep_ref, core), (send_ref, 1 - core)):
                ref[:, 0:768] = gp_s[:, 768 * half : 768 * half + 768]
                ref[:, 768:1024] = own_ref[128:256, 256 * half : 256 * half + 256]


def grads_kernel(factor, features_ref, keep_ref, got_features_ref, got_ref, out_ref):
    features = jnp.concatenate([features_ref[...], got_features_ref[...]], axis=1)
    grads = jnp.concatenate([keep_ref[...], got_ref[...]], axis=0)
    out_ref[:, 0:768] = (mm(features[:512], grads[:, :768]) * factor).astype(BF16)
    out_ref[:, 768:1024] = (mm(features[512:], grads[:, 768:]) * factor).astype(BF16)


def sum_kernel(rows, parts_ref, out_ref):
    count = parts_ref.shape[0] // rows
    step = max(rows, 16)
    total = parts_ref[0:step, :].astype(F32)
    for i in range(1, count * rows // step):
        total = total + parts_ref[step * i : step * (i + 1), :].astype(F32)
    while total.shape[0] > rows:
        half = total.shape[0] // 2
        total = total[:half] + total[half:]
    block = jnp.concatenate([total] * (step // rows), axis=0).astype(BF16)
    for i in range(count * rows // step):
        out_ref[step * i : step * (i + 1), :] = block


def final_kernel(half_ref, half_grads_ref, *refs):
    qkv_ref, out_ref = refs[-2:]
    qkv_ref[...] = half_grads_ref[:, 0:768].astype(F32)
    out_ref[...] = half_grads_ref[:, 768:1024].astype(F32)


def write_half(half, half_grads, *whole):
    steps = 4
    rows = half_grads.shape[0] // steps
    return pl.pallas_call(
        final_kernel,
        grid_spec=pltpu.PrefetchScalarGridSpec(
            num_scalar_prefetch=1,
            grid=(steps,),
            in_specs=[pl.BlockSpec((rows, 1024), lambda i, half: (i, 0))]
            + [pl.BlockSpec(memory_space=pl.ANY)] * len(whole),
            out_specs=[
                pl.BlockSpec((rows, 768), lambda i, half: (i, half[0])),
                pl.BlockSpec((rows, 256), lambda i, half: (i, half[0])),
            ],
        ),
        out_shape=[
            jax.ShapeDtypeStruct((512, 1536), F32),
            jax.ShapeDtypeStruct((512, 512), F32),
        ],
        input_output_aliases={2: 0, 3: 1} if whole else {},
        compiler_params=pltpu.CompilerParams(vmem_limit_bytes=8 * 1024 * 1024),
        cost_estimate=pl.CostEstimate(flops=1 << 20, bytes_accessed=3 << 20, transcendentals=0),
    )(half, half_grads, *whole)


def call(kernel, outs, scratch=(), flops=0, scalars=0, inputs=0, limit=VMEM_LIMIT):
    whole = pl.BlockSpec(memory_space=pltpu.VMEM)
    return pl.pallas_call(
        kernel,
        out_shape=outs,
        in_specs=[pl.BlockSpec(memory_space=pltpu.SMEM)] * scalars
        + [whole] * inputs,
        out_specs=jax.tree.map(lambda _: whole, outs),
        scratch_shapes=list(scratch),
        compiler_params=pltpu.CompilerParams(vmem_limit_bytes=limit),
        cost_estimate=pl.CostEstimate(flops=flops, bytes_accessed=4 << 20, transcendentals=0),
    )


def condition(noise_level_step, label, category_gain_offset, noise_level_gain_matrix):
    half_freqs = noise_level_gain_matrix.shape[0] // 2
    steps_idx = jnp.arange(half_freqs, dtype=F32)
    freq_rates = 2.0 * math.pi * jnp.exp(steps_idx * (math.log(64.0) / half_freqs))
    angles = noise_level_step[0].astype(F32) * 0.001 * freq_rates
    features = jnp.concatenate([jnp.cos(angles), jnp.sin(angles)]).astype(BF16)
    shifted = jnp.dot(features[None, :], noise_level_gain_matrix, preferred_element_type=F32)
    class_row = lax.dynamic_slice_in_dim(category_gain_offset, label[0], 1, 0).astype(F32)
    return 1.0 + class_row + shifted


def swapped(value, row_to, col_to):
    n_rows, n_cols = lax.axis_size("rows"), lax.axis_size("cols")
    pairs = []
    for r in range(n_rows):
        for c in range(n_cols):
            to_row, to_col = row_to(r), col_to(c)
            if 0 <= to_row < n_rows and 0 <= to_col < n_cols:
                pairs.append((r * n_cols + c, to_row * n_cols + to_col))
    return lax.ppermute(value, AXES, pairs)


def same(i):
    return i


def paired(i):
    return i ^ 1


def across(i):
    return i - 1 if i % 2 == 0 else i + 1


def per_device(
    grid_token_states, upstream_gradient, noise_level_step, picture_category_label,
    category_gain_offset, noise_level_gain_matrix, attention_input_matrix,
    final_projection_matrix, cosine_logit_gain,
):
    x, du = grid_token_states, upstream_gradient
    height, columns, width = x.shape
    n_rows, n_cols = lax.axis_size("rows"), lax.axis_size("cols")
    tokens = height * columns
    bf = lambda *shape: jax.ShapeDtypeStruct(shape, BF16)
    vm = pltpu.VMEM
    x2, du2 = x.reshape(tokens, width), du.reshape(tokens, width)

    to_c, to_d, own = call(
        rows_kernel, (bf(144, width), bf(144, width), bf(256, width)), inputs=2, limit=SMALL_LIMIT
    )(x2, du2)
    from_c = swapped(to_c, paired, same)
    from_d = swapped(to_d, across, same)
    mate = swapped(own, same, paired)
    scale = condition(
        noise_level_step, picture_category_label, category_gain_offset, noise_level_gain_matrix
    )
    half = (lax.axis_index("cols") % 2).astype(jnp.int32).reshape(1)
    to_far, to_mate = call(
        columns_kernel, (bf(176, width), bf(288, width)), flops=16 << 30, inputs=3, limit=SMALL_LIMIT
    )(own, from_c, from_d)
    far = swapped(to_far, same, across)
    mate_rows = swapped(to_mate, same, paired)
    weights = (attention_input_matrix, final_projection_matrix, scale)
    k, v, q, do, kraw, qraw, normed = call(
        near_kernel,
        (bf(480, width), bf(480, width), bf(336, width), bf(336, width), bf(128, width), bf(128, width), bf(128, width)),
        scratch=[vm((320, 512), F32), vm((160, 512), F32), vm((336, 512), BF16)],
        flops=4 << 30, scalars=1, inputs=8,
    )(cosine_logit_gain, own, mate, from_c, from_d, mate_rows, *weights)

    output, grad_latent, features, send, keep = call(
        main_kernel,
        (bf(tokens, width), bf(tokens, width), bf(1024, tokens), bf(tokens, 1024), bf(tokens, 1024)),
        scratch=[
            vm((160, 512), BF16), vm((160, 512), BF16), vm((112, 512), BF16), vm((112, 512), BF16),
            vm((128, 512), BF16), vm((128, 512), BF16), vm((128, 512), F32), vm((128, 512), F32),
            vm((128, 1536), BF16),
        ],
        flops=8 << 30, scalars=1, inputs=12,
    )(cosine_logit_gain, own, far, k, v, q, do, kraw, qraw, normed, *weights)

    got_features = swapped(features, same, paired)
    got = swapped(send, same, paired)
    factor = 1.0 / math.sqrt(tokens * n_rows * n_cols)
    partial = call(
        functools.partial(grads_kernel, factor), bf(512, 1024), flops=1 << 29, inputs=4, limit=SMALL_LIMIT
    )(features, keep, got_features, got)

    groups = [
        [r * n_cols + 2 * c + core_ for r in range(n_rows) for c in range(n_cols // 2)]
        for core_ in range(2)
    ]
    members = n_rows * n_cols // 2
    each = 512 // members

    def exchange(value):
        return lax.all_to_all(
            value.reshape(members, each, 1024), AXES, 0, 0, axis_index_groups=groups, tiled=True
        ).reshape(512, 1024)

    summed = call(
        functools.partial(sum_kernel, each), bf(512, 1024), inputs=1, limit=SMALL_LIMIT
    )(exchange(partial))
    mine = exchange(summed)
    other = swapped(mine, same, paired)
    qkv_grad, out_grad = write_half(1 - half, other, *write_half(half, mine))
    return output.reshape(x.shape), grad_latent.reshape(x.shape), qkv_grad, out_grad


def solution(mesh):
    placed = (P("rows", "cols", None), P("rows", "cols", None)) + (P(),) * 7
    return jax.shard_map(
        per_device,
        mesh=mesh,
        in_specs=placed,
        out_specs=(P("rows", "cols", None), P("rows", "cols", None), P(), P()),
        check_vma=False,
    )
```

time: 111 us -> 95.7 us (0.86)
  waiting for transfers between devices: 11.6 us -> 3.03 us
  Pallas kernels: 22 us -> 17.6 us
  blocking collectives: 49.5 us -> 51.5 us
  local copies, waits for them, and re-layouts: 6.69 us -> 4.86 us
  starting transfers between devices: 16.9 us -> 15.4 us
    ppermute x6 -> x8, waiting for transfers between devices: 11.6 us -> 3.03 us  [swapped(): return lax.ppermute(value, AXES, pairs)]
    slice x5 -> x0, local copies, waits for them, and re-layouts: 2.84 us -> none  [the longest x2 1.86 us: per_device(): down = shifted(jnp.concatenate([x[:6], du[:3]], axis=0), 'rows', -1)]
    unnamed x18 -> x22, local copies, waits for them, and re-layouts: 2.51 us -> 4.86 us
    pallas_call x1, Pallas kernels: 2.64 us -> 0.44 us  [per_device(): call(functools.partial(grads_kernel, factor), bf(512, 1024), flops=1 << 2...]
    pallas_call x3 -> x7, Pallas kernels: 19.3 us -> 17.2 us  [the longest x1 8.97 us: per_device(): call(main_kernel, (bf(tokens, width), bf(tokens, width), bf(1024, tokens)...]
    all_to_all x2, blocking collectives: 49.5 us -> 51.5 us  [exchange(): lax.all_to_all(value.reshape(members, each, 1024), AXES, 0, 0, axis_index...]
    ppermute x6 -> x8, starting transfers between devices: 16.9 us -> 15.4 us  [swapped(): return lax.ppermute(value, AXES, pairs)]
    another operation x2 -> x0, local copies, waits for them, and re-layouts: 1.28 us -> none  [the longest x1 0.67 us: per_device(): gain = jnp.repeat(cosine_logit_gain, HEAD)[None, :]]
  transfers between devices with their start and end apart: 6 -> 8, of which waited for: 4 -> 4; matrix products, arithmetic and copies ran while one was open for 4% -> 1% of each run, Pallas kernels for 0% -> 6%
where the time goes in v2:
time: 95.7 us; the launch traced here: 95.4 us
  blocking collectives  51.5 us (54%)
  Pallas kernels  17.6 us (18%)
  starting transfers between devices  15.4 us (16%)
  local copies, waits for them, and re-layouts  4.86 us (5%)
  waiting for transfers between devices  3.03 us (3%)
  between operations  2.12 us (2%)
    all_to_all x2, blocking collectives, exchange(): lax.all_to_all(value.reshape(members, each, 1024), AXES, 0, 0, axis_index...  51.5 us
    ppermute x8, starting transfers between devices, swapped(): return lax.ppermute(value, AXES, pairs)  15.4 us
    pallas_call x1, Pallas kernels, per_device(): call(main_kernel, (bf(tokens, width), bf(tokens, width), bf(1024, tokens)...  8.97 us
    unnamed x22, local copies, waits for them, and re-layouts  4.86 us
    pallas_call x1, Pallas kernels, per_device(): call(near_kernel, (bf(480, width), bf(480, width), bf(336, width), bf(336...  4.15 us
    pallas_call x2, Pallas kernels, write_half(): pl.pallas_call(final_kernel, grid_spec=pltpu.PrefetchScalarGridSpec(num_s...  3.59 us
    ppermute x8, waiting for transfers between devices, swapped(): return lax.ppermute(value, AXES, pairs)  3.03 us
  transfers between devices with their start and end apart: 8, of which 4 were waited for; matrix products, arithmetic and copies ran while one was open for 1% of the time, Pallas kernels for 6%

profile of v2, /device:TPU:1, one launch (start us, length us, event | category | flops | bytes accessed | tf_op | source)
XLA Modules:
  0.0 95.4 jit_solution(17476763439038263119)
XLA Ops:
  0.6 0.0 copy-start
  0.6 0.0 copy-start.1
  0.7 0.9 copy-done.1
  1.6 0.0 copy-start.2
  1.6 0.9 copy-done.2
  2.5 4.5 %collective-permute-start = (bf16[144,512]{1,0:T(8,128)(2,1)S(1)}, bf16[144,512]{1,0:T(8,128)(2,1)S(1)}, u32[]{:S(2)}, u32[]{:S(2)}) collective-permute-start(bf16[144,512]{1,0:T(8,128)(2,1)S(1)} %get-tuple-element.26), channel_id=1, source_target_pairs={{0,16},{1,17},{2,18},{3,19},{4,20},{5,21},{6,22},{7,23},{8,24},{9,... | collective-permute-start | bytes 442376 | tf_op jit(solution)/shard_map/ppermute | solution.py:422
  7.0 0.7 collective-permute-start.1
  7.7 1.0 %collective-permute-start.3 = (bf16[256,512]{1,0:T(8,128)(2,1)S(1)}, bf16[256,512]{1,0:T(8,128)(2,1)S(1)}, u32[]{:S(2)}, u32[]{:S(2)}) collective-permute-start(bf16[256,512]{1,0:T(8,128)(2,1)S(1)} %get-tuple-element.25.own_ref), channel_id=1, source_target_pairs={{0,1},{1,0},{2,3},{3,2},{4,5},{5,4},{6,7},{7,6},{8,9},{9,8},{10,11... | collective-permute-start | bytes 786440 | tf_op jit(solution)/shard_map/ppermute | solution.py:422
  9.4 0.1 sine_convert_fusion
  9.5 0.0 copy-start.3
  9.5 0.0 copy-start.4
  9.5 0.0 copy-start.10
  9.5 1.1 %collective-permute-done.c_ref = bf16[144,512]{1,0:T(8,128)(2,1)S(1)} collective-permute-done((bf16[144,512]{1,0:T(8,128)(2,1)S(1)}, bf16[144,512]{1,0:T(8,128)(2,1)S(1)}, u32[]{:S(2)}, u32[]{:S(2)}) %collective-permute-start) | collective-permute-done | bytes 147488 | tf_op jit(solution)/shard_map/ppermute | solution.py:422
  10.6 0.0 copy-start.6
  10.6 0.0 collective-permute-done.1.d_ref
  10.6 0.0 copy-start.8
  10.6 0.2 shard_map.121
  10.8 0.5 copy-done.6
  11.3 0.0 copy-done.8
  11.3 0.0 copy-start.5
  11.3 0.7 copy-done.5
  12.0 3.7 %collective-permute-start.4 = (bf16[288,512]{1,0:T(8,128)(2,1)S(1)}, bf16[288,512]{1,0:T(8,128)(2,1)S(1)}, u32[]{:S(2)}, u32[]{:S(2)}) collective-permute-start(bf16[288,512]{1,0:T(8,128)(2,1)S(1)} %get-tuple-element.29), channel_id=1, source_target_pairs={{0,1},{1,0},{2,3},{3,2},{4,5},{5,4},{6,7},{7,6},{8,9},{9,8},{10,11... | collective-permute-start | bytes 884744 | tf_op jit(solution)/shard_map/ppermute | solution.py:422
  16.4 0.0 copy-done
  16.4 0.8 convolution_add_fusion.scale_ref
  17.2 1.9 %collective-permute-start.2 = (bf16[176,512]{1,0:T(8,128)(2,1)}, bf16[176,512]{1,0:T(8,128)(2,1)S(1)}, u32[]{:S(2)}, u32[]{:S(2)}) collective-permute-start(bf16[176,512]{1,0:T(8,128)(2,1)} %copy-done.5), channel_id=1, source_target_pairs={{1,2},{2,1},{3,4},{4,3},{5,6},{6,5},{7,8},{8,7},{9,10},{10,9},{11,... | collective-permute-start | bytes 540680 | tf_op jit(solution)/shard_map/ppermute | solution.py:422
  19.1 0.0 collective-permute-done.3.mate_ref
  19.1 0.0 collective-permute-done.4.mate_rows_ref
  19.2 0.0 copy-done.3
  19.2 0.0 copy-done.4
  19.2 0.0 copy-done.10
  19.2 0.0 copy-start.7
  19.2 0.9 copy-done.7
  20.1 0.9 copy-done.9
  21.0 4.2 %shard_map.122 = (bf16[480,512]{1,0:T(8,128)(2,1)S(1)}, bf16[480,512]{1,0:T(8,128)(2,1)S(1)}, bf16[336,512]{1,0:T(8,128)(2,1)S(1)}, bf16[336,512]{1,0:T(8,128)(2...) custom-call(f32[8]{0:T(128)S(1)} %copy-done.10, ...), custom_call_target="tpu_custom_call" | custom-call | flops 4294967296 | bytes 4194304 | tf_op jit(solution)/shard_map/pallas_call | solution.py:466
  25.2 0.0 collective-permute-done.2.far_ref
  25.2 9.0 %shard_map.123 = (bf16[128,512]{1,0:T(8,128)(2,1)}, bf16[128,512]{1,0:T(8,128)(2,1)}, bf16[1024,128]{1,0:T(8,128)(2,1)S(1)}, bf16[128,1024]{1,0:T(8,128)(2,1)S(1)}, bf16[128,1024]{1,0:T(8,128)(2,1)S(1)}) custom-call(f32[8]{0:T(128)S(1)} %copy-done.10, bf16[256,512]{1,0:T(8,128)(2,1)S(1)} %get-tuple-element.25.own_ref, ...), custom_call_target="tpu_custom_call" | custom-call | flops 8589934592 | bytes 4194304 | tf_op jit(solution)/shard_map/pallas_call | solution.py:473
  34.2 0.0 collective-permute-start.6
  34.2 0.5 collective-permute-start.5
  34.7 1.0 %collective-permute-done.6.got_ref = bf16[128,1024]{1,0:T(8,128)(2,1)S(1)} collective-permute-done((bf16[128,1024]{1,0:T(8,128)(2,1)S(1)}, bf16[128,1024]{1,0:T(8,128)(2,1)S(1)}, u32[]{:S(2)}, u32[]{:S(2)}) %collective-permute-start.6) | collective-permute-done | bytes 262176 | tf_op jit(solution)/shard_map/ppermute | solution.py:422
  35.7 0.4 collective-permute-done.5.got_features_ref
  36.1 0.4 shard_map.124
  36.5 30.5 %all_to_all.10 = bf16[64,8,1024]{2,1,0:T(8,128)(2,1)S(1)} all-to-all(bf16[64,8,1024]{2,1,0:T(8,128)(2,1)S(1)} %bitcast.19), channel_id=1, replica_groups={{0,2,4,6,8,10,12,14,16,18,20,22,24,26,28,30,32,34,36,38,40,42,44,46,48,..., dimensions={0} | all-to-all | bytes 2097152 | tf_op jit(solution)/shard_map/all_to_all | solution.py:499
  67.0 0.2 shard_map.125
  67.2 21.0 %all_to_all.11 = bf16[64,8,1024]{2,1,0:T(8,128)(2,1)S(1)} all-to-all(bf16[64,8,1024]{2,1,0:T(8,128)(2,1)S(1)} %bitcast.21), channel_id=1, replica_groups={{0,2,4,6,8,10,12,14,16,18,20,22,24,26,28,30,32,34,36,38,40,42,44,46,48,..., dimensions={0} | all-to-all | bytes 2097152 | tf_op jit(solution)/shard_map/all_to_all | solution.py:499
  88.2 3.1 %collective-permute-start.7 = (bf16[512,1024]{1,0:T(8,128)(2,1)S(1)}, bf16[512,1024]{1,0:T(8,128)(2,1)S(1)}, u32[]{:S(2)}, u32[]{:S(2)}) collective-permute-start(bf16[512,1024]{1,0:T(8,128)(2,1)S(1)} %bitcast.17), channel_id=1, source_target_pairs={{0,1},{1,0},{2,3},{3,2},{4,5},{5,4},{6,7},{7,6},{8,9},{9,8},{10,11... | collective-permute-start | bytes 3145736 | tf_op jit(solution)/shard_map/ppermute | solution.py:422
  91.3 1.8 %shard_map.126 = (f32[512,1536]{1,0:T(8,128)}, f32[512,512]{1,0:T(8,128)}) custom-call(s32[1]{0:T(128)} %bitcast.7.half_ref, bf16[512,1024]{1,0:T(8,128)(2,1)S(1)} %bitcast.18), custom_call_target="tpu_custom_call" | custom-call | flops 1048576 | bytes 3145728 | tf_op jit(solution)/shard_map/pallas_call | solution.py:367
  93.1 0.5 collective-permute-done.7.half_grads_ref
  93.6 1.8 %shard_map.127 = (f32[512,1536]{1,0:T(8,128)}, f32[512,512]{1,0:T(8,128)}) custom-call(s32[1]{0:T(128)S(6)} %sub.3.half_ref, bf16[512,1024]{1,0:T(8,128)(2,1)S(1)} %collective-permute-done.7.half_grads_ref, f32[512,1536]{1,0:T(8,128)} %get-tuple-element.42.refs_0_, f32[512,512]{1,0:T(8,128)} %get-tuple-element.43.refs_1_), custom_call_target="tpu_custom_call", output_to_operand_aliasing={{0}: (2, {}), {1}: (3, {})} | custom-call | flops 1048576 | bytes 3145728 | tf_op jit(solution)/shard_map/pallas_call | solution.py:367
  (4 shorter events, 0.1 us)
Async XLA Ops:
  0.6 15.7 %copy-start = (bf16[256,512]{1,0:T(8,128)(2,1)S(1)}, bf16[256,512]{1,0:T(8,128)(2,1)}, u32[]{:S(2)}) copy-start(bf16[256,512]{1,0:T(8,128)(2,1)} %param.14) | copy-start | bytes 786436
  0.6 0.9 copy-start.1
  1.6 0.9 copy-start.2
  2.5 8.1 %collective-permute-start = (bf16[144,512]{1,0:T(8,128)(2,1)S(1)}, bf16[144,512]{1,0:T(8,128)(2,1)S(1)}, u32[]{:S(2)}, u32[]{:S(2)}) collective-permute-start(bf16[144,512]{1,0:T(8,128)(2,1)S(1)} %get-tuple-element.26), channel_id=1, source_target_pairs={{0,16},{1,17},{2,18},{3,19},{4,20},{5,21},{6,22},{7,23},{8,24},{9,... | collective-permute-start | bytes 442376 | tf_op jit(solution)/shard_map/ppermute | solution.py:422
  7.0 3.6 %collective-permute-start.1 = (bf16[144,512]{1,0:T(8,128)(2,1)S(1)}, bf16[144,512]{1,0:T(8,128)(2,1)S(1)}, u32[]{:S(2)}, u32[]{:S(2)}) collective-permute-start(bf16[144,512]{1,0:T(8,128)(2,1)S(1)} %get-tuple-element.27), channel_id=1, source_target_pairs={{16,32},{17,33},{18,34},{19,35},{20,36},{21,37},{22,38},{23,39},{2... | collective-permute-start | bytes 442376 | tf_op jit(solution)/shard_map/ppermute | solution.py:422
  7.7 11.4 %collective-permute-start.3 = (bf16[256,512]{1,0:T(8,128)(2,1)S(1)}, bf16[256,512]{1,0:T(8,128)(2,1)S(1)}, u32[]{:S(2)}, u32[]{:S(2)}) collective-permute-start(bf16[256,512]{1,0:T(8,128)(2,1)S(1)} %get-tuple-element.25.own_ref), channel_id=1, source_target_pairs={{0,1},{1,0},{2,3},{3,2},{4,5},{5,4},{6,7},{7,6},{8,9},{9,8},{10,11... | collective-permute-start | bytes 786440 | tf_op jit(solution)/shard_map/ppermute | solution.py:422
  9.5 9.7 %copy-start.3 = (bf16[512,1536]{1,0:T(8,128)(2,1)S(1)}, bf16[512,1536]{1,0:T(8,128)(2,1)}, u32[]{:S(2)}) copy-start(bf16[512,1536]{1,0:T(8,128)(2,1)} %win_ref.3) | copy-start | bytes 4718596
  9.5 9.7 %copy-start.4 = (bf16[512,512]{1,0:T(8,128)(2,1)S(1)}, bf16[512,512]{1,0:T(8,128)(2,1)}, u32[]{:S(2)}) copy-start(bf16[512,512]{1,0:T(8,128)(2,1)} %wo_ref.3) | copy-start | bytes 1572868
  9.5 9.7 %copy-start.10 = (f32[8]{0:T(128)S(1)}, f32[8]{0:T(128)}, u32[]{:S(2)}) copy-start(f32[8]{0:T(128)} %gain_ref.3) | copy-start | bytes 100
  10.6 0.7 copy-start.6
  10.6 0.7 copy-start.8
  11.3 0.7 copy-start.5
  12.0 7.1 %collective-permute-start.4 = (bf16[288,512]{1,0:T(8,128)(2,1)S(1)}, bf16[288,512]{1,0:T(8,128)(2,1)S(1)}, u32[]{:S(2)}, u32[]{:S(2)}) collective-permute-start(bf16[288,512]{1,0:T(8,128)(2,1)S(1)} %get-tuple-element.29), channel_id=1, source_target_pairs={{0,1},{1,0},{2,3},{3,2},{4,5},{5,4},{6,7},{7,6},{8,9},{9,8},{10,11... | collective-permute-start | bytes 884744 | tf_op jit(solution)/shard_map/ppermute | solution.py:422
  17.2 8.0 %collective-permute-start.2 = (bf16[176,512]{1,0:T(8,128)(2,1)}, bf16[176,512]{1,0:T(8,128)(2,1)S(1)}, u32[]{:S(2)}, u32[]{:S(2)}) collective-permute-start(bf16[176,512]{1,0:T(8,128)(2,1)} %copy-done.5), channel_id=1, source_target_pairs={{1,2},{2,1},{3,4},{4,3},{5,6},{6,5},{7,8},{8,7},{9,10},{10,9},{11,... | collective-permute-start | bytes 540680 | tf_op jit(solution)/shard_map/ppermute | solution.py:422
  19.2 0.9 copy-start.7
  20.1 0.9 copy-start.9
  34.2 1.5 %collective-permute-start.6 = (bf16[128,1024]{1,0:T(8,128)(2,1)S(1)}, bf16[128,1024]{1,0:T(8,128)(2,1)S(1)}, u32[]{:S(2)}, u32[]{:S(2)}) collective-permute-start(bf16[128,1024]{1,0:T(8,128)(2,1)S(1)} %get-tuple-element.41), channel_id=1, source_target_pairs={{0,1},{1,0},{2,3},{3,2},{4,5},{5,4},{6,7},{7,6},{8,9},{9,8},{10,11... | collective-permute-start | bytes 786440 | tf_op jit(solution)/shard_map/ppermute | solution.py:422
  34.2 1.9 %collective-permute-start.5 = (bf16[1024,128]{1,0:T(8,128)(2,1)S(1)}, bf16[1024,128]{1,0:T(8,128)(2,1)S(1)}, u32[]{:S(2)}, u32[]{:S(2)}) collective-permute-start(bf16[1024,128]{1,0:T(8,128)(2,1)S(1)} %get-tuple-element.39.features_ref), channel_id=1, source_target_pairs={{0,1},{1,0},{2,3},{3,2},{4,5},{5,4},{6,7},{7,6},{8,9},{9,8},{10,11... | collective-permute-start | bytes 786440 | tf_op jit(solution)/shard_map/ppermute | solution.py:422
  88.2 5.3 %collective-permute-start.7 = (bf16[512,1024]{1,0:T(8,128)(2,1)S(1)}, bf16[512,1024]{1,0:T(8,128)(2,1)S(1)}, u32[]{:S(2)}, u32[]{:S(2)}) collective-permute-start(bf16[512,1024]{1,0:T(8,128)(2,1)S(1)} %bitcast.17), channel_id=1, source_target_pairs={{0,1},{1,0},{2,3},{3,2},{4,5},{5,4},{6,7},{7,6},{8,9},{9,8},{10,11... | collective-permute-start | bytes 3145736 | tf_op jit(solution)/shard_map/ppermute | solution.py:422

commit v3 on v2

--- a/solution.py
+++ b/solution.py
@@ -12,8 +12,8 @@
 HEAD = 64
 BF16 = jnp.bfloat16
 F32 = jnp.float32
-VMEM_LIMIT = 40 * 1024 * 1024
-SMALL_LIMIT = 16 * 1024 * 1024
+VMEM_LIMIT = 28 * 1024 * 1024
+SMALL_LIMIT = 8 * 1024 * 1024
 AXES = ("rows", "cols")
 NEAR, FAR = 48, 16
 
@@ -101,7 +101,7 @@
             ref[96:144, :] = du_ref[0:48, :]
 
 
-def columns_kernel(own_ref, c_ref, d_ref, far_ref, both_ref):
+def columns_kernel(own_ref, c_ref, d_ref, _scale, _row, _bias, far_ref, both_ref):
     even = lax.axis_index("rows") % 2 == 0
     first_core = lax.axis_index("cols") % 2 == 0
     sub = lax.broadcasted_iota(jnp.int32, (8, 512), 0)
@@ -132,7 +132,7 @@
 
 
 def near_kernel(
-    gain_ref, own_ref, mate_ref, c_ref, d_ref, mate_rows_ref, win_ref, wo_ref, scale_ref,
+    gain_ref, own_ref, mate_ref, rows_ref, mate_rows_ref, win_ref, wo_ref, scale_ref,
     k_ref, v_ref, q_ref, do_ref, kraw_ref, qraw_ref, normed_ref,
     own_s, mate_s, du_s,
 ):
@@ -151,7 +151,7 @@
         else:
             above = row < 0
             j = (row + (6 if above else -8)) if first == 0 else 6 + (row + (3 if above else -8))
-            own = pick(block(c_ref, j), block(d_ref, j), above)
+            own = pick(block(rows_ref, j), block(rows_ref, 9 + j), above)
             mate = pick(block(mate_rows_ref, j), block(mate_rows_ref, 9 + j), above)
         return own, jnp.where(first_core, mate[:8], mate[8:])
 
@@ -195,9 +195,36 @@
                 qraw_ref[16 * at : 16 * at + 16, :] = raw[here : here + 16].astype(BF16)
 
 
+def mask_kernel(row_ref, bias_ref):
+    my_col = lax.axis_index("cols")
+    first_core = my_col % 2 == 0
+    mate_base = jnp.where(first_core, 16, -8)
+    far_base = jnp.where(first_core, -6, 16)
+
+    def places(index, near):
+        in_near = index < near
+        pair = jnp.where(in_near, index // NEAR, 0)
+        j = jnp.where(in_near, index % NEAR, index - near)
+        mine = in_near & (j < 32)
+        eights = jnp.where(in_near, j - 32, j)
+        row = jnp.where(mine, 2 * pair + j // 16, 2 * pair + eights // 8)
+        slot = eights % 8
+        far_col = jnp.where(slot < 6, far_base + slot, 1000)
+        return row, jnp.where(mine, j % 16, jnp.where(in_near, mate_base + slot, far_col))
+
+    key_row, key_col = places(lax.broadcasted_iota(jnp.int32, (256, 128), 0), 4 * NEAR)
+    query_row, query_col = places(lax.broadcasted_iota(jnp.int32, (256, 128), 1) % 64, NEAR)
+    row_gap, col_gap = key_row - query_row, key_col - query_col
+    near = (row_gap >= 0) & (row_gap <= 6) & (col_gap >= -3) & (col_gap <= 3) & (key_col < 1000)
+    image_col = key_col + 16 * my_col
+    near = near & (image_col >= 0) & (image_col < 16 * lax.axis_size("cols"))
+    row_ref[...] = key_row
+    bias_ref[...] = jnp.where(near, 0.0, -1e30)
+
+
 def main_kernel(
     gain_ref, own_ref, far_ref, kn_ref, vn_ref, qn_ref, don_ref, kraw_ref, qraw_ref, normed_ref,
-    win_ref, wo_ref, scale_ref,
+    row_ref, bias_ref, win_ref, wo_ref, scale_ref,
     out_ref, dx_ref, features_ref, send_ref, keep_ref,
     kf_s, vf_s, qf_s, dof_s, att_s, dq_s, dk_s, dv_s, gp_s,
 ):
@@ -236,34 +263,12 @@
     qf_s[...] = (unit(raw, ones) * gain).astype(BF16)
     dof_s[...] = mm_nt(jnp.concatenate(du_far, axis=0).astype(BF16), wo_ref[...]).astype(BF16)
 
-    mate_base = jnp.where(first_core, 16, -8)
-    far_base = jnp.where(first_core, -6, 16)
-
-    def places(index, near):
-        in_near = index < near
-        pair = jnp.where(in_near, index // NEAR, 0)
-        j = jnp.where(in_near, index % NEAR, index - near)
-        mine = in_near & (j < 32)
-        eights = jnp.where(in_near, j - 32, j)
-        row = jnp.where(mine, 2 * pair + j // 16, 2 * pair + eights // 8)
-        slot = eights % 8
-        far_col = jnp.where(slot < 6, far_base + slot, 1000)
-        return row, jnp.where(mine, j % 16, jnp.where(in_near, mate_base + slot, far_col))
-
-    key_row, key_col = places(lax.broadcasted_iota(jnp.int32, (256, 128), 0), 4 * NEAR)
-    query_row, query_col = places(lax.broadcasted_iota(jnp.int32, (256, 128), 1) % 64, NEAR)
-    row_gap, col_gap = key_row - query_row, key_col - query_col
-    near = (row_gap >= 0) & (row_gap <= 6) & (col_gap >= -3) & (col_gap <= 3) & (key_col < 1000)
-    image_col = key_col + 16 * my_col
-    near = near & (image_col >= 0) & (image_col < 16 * lax.axis_size("cols"))
-    bias_near = jnp.where(near, 0.0, -1e30)
-
     dk_s[...] = jnp.zeros_like(dk_s)
     dv_s[...] = jnp.zeros_like(dv_s)
     for i in range(7):
-        image_row = key_row + (8 * my_row - 6 + 2 * i)
+        image_row = row_ref[...] + (8 * my_row - 6 + 2 * i)
         inside = (image_row >= 0) & (image_row < 8 * lax.axis_size("rows"))
-        bias = jnp.where(inside, bias_near, -1e30)
+        bias = jnp.where(inside, bias_ref[...], -1e30)
         bias = jnp.concatenate([bias, bias], axis=1)
         blocks = range(max(i, 3), min(i + 4, 7))
         there = slice(32 * (blocks[0] - 3), 32 * (blocks[-1] - 2))
@@ -289,7 +294,7 @@
             weight = jnp.exp(scores - jnp.max(scores, axis=0, keepdims=True))
             weight = weight * (1.0 / jnp.sum(weight, axis=0, keepdims=True))
             prob = weight.astype(BF16)
-            dprob = mm_nt(v_t, do_h).astype(BF16).astype(F32)
+            dprob = mm_nt(v_t, do_h)
             mean = jnp.sum(weight * dprob, axis=0, keepdims=True)
             dscore = (weight * (dprob - mean)).astype(BF16)
             dv_s[there, lanes] += mm(own_keys(prob), do_h)
@@ -355,35 +360,47 @@
         out_ref[step * i : step * (i + 1), :] = block
 
 
-def final_kernel(half_ref, half_grads_ref, *refs):
-    qkv_ref, out_ref = refs[-2:]
-    qkv_ref[...] = half_grads_ref[:, 0:768].astype(F32)
-    out_ref[...] = half_grads_ref[:, 768:1024].astype(F32)
-
-
-def write_half(half, half_grads, *whole):
-    steps = 4
-    rows = half_grads.shape[0] // steps
+def final_kernel(mine, grads_ref, *refs):
+    qkv_ref, out_ref, qkv_s, out_s, sems = refs[-5:]
+    steps = sems.shape[1]
+    rows = grads_ref.shape[0] // steps
+    for core in range(2):
+
+        @pl.when(lax.axis_index("cols") % 2 == core)
+        def _():
+            half = core if mine else 1 - core
+            copies = []
+            for i in range(steps):
+                part = slice(rows * i, rows * (i + 1))
+                qkv_s[part, :] = grads_ref[part, 0:768].astype(F32)
+                out_s[part, :] = grads_ref[part, 768:1024].astype(F32)
+                lanes = slice(768 * half, 768 * half + 768)
+                copies.append(pltpu.make_async_copy(qkv_s.at[part], qkv_ref.at[part, lanes], sems.at[0, i]))
+                lanes = slice(256 * half, 256 * half + 256)
+                copies.append(pltpu.make_async_copy(out_s.at[part], out_ref.at[part, lanes], sems.at[1, i]))
+                copies[-2].start()
+                copies[-1].start()
+            for copy in copies:
+                copy.wait()
+
+
+def write_half(mine, half_grads, *whole):
+    unplaced = pl.BlockSpec(memory_space=pl.ANY)
     return pl.pallas_call(
-        final_kernel,
-        grid_spec=pltpu.PrefetchScalarGridSpec(
-            num_scalar_prefetch=1,
-            grid=(steps,),
-            in_specs=[pl.BlockSpec((rows, 1024), lambda i, half: (i, 0))]
-            + [pl.BlockSpec(memory_space=pl.ANY)] * len(whole),
-            out_specs=[
-                pl.BlockSpec((rows, 768), lambda i, half: (i, half[0])),
-                pl.BlockSpec((rows, 256), lambda i, half: (i, half[0])),
-            ],
-        ),
+        functools.partial(final_kernel, mine),
+        in_specs=[pl.BlockSpec(memory_space=pltpu.VMEM)] + [unplaced] * len(whole),
+        out_specs=[unplaced, unplaced],
         out_shape=[
             jax.ShapeDtypeStruct((512, 1536), F32),
             jax.ShapeDtypeStruct((512, 512), F32),
         ],
-        input_output_aliases={2: 0, 3: 1} if whole else {},
-        compiler_params=pltpu.CompilerParams(vmem_limit_bytes=8 * 1024 * 1024),
+        scratch_shapes=[
+            pltpu.VMEM((512, 768), F32), pltpu.VMEM((512, 256), F32), pltpu.SemaphoreType.DMA((2, 8)),
+        ],
+        input_output_aliases={1: 0, 2: 1} if whole else {},
+        compiler_params=pltpu.CompilerParams(vmem_limit_bytes=SMALL_LIMIT),
         cost_estimate=pl.CostEstimate(flops=1 << 20, bytes_accessed=3 << 20, transcendentals=0),
-    )(half, half_grads, *whole)
+    )(half_grads, *whole)
 
 
 def call(kernel, outs, scratch=(), flops=0, scalars=0, inputs=0, limit=VMEM_LIMIT):
@@ -456,19 +473,23 @@
     scale = condition(
         noise_level_step, picture_category_label, category_gain_offset, noise_level_gain_matrix
     )
-    half = (lax.axis_index("cols") % 2).astype(jnp.int32).reshape(1)
-    to_far, to_mate = call(
-        columns_kernel, (bf(176, width), bf(288, width)), flops=16 << 30, inputs=3, limit=SMALL_LIMIT
-    )(own, from_c, from_d)
+    mask = call(
+        mask_kernel,
+        (jax.ShapeDtypeStruct((256, 128), jnp.int32), jax.ShapeDtypeStruct((256, 128), F32)),
+        limit=SMALL_LIMIT,
+    )()
+    to_far, rows = call(
+        columns_kernel, (bf(176, width), bf(288, width)), flops=16 << 30, inputs=6, limit=SMALL_LIMIT
+    )(own, from_c, from_d, scale, *mask)
     far = swapped(to_far, same, across)
-    mate_rows = swapped(to_mate, same, paired)
+    mate_rows = swapped(rows, same, paired)
     weights = (attention_input_matrix, final_projection_matrix, scale)
     k, v, q, do, kraw, qraw, normed = call(
         near_kernel,
         (bf(480, width), bf(480, width), bf(336, width), bf(336, width), bf(128, width), bf(128, width), bf(128, width)),
         scratch=[vm((320, 512), F32), vm((160, 512), F32), vm((336, 512), BF16)],
-        flops=4 << 30, scalars=1, inputs=8,
-    )(cosine_logit_gain, own, mate, from_c, from_d, mate_rows, *weights)
+        flops=4 << 30, scalars=1, inputs=7,
+    )(cosine_logit_gain, own, mate, rows, mate_rows, *weights)
 
     output, grad_latent, features, send, keep = call(
         main_kernel,
@@ -478,8 +499,8 @@
             vm((128, 512), BF16), vm((128, 512), BF16), vm((128, 512), F32), vm((128, 512), F32),
             vm((128, 1536), BF16),
         ],
-        flops=8 << 30, scalars=1, inputs=12,
-    )(cosine_logit_gain, own, far, k, v, q, do, kraw, qraw, normed, *weights)
+        flops=8 << 30, scalars=1, inputs=14,
+    )(cosine_logit_gain, own, far, k, v, q, do, kraw, qraw, normed, *mask, *weights)
 
     got_features = swapped(features, same, paired)
     got = swapped(send, same, paired)
@@ -505,7 +526,7 @@
     )(exchange(partial))
     mine = exchange(summed)
     other = swapped(mine, same, paired)
-    qkv_grad, out_grad = write_half(1 - half, other, *write_half(half, mine))
+    qkv_grad, out_grad = write_half(False, other, *write_half(True, mine))
     return output.reshape(x.shape), grad_latent.reshape(x.shape), qkv_grad, out_grad
 
 

time: 95.7 us -> 92.1 us (0.962)
  local copies, waits for them, and re-layouts: 4.86 us -> 1.87 us
    unnamed x22 -> x12, local copies, waits for them, and re-layouts: 4.86 us -> 1.86 us
    pallas_call x2 -> x3, Pallas kernels: 3.59 us -> 3.19 us  [the longest x2 2.89 us: write_half(): pl.pallas_call(functools.partial(final_kernel, mine), in_specs=[pl.BlockS...]
  transfers between devices with their start and end apart: 8 -> 8, of which waited for: 4 -> 5; matrix products, arithmetic and copies ran while one was open for 1% -> 1% of each run, Pallas kernels for 6% -> 7%
where the time goes in v3:
time: 92.1 us; the launch traced here: 91.8 us
  blocking collectives  52.1 us (57%)
  Pallas kernels  16.9 us (18%)
  starting transfers between devices  14.5 us (16%)
  waiting for transfers between devices  3.17 us (3%)
  between operations  2.26 us (2%)
  local copies, waits for them, and re-layouts  1.87 us (2%)
    all_to_all x2, blocking collectives, exchange(): lax.all_to_all(value.reshape(members, each, 1024), AXES, 0, 0, axis_index...  52.1 us
    ppermute x8, starting transfers between devices, swapped(): return lax.ppermute(value, AXES, pairs)  14.5 us
    pallas_call x1, Pallas kernels, per_device(): call(main_kernel, (bf(tokens, width), bf(tokens, width), bf(1024, tokens)...  8.57 us
    pallas_call x1, Pallas kernels, per_device(): call(near_kernel, (bf(480, width), bf(480, width), bf(336, width), bf(336...  4.26 us
    ppermute x8, waiting for transfers between devices, swapped(): return lax.ppermute(value, AXES, pairs)  3.17 us
    pallas_call x2, Pallas kernels, write_half(): pl.pallas_call(functools.partial(final_kernel, mine), in_specs=[pl.BlockS...  2.89 us
    unnamed x12, local copies, waits for them, and re-layouts  1.86 us
  transfers between devices with their start and end apart: 8, of which 5 were waited for; matrix products, arithmetic and copies ran while one was open for 1% of the time, Pallas kernels for 7%

profile of v3, /device:TPU:1, one launch (start us, length us, event | category | flops | bytes accessed | tf_op | source)
XLA Modules:
  0.0 91.8 jit_solution(15488949995227817662)
XLA Ops:
  0.6 0.0 copy-start
  0.6 0.0 copy-start.1
  0.7 0.9 %copy-done.1 = bf16[8,16,512]{2,1,0:T(8,128)(2,1)S(1)} copy-done((bf16[8,16,512]{2,1,0:T(8,128)(2,1)S(1)}, bf16[8,16,512]{2,1,0:T(8,128)(2,1)}, u32[]{:S(2)}) %copy-start.1) | copy-done | bytes 131096
  1.6 0.0 copy-start.2
  1.6 0.9 copy-done.2
  2.5 4.5 %collective-permute-start = (bf16[144,512]{1,0:T(8,128)(2,1)S(1)}, bf16[144,512]{1,0:T(8,128)(2,1)S(1)}, u32[]{:S(2)}, u32[]{:S(2)}) collective-permute-start(bf16[144,512]{1,0:T(8,128)(2,1)S(1)} %get-tuple-element.28), channel_id=1, source_target_pairs={{0,16},{1,17},{2,18},{3,19},{4,20},{5,21},{6,22},{7,23},{8,24},{9,... | collective-permute-start | bytes 442376 | tf_op jit(solution)/shard_map/ppermute | solution.py:439
  7.0 0.7 collective-permute-start.1
  7.7 0.3 shard_map.121
  9.3 0.1 sine_convert_fusion
  9.4 0.0 copy-done
  9.4 0.8 convolution_add_fusion._scale.scale_ref
  10.3 0.4 collective-permute-done.c_ref
  10.6 0.0 collective-permute-done.1.d_ref
  10.6 0.0 copy-start.3
  10.6 0.0 copy-start.4
  10.6 0.0 copy-start.5
  10.6 0.2 shard_map.122
  10.8 3.8 %collective-permute-start.4 = (bf16[288,512]{1,0:T(8,128)(2,1)S(1)}, bf16[288,512]{1,0:T(8,128)(2,1)S(1)}, u32[]{:S(2)}, u32[]{:S(2)}) collective-permute-start(bf16[288,512]{1,0:T(8,128)(2,1)S(1)} %get-tuple-element.33.rows_ref), channel_id=1, source_target_pairs={{0,1},{1,0},{2,3},{3,2},{4,5},{5,4},{6,7},{7,6},{8,9},{9,8},{10,11... | collective-permute-start | bytes 884744 | tf_op jit(solution)/shard_map/ppermute | solution.py:439
  14.6 0.1 collective-permute-start.3
  14.7 1.9 %collective-permute-start.2 = (bf16[176,512]{1,0:T(8,128)(2,1)S(1)}, bf16[176,512]{1,0:T(8,128)(2,1)S(1)}, u32[]{:S(2)}, u32[]{:S(2)}) collective-permute-start(bf16[176,512]{1,0:T(8,128)(2,1)S(1)} %get-tuple-element.32), channel_id=1, source_target_pairs={{1,2},{2,1},{3,4},{4,3},{5,6},{6,5},{7,8},{8,7},{9,10},{10,9},{11,... | collective-permute-start | bytes 540680 | tf_op jit(solution)/shard_map/ppermute | solution.py:439
  16.6 0.0 collective-permute-done.3.mate_ref
  16.6 0.0 collective-permute-done.4.mate_rows_ref
  16.6 0.0 copy-done.3
  16.6 0.0 copy-done.4
  16.7 0.0 copy-done.5
  16.7 4.3 %shard_map.123 = (bf16[480,512]{1,0:T(8,128)(2,1)S(1)}, bf16[480,512]{1,0:T(8,128)(2,1)S(1)}, bf16[336,512]{1,0:T(8,128)(2,1)S(1)}, bf16[336,512]{1,0:T(8,128)(2...) custom-call(f32[8]{0:T(128)S(1)} %copy-done.5, ...), custom_call_target="tpu_custom_call" | custom-call | flops 4294967296 | bytes 4194304 | tf_op jit(solution)/shard_map/pallas_call | solution.py:487
  20.9 0.6 collective-permute-done.2.far_ref
  21.5 8.6 %shard_map.124 = (bf16[128,512]{1,0:T(8,128)(2,1)}, bf16[128,512]{1,0:T(8,128)(2,1)}, bf16[1024,128]{1,0:T(8,128)(2,1)S(1)}, bf16[128,1024]{1,0:T(8,128)(2,1)S(1)}, bf16[128,1024]{1,0:T(8,128)(2,1)S(1)}) custom-call(f32[8]{0:T(128)S(1)} %copy-done.5, bf16[256,512]{1,0:T(8,128)(2,1)S(1)} %get-tuple-element.27.own_ref, ...), custom_call_target="tpu_custom_call" | custom-call | flops 8589934592 | bytes 4194304 | tf_op jit(solution)/shard_map/pallas_call | solution.py:494
  30.1 0.0 collective-permute-start.6
  30.1 0.5 collective-permute-start.5
  30.6 1.0 %collective-permute-done.6.got_ref = bf16[128,1024]{1,0:T(8,128)(2,1)S(1)} collective-permute-done((bf16[128,1024]{1,0:T(8,128)(2,1)S(1)}, bf16[128,1024]{1,0:T(8,128)(2,1)S(1)}, u32[]{:S(2)}, u32[]{:S(2)}) %collective-permute-start.6) | collective-permute-done | bytes 262176 | tf_op jit(solution)/shard_map/ppermute | solution.py:439
  31.6 0.4 collective-permute-done.5.got_features_ref
  32.0 0.4 shard_map.125
  32.4 30.9 %all_to_all.10 = bf16[64,8,1024]{2,1,0:T(8,128)(2,1)S(1)} all-to-all(bf16[64,8,1024]{2,1,0:T(8,128)(2,1)S(1)} %bitcast.18), channel_id=1, replica_groups={{0,2,4,6,8,10,12,14,16,18,20,22,24,26,28,30,32,34,36,38,40,42,44,46,48,..., dimensions={0} | all-to-all | bytes 2097152 | tf_op jit(solution)/shard_map/all_to_all | solution.py:520
  63.4 0.2 shard_map.126
  63.6 21.2 %all_to_all.11 = bf16[64,8,1024]{2,1,0:T(8,128)(2,1)S(1)} all-to-all(bf16[64,8,1024]{2,1,0:T(8,128)(2,1)S(1)} %bitcast.20), channel_id=1, replica_groups={{0,2,4,6,8,10,12,14,16,18,20,22,24,26,28,30,32,34,36,38,40,42,44,46,48,..., dimensions={0} | all-to-all | bytes 2097152 | tf_op jit(solution)/shard_map/all_to_all | solution.py:520
  84.8 3.1 %collective-permute-start.7 = (bf16[512,1024]{1,0:T(8,128)(2,1)S(1)}, bf16[512,1024]{1,0:T(8,128)(2,1)S(1)}, u32[]{:S(2)}, u32[]{:S(2)}) collective-permute-start(bf16[512,1024]{1,0:T(8,128)(2,1)S(1)} %bitcast.16), channel_id=1, source_target_pairs={{0,1},{1,0},{2,3},{3,2},{4,5},{5,4},{6,7},{7,6},{8,9},{9,8},{10,11... | collective-permute-start | bytes 3145736 | tf_op jit(solution)/shard_map/ppermute | solution.py:439
  87.9 1.4 %shard_map.127 = (f32[512,1536]{1,0:T(8,128)}, f32[512,512]{1,0:T(8,128)}) custom-call(bf16[512,1024]{1,0:T(8,128)(2,1)S(1)} %bitcast.17), custom_call_target="tpu_custom_call" | custom-call | flops 1048576 | bytes 3145728 | tf_op jit(solution)/shard_map/pallas_call | solution.py:389
  89.3 0.8 collective-permute-done.7.grads_ref
  90.1 1.4 %shard_map.128 = (f32[512,1536]{1,0:T(8,128)}, f32[512,512]{1,0:T(8,128)}) custom-call(bf16[512,1024]{1,0:T(8,128)(2,1)S(1)} %collective-permute-done.7.grads_ref, f32[512,1536]{1,0:T(8,128)} %get-tuple-element.46.refs_0_, f32[512,512]{1,0:T(8,128)} %get-tuple-element.47.refs_1_), custom_call_target="tpu_custom_call", output_to_operand_aliasing={{0}: (1, {}), {1}: (2, {})} | custom-call | flops 1048576 | bytes 3145728 | tf_op jit(solution)/shard_map/pallas_call | solution.py:389
  (3 shorter events, 0.1 us)
Async XLA Ops:
  0.6 8.8 %copy-start = (bf16[256,512]{1,0:T(8,128)(2,1)S(1)}, bf16[256,512]{1,0:T(8,128)(2,1)}, u32[]{:S(2)}) copy-start(bf16[256,512]{1,0:T(8,128)(2,1)} %param.14) | copy-start | bytes 786436
  0.6 0.9 %copy-start.1 = (bf16[8,16,512]{2,1,0:T(8,128)(2,1)S(1)}, bf16[8,16,512]{2,1,0:T(8,128)(2,1)}, u32[]{:S(2)}) copy-start(bf16[8,16,512]{2,1,0:T(8,128)(2,1)} %param.9) | copy-start | bytes 393220
  1.6 0.9 copy-start.2
  2.5 8.1 %collective-permute-start = (bf16[144,512]{1,0:T(8,128)(2,1)S(1)}, bf16[144,512]{1,0:T(8,128)(2,1)S(1)}, u32[]{:S(2)}, u32[]{:S(2)}) collective-permute-start(bf16[144,512]{1,0:T(8,128)(2,1)S(1)} %get-tuple-element.28), channel_id=1, source_target_pairs={{0,16},{1,17},{2,18},{3,19},{4,20},{5,21},{6,22},{7,23},{8,24},{9,... | collective-permute-start | bytes 442376 | tf_op jit(solution)/shard_map/ppermute | solution.py:439
  7.0 3.6 %collective-permute-start.1 = (bf16[144,512]{1,0:T(8,128)(2,1)S(1)}, bf16[144,512]{1,0:T(8,128)(2,1)S(1)}, u32[]{:S(2)}, u32[]{:S(2)}) collective-permute-start(bf16[144,512]{1,0:T(8,128)(2,1)S(1)} %get-tuple-element.29), channel_id=1, source_target_pairs={{16,32},{17,33},{18,34},{19,35},{20,36},{21,37},{22,38},{23,39},{2... | collective-permute-start | bytes 442376 | tf_op jit(solution)/shard_map/ppermute | solution.py:439
  10.6 6.0 %copy-start.3 = (bf16[512,1536]{1,0:T(8,128)(2,1)S(1)}, bf16[512,1536]{1,0:T(8,128)(2,1)}, u32[]{:S(2)}) copy-start(bf16[512,1536]{1,0:T(8,128)(2,1)} %win_ref.3) | copy-start | bytes 4718596
  10.6 6.0 %copy-start.4 = (bf16[512,512]{1,0:T(8,128)(2,1)S(1)}, bf16[512,512]{1,0:T(8,128)(2,1)}, u32[]{:S(2)}) copy-start(bf16[512,512]{1,0:T(8,128)(2,1)} %wo_ref.3) | copy-start | bytes 1572868
  10.6 6.0 %copy-start.5 = (f32[8]{0:T(128)S(1)}, f32[8]{0:T(128)}, u32[]{:S(2)}) copy-start(f32[8]{0:T(128)} %gain_ref.3) | copy-start | bytes 100
  10.8 5.8 %collective-permute-start.4 = (bf16[288,512]{1,0:T(8,128)(2,1)S(1)}, bf16[288,512]{1,0:T(8,128)(2,1)S(1)}, u32[]{:S(2)}, u32[]{:S(2)}) collective-permute-start(bf16[288,512]{1,0:T(8,128)(2,1)S(1)} %get-tuple-element.33.rows_ref), channel_id=1, source_target_pairs={{0,1},{1,0},{2,3},{3,2},{4,5},{5,4},{6,7},{7,6},{8,9},{9,8},{10,11... | collective-permute-start | bytes 884744 | tf_op jit(solution)/shard_map/ppermute | solution.py:439
  14.6 2.0 %collective-permute-start.3 = (bf16[256,512]{1,0:T(8,128)(2,1)S(1)}, bf16[256,512]{1,0:T(8,128)(2,1)S(1)}, u32[]{:S(2)}, u32[]{:S(2)}) collective-permute-start(bf16[256,512]{1,0:T(8,128)(2,1)S(1)} %get-tuple-element.27.own_ref), channel_id=1, source_target_pairs={{0,1},{1,0},{2,3},{3,2},{4,5},{5,4},{6,7},{7,6},{8,9},{9,8},{10,11... | collective-permute-start | bytes 786440 | tf_op jit(solution)/shard_map/ppermute | solution.py:439
  14.7 6.8 %collective-permute-start.2 = (bf16[176,512]{1,0:T(8,128)(2,1)S(1)}, bf16[176,512]{1,0:T(8,128)(2,1)S(1)}, u32[]{:S(2)}, u32[]{:S(2)}) collective-permute-start(bf16[176,512]{1,0:T(8,128)(2,1)S(1)} %get-tuple-element.32), channel_id=1, source_target_pairs={{1,2},{2,1},{3,4},{4,3},{5,6},{6,5},{7,8},{8,7},{9,10},{10,9},{11,... | collective-permute-start | bytes 540680 | tf_op jit(solution)/shard_map/ppermute | solution.py:439
  30.1 1.5 %collective-permute-start.6 = (bf16[128,1024]{1,0:T(8,128)(2,1)S(1)}, bf16[128,1024]{1,0:T(8,128)(2,1)S(1)}, u32[]{:S(2)}, u32[]{:S(2)}) collective-permute-start(bf16[128,1024]{1,0:T(8,128)(2,1)S(1)} %get-tuple-element.45), channel_id=1, source_target_pairs={{0,1},{1,0},{2,3},{3,2},{4,5},{5,4},{6,7},{7,6},{8,9},{9,8},{10,11... | collective-permute-start | bytes 786440 | tf_op jit(solution)/shard_map/ppermute | solution.py:439
  30.1 1.9 %collective-permute-start.5 = (bf16[1024,128]{1,0:T(8,128)(2,1)S(1)}, bf16[1024,128]{1,0:T(8,128)(2,1)S(1)}, u32[]{:S(2)}, u32[]{:S(2)}) collective-permute-start(bf16[1024,128]{1,0:T(8,128)(2,1)S(1)} %get-tuple-element.43.features_ref), channel_id=1, source_target_pairs={{0,1},{1,0},{2,3},{3,2},{4,5},{5,4},{6,7},{7,6},{8,9},{9,8},{10,11... | collective-permute-start | bytes 786440 | tf_op jit(solution)/shard_map/ppermute | solution.py:439
  84.8 5.4 %collective-permute-start.7 = (bf16[512,1024]{1,0:T(8,128)(2,1)S(1)}, bf16[512,1024]{1,0:T(8,128)(2,1)S(1)}, u32[]{:S(2)}, u32[]{:S(2)}) collective-permute-start(bf16[512,1024]{1,0:T(8,128)(2,1)S(1)} %bitcast.16), channel_id=1, source_target_pairs={{0,1},{1,0},{2,3},{3,2},{4,5},{5,4},{6,7},{7,6},{8,9},{9,8},{10,11... | collective-permute-start | bytes 3145736 | tf_op jit(solution)/shard_map/ppermute | solution.py:439

commit v4 on v3

--- a/solution.py
+++ b/solution.py
@@ -84,24 +84,22 @@
     return raw * lax.rsqrt(head_sums(raw * raw, ones) + 1e-06)
 
 
-def rows_kernel(x_ref, du_ref, c_ref, d_ref, own_ref):
+def rows_kernel(own_ref, c_ref, d_ref):
     even = lax.axis_index("rows") % 2 == 0
-    own_ref[0:128, :] = x_ref[...]
-    own_ref[128:256, :] = du_ref[...]
     for ref, take_last in ((c_ref, even), (d_ref, jnp.logical_not(even))):
 
         @pl.when(take_last)
         def _():
-            ref[0:96, :] = x_ref[32:128, :]
-            ref[96:144, :] = du_ref[80:128, :]
+            ref[0:96, :] = own_ref[32:128, :]
+            ref[96:144, :] = own_ref[208:256, :]
 
         @pl.when(jnp.logical_not(take_last))
         def _():
-            ref[0:96, :] = x_ref[0:96, :]
-            ref[96:144, :] = du_ref[0:48, :]
-
-
-def columns_kernel(own_ref, c_ref, d_ref, _scale, _row, _bias, far_ref, both_ref):
+            ref[0:96, :] = own_ref[0:96, :]
+            ref[96:144, :] = own_ref[128:176, :]
+
+
+def columns_kernel(own_ref, c_ref, d_ref, _mate, _scale, _row, _bias, far_ref, both_ref):
     even = lax.axis_index("rows") % 2 == 0
     first_core = lax.axis_index("cols") % 2 == 0
     sub = lax.broadcasted_iota(jnp.int32, (8, 512), 0)
@@ -462,11 +460,10 @@
     tokens = height * columns
     bf = lambda *shape: jax.ShapeDtypeStruct(shape, BF16)
     vm = pltpu.VMEM
-    x2, du2 = x.reshape(tokens, width), du.reshape(tokens, width)
-
-    to_c, to_d, own = call(
-        rows_kernel, (bf(144, width), bf(144, width), bf(256, width)), inputs=2, limit=SMALL_LIMIT
-    )(x2, du2)
+    own = jnp.concatenate([x, du], axis=0).reshape(2 * tokens, width)
+    to_c, to_d = call(
+        rows_kernel, (bf(144, width), bf(144, width)), inputs=1, limit=SMALL_LIMIT
+    )(own)
     from_c = swapped(to_c, paired, same)
     from_d = swapped(to_d, across, same)
     mate = swapped(own, same, paired)
@@ -479,8 +476,8 @@
         limit=SMALL_LIMIT,
     )()
     to_far, rows = call(
-        columns_kernel, (bf(176, width), bf(288, width)), flops=16 << 30, inputs=6, limit=SMALL_LIMIT
-    )(own, from_c, from_d, scale, *mask)
+        columns_kernel, (bf(176, width), bf(288, width)), flops=16 << 30, inputs=7, limit=SMALL_LIMIT
+    )(own, from_c, from_d, mate, scale, *mask)
     far = swapped(to_far, same, across)
     mate_rows = swapped(rows, same, paired)
     weights = (attention_input_matrix, final_projection_matrix, scale)
@@ -488,7 +485,7 @@
         near_kernel,
         (bf(480, width), bf(480, width), bf(336, width), bf(336, width), bf(128, width), bf(128, width), bf(128, width)),
         scratch=[vm((320, 512), F32), vm((160, 512), F32), vm((336, 512), BF16)],
-        flops=4 << 30, scalars=1, inputs=7,
+        flops=1 << 20, scalars=1, inputs=7,
     )(cosine_logit_gain, own, mate, rows, mate_rows, *weights)
 
     output, grad_latent, features, send, keep = call(

time: 92.1 us -> 91.6 us (level)
  local copies, waits for them, and re-layouts: 1.87 us -> 0.03 us
  other arithmetic: 0.06 us -> 1.09 us
    unnamed x12 -> x8, local copies, waits for them, and re-layouts: 1.86 us -> 0.03 us
    concatenate x0 -> x1, other arithmetic: none -> 1.04 us  [per_device(): own = jnp.concatenate([x, du], axis=0).reshape(2 * tokens, width)]
  transfers between devices with their start and end apart: 8 -> 8, of which waited for: 5 -> 5; matrix products, arithmetic and copies ran while one was open for 1% -> 1% of each run, Pallas kernels for 7% -> 6%
where the time goes in v4:
time: 91.6 us; the launch traced here: 91.3 us
  blocking collectives  51.8 us (57%)
  Pallas kernels  16.8 us (18%)
  starting transfers between devices  14.6 us (16%)
  waiting for transfers between devices  3.91 us (4%)
  between operations  2.26 us (2%)
  other arithmetic  1.09 us (1%)
    all_to_all x2, blocking collectives, exchange(): lax.all_to_all(value.reshape(members, each, 1024), AXES, 0, 0, axis_index...  51.8 us
    ppermute x8, starting transfers between devices, swapped(): return lax.ppermute(value, AXES, pairs)  14.6 us
    pallas_call x1, Pallas kernels, per_device(): call(main_kernel, (bf(tokens, width), bf(tokens, width), bf(1024, tokens)...  8.52 us
    pallas_call x1, Pallas kernels, per_device(): call(near_kernel, (bf(480, width), bf(480, width), bf(336, width), bf(336...  4.14 us
    ppermute x8, waiting for transfers between devices, swapped(): return lax.ppermute(value, AXES, pairs)  3.91 us
    pallas_call x2, Pallas kernels, write_half(): pl.pallas_call(functools.partial(final_kernel, mine), in_specs=[pl.BlockS...  2.89 us
  transfers between devices with their start and end apart: 8, of which 5 were waited for; matrix products, arithmetic and copies ran while one was open for 1% of the time, Pallas kernels for 6%

profile of v4, /device:TPU:1, one launch (start us, length us, event | category | flops | bytes accessed | tf_op | source)
XLA Modules:
  0.0 91.3 jit_solution(8581082438362235758)
XLA Ops:
  0.6 0.0 copy-start
  0.6 1.0 %pad_maximum_fusion = bf16[16,16,512]{2,1,0:T(8,128)(2,1)S(1)} fusion(bf16[8,16,512]{2,1,0:T(8,128)(2,1)} %param.10, bf16[8,16,512]{2,1,0:T(8,128)(2,1)} %param.9), kind=kLoop, calls=%fused_computation.1 | loop fusion | flops 131072 | bytes 524288 | tf_op jit(solution)/shard_map/concatenate | solution.py:463
  1.7 1.5 %collective-permute-start.2 = (bf16[256,512]{1,0:T(8,128)(2,1)S(1)}, bf16[256,512]{1,0:T(8,128)(2,1)S(1)}, u32[]{:S(2)}, u32[]{:S(2)}) collective-permute-start(bf16[256,512]{1,0:T(8,128)(2,1)S(1)} %bitcast.20), channel_id=1, source_target_pairs={{0,1},{1,0},{2,3},{3,2},{4,5},{5,4},{6,7},{7,6},{8,9},{9,8},{10,11... | collective-permute-start | bytes 786440 | tf_op jit(solution)/shard_map/ppermute | solution.py:437
  3.2 3.8 %collective-permute-start = (bf16[144,512]{1,0:T(8,128)(2,1)S(1)}, bf16[144,512]{1,0:T(8,128)(2,1)S(1)}, u32[]{:S(2)}, u32[]{:S(2)}) collective-permute-start(bf16[144,512]{1,0:T(8,128)(2,1)S(1)} %get-tuple-element.26), channel_id=1, source_target_pairs={{0,16},{1,17},{2,18},{3,19},{4,20},{5,21},{6,22},{7,23},{8,24},{9,... | collective-permute-start | bytes 442376 | tf_op jit(solution)/shard_map/ppermute | solution.py:437
  7.0 0.7 collective-permute-start.1
  8.3 0.1 sine_convert_fusion
  8.4 0.3 shard_map.121
  9.3 0.0 copy-done
  9.3 0.8 convolution_add_fusion._scale.scale_ref
  10.2 1.0 %collective-permute-done.c_ref = bf16[144,512]{1,0:T(8,128)(2,1)S(1)} collective-permute-done((bf16[144,512]{1,0:T(8,128)(2,1)S(1)}, bf16[144,512]{1,0:T(8,128)(2,1)S(1)}, u32[]{:S(2)}, u32[]{:S(2)}) %collective-permute-start) | collective-permute-done | bytes 147488 | tf_op jit(solution)/shard_map/ppermute | solution.py:437
  11.2 0.0 collective-permute-done.1.d_ref
  11.2 0.0 collective-permute-done.2._mate.mate_ref
  11.2 0.0 copy-start.1
  11.2 0.0 copy-start.2
  11.2 0.0 copy-start.3
  11.2 0.2 shard_map.122
  11.4 3.1 %collective-permute-start.4 = (bf16[288,512]{1,0:T(8,128)(2,1)S(1)}, bf16[288,512]{1,0:T(8,128)(2,1)S(1)}, u32[]{:S(2)}, u32[]{:S(2)}) collective-permute-start(bf16[288,512]{1,0:T(8,128)(2,1)S(1)} %get-tuple-element.31.rows_ref), channel_id=1, source_target_pairs={{0,1},{1,0},{2,3},{3,2},{4,5},{5,4},{6,7},{7,6},{8,9},{9,8},{10,11... | collective-permute-start | bytes 884744 | tf_op jit(solution)/shard_map/ppermute | solution.py:437
  14.5 1.9 %collective-permute-start.3 = (bf16[176,512]{1,0:T(8,128)(2,1)S(1)}, bf16[176,512]{1,0:T(8,128)(2,1)S(1)}, u32[]{:S(2)}, u32[]{:S(2)}) collective-permute-start(bf16[176,512]{1,0:T(8,128)(2,1)S(1)} %get-tuple-element.30), channel_id=1, source_target_pairs={{1,2},{2,1},{3,4},{4,3},{5,6},{6,5},{7,8},{8,7},{9,10},{10,9},{11,... | collective-permute-start | bytes 540680 | tf_op jit(solution)/shard_map/ppermute | solution.py:437
  16.5 0.0 collective-permute-done.4.mate_rows_ref
  16.5 0.0 copy-done.1
  16.5 0.0 copy-done.2
  16.5 0.0 copy-done.3
  16.5 4.1 %shard_map.123 = (bf16[480,512]{1,0:T(8,128)(2,1)S(1)}, bf16[480,512]{1,0:T(8,128)(2,1)S(1)}, bf16[336,512]{1,0:T(8,128)(2,1)S(1)}, bf16[336,512]{1,0:T(8,128)(2...) custom-call(f32[8]{0:T(128)S(1)} %copy-done.3, ...), custom_call_target="tpu_custom_call" | custom-call | flops 1048576 | bytes 4194304 | tf_op jit(solution)/shard_map/pallas_call | solution.py:484
  20.7 0.7 collective-permute-done.3.far_ref
  21.3 8.5 %shard_map.124 = (bf16[128,512]{1,0:T(8,128)(2,1)}, bf16[128,512]{1,0:T(8,128)(2,1)}, bf16[1024,128]{1,0:T(8,128)(2,1)S(1)}, bf16[128,1024]{1,0:T(8,128)(2,1)S(1)}, bf16[128,1024]{1,0:T(8,128)(2,1)S(1)}) custom-call(f32[8]{0:T(128)S(1)} %copy-done.3, bf16[256,512]{1,0:T(8,128)(2,1)S(1)} %bitcast.24, bf16[176,512]{1,0:T(8,128)(2,1)S(1)} %collective-permute-done.3.far_ref, ...), custom_call_target="tpu_custom_call" | custom-call | flops 8589934592 | bytes 4194304 | tf_op jit(solution)/shard_map/pallas_call | solution.py:491
  29.9 0.0 collective-permute-start.6
  29.9 0.5 collective-permute-start.5
  30.4 1.0 %collective-permute-done.6.got_ref = bf16[128,1024]{1,0:T(8,128)(2,1)S(1)} collective-permute-done((bf16[128,1024]{1,0:T(8,128)(2,1)S(1)}, bf16[128,1024]{1,0:T(8,128)(2,1)S(1)}, u32[]{:S(2)}, u32[]{:S(2)}) %collective-permute-start.6) | collective-permute-done | bytes 262176 | tf_op jit(solution)/shard_map/ppermute | solution.py:437
  31.4 0.4 collective-permute-done.5.got_features_ref
  31.8 0.4 shard_map.125
  32.2 30.7 %all_to_all.10 = bf16[64,8,1024]{2,1,0:T(8,128)(2,1)S(1)} all-to-all(bf16[64,8,1024]{2,1,0:T(8,128)(2,1)S(1)} %bitcast.17), channel_id=1, replica_groups={{0,2,4,6,8,10,12,14,16,18,20,22,24,26,28,30,32,34,36,38,40,42,44,46,48,..., dimensions={0} | all-to-all | bytes 2097152 | tf_op jit(solution)/shard_map/all_to_all | solution.py:517
  62.9 0.2 shard_map.126
  63.1 21.2 %all_to_all.11 = bf16[64,8,1024]{2,1,0:T(8,128)(2,1)S(1)} all-to-all(bf16[64,8,1024]{2,1,0:T(8,128)(2,1)S(1)} %bitcast.19), channel_id=1, replica_groups={{0,2,4,6,8,10,12,14,16,18,20,22,24,26,28,30,32,34,36,38,40,42,44,46,48,..., dimensions={0} | all-to-all | bytes 2097152 | tf_op jit(solution)/shard_map/all_to_all | solution.py:517
  84.3 3.1 %collective-permute-start.7 = (bf16[512,1024]{1,0:T(8,128)(2,1)S(1)}, bf16[512,1024]{1,0:T(8,128)(2,1)S(1)}, u32[]{:S(2)}, u32[]{:S(2)}) collective-permute-start(bf16[512,1024]{1,0:T(8,128)(2,1)S(1)} %bitcast.15), channel_id=1, source_target_pairs={{0,1},{1,0},{2,3},{3,2},{4,5},{5,4},{6,7},{7,6},{8,9},{9,8},{10,11... | collective-permute-start | bytes 3145736 | tf_op jit(solution)/shard_map/ppermute | solution.py:437
  87.4 1.4 %shard_map.127 = (f32[512,1536]{1,0:T(8,128)}, f32[512,512]{1,0:T(8,128)}) custom-call(bf16[512,1024]{1,0:T(8,128)(2,1)S(1)} %bitcast.16), custom_call_target="tpu_custom_call" | custom-call | flops 1048576 | bytes 3145728 | tf_op jit(solution)/shard_map/pallas_call | solution.py:387
  88.9 0.8 collective-permute-done.7.grads_ref
  89.7 1.4 %shard_map.128 = (f32[512,1536]{1,0:T(8,128)}, f32[512,512]{1,0:T(8,128)}) custom-call(bf16[512,1024]{1,0:T(8,128)(2,1)S(1)} %collective-permute-done.7.grads_ref, f32[512,1536]{1,0:T(8,128)} %get-tuple-element.44.refs_0_, f32[512,512]{1,0:T(8,128)} %get-tuple-element.45.refs_1_), custom_call_target="tpu_custom_call", output_to_operand_aliasing={{0}: (1, {}), {1}: (2, {})} | custom-call | flops 1048576 | bytes 3145728 | tf_op jit(solution)/shard_map/pallas_call | solution.py:387
  (3 shorter events, 0.0 us)
Async XLA Ops:
  0.6 8.7 %copy-start = (bf16[256,512]{1,0:T(8,128)(2,1)S(1)}, bf16[256,512]{1,0:T(8,128)(2,1)}, u32[]{:S(2)}) copy-start(bf16[256,512]{1,0:T(8,128)(2,1)} %param.14) | copy-start | bytes 786436
  1.7 9.5 %collective-permute-start.2 = (bf16[256,512]{1,0:T(8,128)(2,1)S(1)}, bf16[256,512]{1,0:T(8,128)(2,1)S(1)}, u32[]{:S(2)}, u32[]{:S(2)}) collective-permute-start(bf16[256,512]{1,0:T(8,128)(2,1)S(1)} %bitcast.20), channel_id=1, source_target_pairs={{0,1},{1,0},{2,3},{3,2},{4,5},{5,4},{6,7},{7,6},{8,9},{9,8},{10,11... | collective-permute-start | bytes 786440 | tf_op jit(solution)/shard_map/ppermute | solution.py:437
  3.2 7.9 %collective-permute-start = (bf16[144,512]{1,0:T(8,128)(2,1)S(1)}, bf16[144,512]{1,0:T(8,128)(2,1)S(1)}, u32[]{:S(2)}, u32[]{:S(2)}) collective-permute-start(bf16[144,512]{1,0:T(8,128)(2,1)S(1)} %get-tuple-element.26), channel_id=1, source_target_pairs={{0,16},{1,17},{2,18},{3,19},{4,20},{5,21},{6,22},{7,23},{8,24},{9,... | collective-permute-start | bytes 442376 | tf_op jit(solution)/shard_map/ppermute | solution.py:437
  7.0 4.2 %collective-permute-start.1 = (bf16[144,512]{1,0:T(8,128)(2,1)S(1)}, bf16[144,512]{1,0:T(8,128)(2,1)S(1)}, u32[]{:S(2)}, u32[]{:S(2)}) collective-permute-start(bf16[144,512]{1,0:T(8,128)(2,1)S(1)} %get-tuple-element.27), channel_id=1, source_target_pairs={{16,32},{17,33},{18,34},{19,35},{20,36},{21,37},{22,38},{23,39},{2... | collective-permute-start | bytes 442376 | tf_op jit(solution)/shard_map/ppermute | solution.py:437
  11.2 5.3 %copy-start.1 = (bf16[512,1536]{1,0:T(8,128)(2,1)S(1)}, bf16[512,1536]{1,0:T(8,128)(2,1)}, u32[]{:S(2)}) copy-start(bf16[512,1536]{1,0:T(8,128)(2,1)} %win_ref.3) | copy-start | bytes 4718596
  11.2 5.3 %copy-start.2 = (bf16[512,512]{1,0:T(8,128)(2,1)S(1)}, bf16[512,512]{1,0:T(8,128)(2,1)}, u32[]{:S(2)}) copy-start(bf16[512,512]{1,0:T(8,128)(2,1)} %wo_ref.3) | copy-start | bytes 1572868
  11.2 5.3 %copy-start.3 = (f32[8]{0:T(128)S(1)}, f32[8]{0:T(128)}, u32[]{:S(2)}) copy-start(f32[8]{0:T(128)} %gain_ref.3) | copy-start | bytes 100
  11.4 5.1 %collective-permute-start.4 = (bf16[288,512]{1,0:T(8,128)(2,1)S(1)}, bf16[288,512]{1,0:T(8,128)(2,1)S(1)}, u32[]{:S(2)}, u32[]{:S(2)}) collective-permute-start(bf16[288,512]{1,0:T(8,128)(2,1)S(1)} %get-tuple-element.31.rows_ref), channel_id=1, source_target_pairs={{0,1},{1,0},{2,3},{3,2},{4,5},{5,4},{6,7},{7,6},{8,9},{9,8},{10,11... | collective-permute-start | bytes 884744 | tf_op jit(solution)/shard_map/ppermute | solution.py:437
  14.5 6.8 %collective-permute-start.3 = (bf16[176,512]{1,0:T(8,128)(2,1)S(1)}, bf16[176,512]{1,0:T(8,128)(2,1)S(1)}, u32[]{:S(2)}, u32[]{:S(2)}) collective-permute-start(bf16[176,512]{1,0:T(8,128)(2,1)S(1)} %get-tuple-element.30), channel_id=1, source_target_pairs={{1,2},{2,1},{3,4},{4,3},{5,6},{6,5},{7,8},{8,7},{9,10},{10,9},{11,... | collective-permute-start | bytes 540680 | tf_op jit(solution)/shard_map/ppermute | solution.py:437
  29.9 1.5 %collective-permute-start.6 = (bf16[128,1024]{1,0:T(8,128)(2,1)S(1)}, bf16[128,1024]{1,0:T(8,128)(2,1)S(1)}, u32[]{:S(2)}, u32[]{:S(2)}) collective-permute-start(bf16[128,1024]{1,0:T(8,128)(2,1)S(1)} %get-tuple-element.43), channel_id=1, source_target_pairs={{0,1},{1,0},{2,3},{3,2},{4,5},{5,4},{6,7},{7,6},{8,9},{9,8},{10,11... | collective-permute-start | bytes 786440 | tf_op jit(solution)/shard_map/ppermute | solution.py:437
  29.9 1.9 %collective-permute-start.5 = (bf16[1024,128]{1,0:T(8,128)(2,1)S(1)}, bf16[1024,128]{1,0:T(8,128)(2,1)S(1)}, u32[]{:S(2)}, u32[]{:S(2)}) collective-permute-start(bf16[1024,128]{1,0:T(8,128)(2,1)S(1)} %get-tuple-element.41.features_ref), channel_id=1, source_target_pairs={{0,1},{1,0},{2,3},{3,2},{4,5},{5,4},{6,7},{7,6},{8,9},{9,8},{10,11... | collective-permute-start | bytes 786440 | tf_op jit(solution)/shard_map/ppermute | solution.py:437
  84.3 5.4 %collective-permute-start.7 = (bf16[512,1024]{1,0:T(8,128)(2,1)S(1)}, bf16[512,1024]{1,0:T(8,128)(2,1)S(1)}, u32[]{:S(2)}, u32[]{:S(2)}) collective-permute-start(bf16[512,1024]{1,0:T(8,128)(2,1)S(1)} %bitcast.15), channel_id=1, source_target_pairs={{0,1},{1,0},{2,3},{3,2},{4,5},{5,4},{6,7},{7,6},{8,9},{9,8},{10,11... | collective-permute-start | bytes 3145736 | tf_op jit(solution)/shard_map/ppermute | solution.py:437

commit v5 on v4

--- a/solution.py
+++ b/solution.py
@@ -84,8 +84,9 @@
     return raw * lax.rsqrt(head_sums(raw * raw, ones) + 1e-06)
 
 
-def rows_kernel(own_ref, c_ref, d_ref):
+def rows_kernel(own_ref, d_ref, c_ref, copy_ref):
     even = lax.axis_index("rows") % 2 == 0
+    copy_ref[...] = own_ref[...]
     for ref, take_last in ((c_ref, even), (d_ref, jnp.logical_not(even))):
 
         @pl.when(take_last)
@@ -99,7 +100,7 @@
             ref[96:144, :] = own_ref[128:176, :]
 
 
-def columns_kernel(own_ref, c_ref, d_ref, _mate, _scale, _row, _bias, far_ref, both_ref):
+def columns_kernel(own_ref, d_ref, c_ref, _mate, _scale, _row, _bias, far_ref, both_ref):
     even = lax.axis_index("rows") % 2 == 0
     first_core = lax.axis_index("cols") % 2 == 0
     sub = lax.broadcasted_iota(jnp.int32, (8, 512), 0)
@@ -461,11 +462,11 @@
     bf = lambda *shape: jax.ShapeDtypeStruct(shape, BF16)
     vm = pltpu.VMEM
     own = jnp.concatenate([x, du], axis=0).reshape(2 * tokens, width)
-    to_c, to_d = call(
-        rows_kernel, (bf(144, width), bf(144, width)), inputs=1, limit=SMALL_LIMIT
+    to_d, to_c, own = call(
+        rows_kernel, (bf(144, width), bf(144, width), bf(256, width)), inputs=1, limit=SMALL_LIMIT
     )(own)
+    from_d = swapped(to_d, across, same)
     from_c = swapped(to_c, paired, same)
-    from_d = swapped(to_d, across, same)
     mate = swapped(own, same, paired)
     scale = condition(
         noise_level_step, picture_category_label, category_gain_offset, noise_level_gain_matrix
@@ -477,7 +478,7 @@
     )()
     to_far, rows = call(
         columns_kernel, (bf(176, width), bf(288, width)), flops=16 << 30, inputs=7, limit=SMALL_LIMIT
-    )(own, from_c, from_d, mate, scale, *mask)
+    )(own, from_d, from_c, mate, scale, *mask)
     far = swapped(to_far, same, across)
     mate_rows = swapped(rows, same, paired)
     weights = (attention_input_matrix, final_projection_matrix, scale)

time: 91.6 us -> 93.4 us (1.020)
  starting transfers between devices: 14.6 us -> 15.9 us
    ppermute x8, starting transfers between devices: 14.6 us -> 15.9 us  [swapped(): return lax.ppermute(value, AXES, pairs)]
where the time goes in v5:
time: 93.4 us; the launch traced here: 93.1 us
  blocking collectives  51.5 us (55%)
  Pallas kernels  16.8 us (18%)
  starting transfers between devices  15.9 us (17%)
  waiting for transfers between devices  4.77 us (5%)
  between operations  2.25 us (2%)
  other arithmetic  1.09 us (1%)
    all_to_all x2, blocking collectives, exchange(): lax.all_to_all(value.reshape(members, each, 1024), AXES, 0, 0, axis_index...  51.5 us
    ppermute x8, starting transfers between devices, swapped(): return lax.ppermute(value, AXES, pairs)  15.9 us
    pallas_call x1, Pallas kernels, per_device(): call(main_kernel, (bf(tokens, width), bf(tokens, width), bf(1024, tokens)...  8.52 us
    ppermute x8, waiting for transfers between devices, swapped(): return lax.ppermute(value, AXES, pairs)  4.77 us
    pallas_call x1, Pallas kernels, per_device(): call(near_kernel, (bf(480, width), bf(480, width), bf(336, width), bf(336...  4.16 us
    pallas_call x2, Pallas kernels, write_half(): pl.pallas_call(functools.partial(final_kernel, mine), in_specs=[pl.BlockS...  2.89 us
  transfers between devices with their start and end apart: 8, of which 5 were waited for; matrix products, arithmetic and copies ran while one was open for 1% of the time, Pallas kernels for 6%

profile of v5, /device:TPU:1, one launch (start us, length us, event | category | flops | bytes accessed | tf_op | source)
XLA Modules:
  0.0 93.1 jit_solution(1491458734572453032)
XLA Ops:
  0.6 0.0 copy-start
  0.6 1.0 %pad_maximum_fusion = bf16[16,16,512]{2,1,0:T(8,128)(2,1)S(1)} fusion(bf16[8,16,512]{2,1,0:T(8,128)(2,1)} %param.10, bf16[8,16,512]{2,1,0:T(8,128)(2,1)} %param.9), kind=kLoop, calls=%fused_computation.1 | loop fusion | flops 131072 | bytes 524288 | tf_op jit(solution)/shard_map/concatenate | solution.py:464
  1.7 0.7 collective-permute-start
  2.4 6.0 %collective-permute-start.1 = (bf16[144,512]{1,0:T(8,128)(2,1)S(1)}, bf16[144,512]{1,0:T(8,128)(2,1)S(1)}, u32[]{:S(2)}, u32[]{:S(2)}) collective-permute-start(bf16[144,512]{1,0:T(8,128)(2,1)S(1)} %get-tuple-element.29), channel_id=1, source_target_pairs={{0,16},{1,17},{2,18},{3,19},{4,20},{5,21},{6,22},{7,23},{8,24},{9,... | collective-permute-start | bytes 442376 | tf_op jit(solution)/shard_map/ppermute | solution.py:438
  8.5 1.2 %collective-permute-start.2 = (bf16[256,512]{1,0:T(8,128)(2,1)S(1)}, bf16[256,512]{1,0:T(8,128)(2,1)S(1)}, u32[]{:S(2)}, u32[]{:S(2)}) collective-permute-start(bf16[256,512]{1,0:T(8,128)(2,1)S(1)} %get-tuple-element.27.own_ref), channel_id=1, source_target_pairs={{0,1},{1,0},{2,3},{3,2},{4,5},{5,4},{6,7},{7,6},{8,9},{9,8},{10,11... | collective-permute-start | bytes 786440 | tf_op jit(solution)/shard_map/ppermute | solution.py:438
  10.3 0.1 sine_convert_fusion
  10.4 0.3 shard_map.121
  11.4 0.0 copy-done
  11.4 0.8 convolution_add_fusion._scale.scale_ref
  12.2 0.0 collective-permute-done.d_ref
  12.2 2.4 %collective-permute-done.1.c_ref = bf16[144,512]{1,0:T(8,128)(2,1)S(1)} collective-permute-done((bf16[144,512]{1,0:T(8,128)(2,1)S(1)}, bf16[144,512]{1,0:T(8,128)(2,1)S(1)}, u32[]{:S(2)}, u32[]{:S(2)}) %collective-permute-start.1) | collective-permute-done | bytes 147488 | tf_op jit(solution)/shard_map/ppermute | solution.py:438
  14.6 0.0 collective-permute-done.2._mate.mate_ref
  14.6 0.0 copy-start.1
  14.6 0.0 copy-start.2
  14.6 0.0 copy-start.3
  14.6 0.2 shard_map.122
  14.9 1.1 %collective-permute-start.4 = (bf16[288,512]{1,0:T(8,128)(2,1)S(1)}, bf16[288,512]{1,0:T(8,128)(2,1)S(1)}, u32[]{:S(2)}, u32[]{:S(2)}) collective-permute-start(bf16[288,512]{1,0:T(8,128)(2,1)S(1)} %get-tuple-element.33.rows_ref), channel_id=1, source_target_pairs={{0,1},{1,0},{2,3},{3,2},{4,5},{5,4},{6,7},{7,6},{8,9},{9,8},{10,11... | collective-permute-start | bytes 884744 | tf_op jit(solution)/shard_map/ppermute | solution.py:438
  16.0 3.2 %collective-permute-start.3 = (bf16[176,512]{1,0:T(8,128)(2,1)S(1)}, bf16[176,512]{1,0:T(8,128)(2,1)S(1)}, u32[]{:S(2)}, u32[]{:S(2)}) collective-permute-start(bf16[176,512]{1,0:T(8,128)(2,1)S(1)} %get-tuple-element.32), channel_id=1, source_target_pairs={{1,2},{2,1},{3,4},{4,3},{5,6},{6,5},{7,8},{8,7},{9,10},{10,9},{11,... | collective-permute-start | bytes 540680 | tf_op jit(solution)/shard_map/ppermute | solution.py:438
  19.2 0.0 collective-permute-done.4.mate_rows_ref
  19.2 0.0 copy-done.1
  19.2 0.0 copy-done.2
  19.2 0.0 copy-done.3
  19.2 4.2 %shard_map.123 = (bf16[480,512]{1,0:T(8,128)(2,1)S(1)}, bf16[480,512]{1,0:T(8,128)(2,1)S(1)}, bf16[336,512]{1,0:T(8,128)(2,1)S(1)}, bf16[336,512]{1,0:T(8,128)(2...) custom-call(f32[8]{0:T(128)S(1)} %copy-done.3, ...), custom_call_target="tpu_custom_call" | custom-call | flops 1048576 | bytes 4194304 | tf_op jit(solution)/shard_map/pallas_call | solution.py:485
  23.4 0.1 collective-permute-done.3.far_ref
  23.5 8.5 %shard_map.124 = (bf16[128,512]{1,0:T(8,128)(2,1)}, bf16[128,512]{1,0:T(8,128)(2,1)}, bf16[1024,128]{1,0:T(8,128)(2,1)S(1)}, bf16[128,1024]{1,0:T(8,128)(2,1)S(1)}, bf16[128,1024]{1,0:T(8,128)(2,1)S(1)}) custom-call(f32[8]{0:T(128)S(1)} %copy-done.3, bf16[256,512]{1,0:T(8,128)(2,1)S(1)} %get-tuple-element.27.own_ref, ...), custom_call_target="tpu_custom_call" | custom-call | flops 8589934592 | bytes 4194304 | tf_op jit(solution)/shard_map/pallas_call | solution.py:492
  32.0 0.0 collective-permute-start.6
  32.0 0.5 collective-permute-start.5
  32.5 1.0 %collective-permute-done.6.got_ref = bf16[128,1024]{1,0:T(8,128)(2,1)S(1)} collective-permute-done((bf16[128,1024]{1,0:T(8,128)(2,1)S(1)}, bf16[128,1024]{1,0:T(8,128)(2,1)S(1)}, u32[]{:S(2)}, u32[]{:S(2)}) %collective-permute-start.6) | collective-permute-done | bytes 262176 | tf_op jit(solution)/shard_map/ppermute | solution.py:438
  33.6 0.4 collective-permute-done.5.got_features_ref
  33.9 0.4 shard_map.125
  34.4 30.3 %all_to_all.10 = bf16[64,8,1024]{2,1,0:T(8,128)(2,1)S(1)} all-to-all(bf16[64,8,1024]{2,1,0:T(8,128)(2,1)S(1)} %bitcast.17), channel_id=1, replica_groups={{0,2,4,6,8,10,12,14,16,18,20,22,24,26,28,30,32,34,36,38,40,42,44,46,48,..., dimensions={0} | all-to-all | bytes 2097152 | tf_op jit(solution)/shard_map/all_to_all | solution.py:518
  64.7 0.2 shard_map.126
  64.9 21.2 %all_to_all.11 = bf16[64,8,1024]{2,1,0:T(8,128)(2,1)S(1)} all-to-all(bf16[64,8,1024]{2,1,0:T(8,128)(2,1)S(1)} %bitcast.19), channel_id=1, replica_groups={{0,2,4,6,8,10,12,14,16,18,20,22,24,26,28,30,32,34,36,38,40,42,44,46,48,..., dimensions={0} | all-to-all | bytes 2097152 | tf_op jit(solution)/shard_map/all_to_all | solution.py:518
  86.1 3.1 %collective-permute-start.7 = (bf16[512,1024]{1,0:T(8,128)(2,1)S(1)}, bf16[512,1024]{1,0:T(8,128)(2,1)S(1)}, u32[]{:S(2)}, u32[]{:S(2)}) collective-permute-start(bf16[512,1024]{1,0:T(8,128)(2,1)S(1)} %bitcast.15), channel_id=1, source_target_pairs={{0,1},{1,0},{2,3},{3,2},{4,5},{5,4},{6,7},{7,6},{8,9},{9,8},{10,11... | collective-permute-start | bytes 3145736 | tf_op jit(solution)/shard_map/ppermute | solution.py:438
  89.2 1.4 %shard_map.127 = (f32[512,1536]{1,0:T(8,128)}, f32[512,512]{1,0:T(8,128)}) custom-call(bf16[512,1024]{1,0:T(8,128)(2,1)S(1)} %bitcast.16), custom_call_target="tpu_custom_call" | custom-call | flops 1048576 | bytes 3145728 | tf_op jit(solution)/shard_map/pallas_call | solution.py:388
  90.6 0.8 collective-permute-done.7.grads_ref
  91.5 1.4 %shard_map.128 = (f32[512,1536]{1,0:T(8,128)}, f32[512,512]{1,0:T(8,128)}) custom-call(bf16[512,1024]{1,0:T(8,128)(2,1)S(1)} %collective-permute-done.7.grads_ref, f32[512,1536]{1,0:T(8,128)} %get-tuple-element.46.refs_0_, f32[512,512]{1,0:T(8,128)} %get-tuple-element.47.refs_1_), custom_call_target="tpu_custom_call", output_to_operand_aliasing={{0}: (1, {}), {1}: (2, {})} | custom-call | flops 1048576 | bytes 3145728 | tf_op jit(solution)/shard_map/pallas_call | solution.py:388
  (3 shorter events, 0.1 us)
Async XLA Ops:
  0.6 10.8 %copy-start = (bf16[256,512]{1,0:T(8,128)(2,1)S(1)}, bf16[256,512]{1,0:T(8,128)(2,1)}, u32[]{:S(2)}) copy-start(bf16[256,512]{1,0:T(8,128)(2,1)} %param.14) | copy-start | bytes 786436
  1.7 10.5 %collective-permute-start = (bf16[144,512]{1,0:T(8,128)(2,1)S(1)}, bf16[144,512]{1,0:T(8,128)(2,1)S(1)}, u32[]{:S(2)}, u32[]{:S(2)}) collective-permute-start(bf16[144,512]{1,0:T(8,128)(2,1)S(1)} %get-tuple-element.28), channel_id=1, source_target_pairs={{16,32},{17,33},{18,34},{19,35},{20,36},{21,37},{22,38},{23,39},{2... | collective-permute-start | bytes 442376 | tf_op jit(solution)/shard_map/ppermute | solution.py:438
  2.4 12.2 %collective-permute-start.1 = (bf16[144,512]{1,0:T(8,128)(2,1)S(1)}, bf16[144,512]{1,0:T(8,128)(2,1)S(1)}, u32[]{:S(2)}, u32[]{:S(2)}) collective-permute-start(bf16[144,512]{1,0:T(8,128)(2,1)S(1)} %get-tuple-element.29), channel_id=1, source_target_pairs={{0,16},{1,17},{2,18},{3,19},{4,20},{5,21},{6,22},{7,23},{8,24},{9,... | collective-permute-start | bytes 442376 | tf_op jit(solution)/shard_map/ppermute | solution.py:438
  8.5 6.2 %collective-permute-start.2 = (bf16[256,512]{1,0:T(8,128)(2,1)S(1)}, bf16[256,512]{1,0:T(8,128)(2,1)S(1)}, u32[]{:S(2)}, u32[]{:S(2)}) collective-permute-start(bf16[256,512]{1,0:T(8,128)(2,1)S(1)} %get-tuple-element.27.own_ref), channel_id=1, source_target_pairs={{0,1},{1,0},{2,3},{3,2},{4,5},{5,4},{6,7},{7,6},{8,9},{9,8},{10,11... | collective-permute-start | bytes 786440 | tf_op jit(solution)/shard_map/ppermute | solution.py:438
  14.6 4.5 %copy-start.1 = (bf16[512,1536]{1,0:T(8,128)(2,1)S(1)}, bf16[512,1536]{1,0:T(8,128)(2,1)}, u32[]{:S(2)}) copy-start(bf16[512,1536]{1,0:T(8,128)(2,1)} %win_ref.3) | copy-start | bytes 4718596
  14.6 4.5 %copy-start.2 = (bf16[512,512]{1,0:T(8,128)(2,1)S(1)}, bf16[512,512]{1,0:T(8,128)(2,1)}, u32[]{:S(2)}) copy-start(bf16[512,512]{1,0:T(8,128)(2,1)} %wo_ref.3) | copy-start | bytes 1572868
  14.6 4.5 %copy-start.3 = (f32[8]{0:T(128)S(1)}, f32[8]{0:T(128)}, u32[]{:S(2)}) copy-start(f32[8]{0:T(128)} %gain_ref.3) | copy-start | bytes 100
  14.9 4.3 %collective-permute-start.4 = (bf16[288,512]{1,0:T(8,128)(2,1)S(1)}, bf16[288,512]{1,0:T(8,128)(2,1)S(1)}, u32[]{:S(2)}, u32[]{:S(2)}) collective-permute-start(bf16[288,512]{1,0:T(8,128)(2,1)S(1)} %get-tuple-element.33.rows_ref), channel_id=1, source_target_pairs={{0,1},{1,0},{2,3},{3,2},{4,5},{5,4},{6,7},{7,6},{8,9},{9,8},{10,11... | collective-permute-start | bytes 884744 | tf_op jit(solution)/shard_map/ppermute | solution.py:438
  16.0 7.5 %collective-permute-start.3 = (bf16[176,512]{1,0:T(8,128)(2,1)S(1)}, bf16[176,512]{1,0:T(8,128)(2,1)S(1)}, u32[]{:S(2)}, u32[]{:S(2)}) collective-permute-start(bf16[176,512]{1,0:T(8,128)(2,1)S(1)} %get-tuple-element.32), channel_id=1, source_target_pairs={{1,2},{2,1},{3,4},{4,3},{5,6},{6,5},{7,8},{8,7},{9,10},{10,9},{11,... | collective-permute-start | bytes 540680 | tf_op jit(solution)/shard_map/ppermute | solution.py:438
  32.0 1.5 %collective-permute-start.6 = (bf16[128,1024]{1,0:T(8,128)(2,1)S(1)}, bf16[128,1024]{1,0:T(8,128)(2,1)S(1)}, u32[]{:S(2)}, u32[]{:S(2)}) collective-permute-start(bf16[128,1024]{1,0:T(8,128)(2,1)S(1)} %get-tuple-element.45), channel_id=1, source_target_pairs={{0,1},{1,0},{2,3},{3,2},{4,5},{5,4},{6,7},{7,6},{8,9},{9,8},{10,11... | collective-permute-start | bytes 786440 | tf_op jit(solution)/shard_map/ppermute | solution.py:438
  32.0 1.9 %collective-permute-start.5 = (bf16[1024,128]{1,0:T(8,128)(2,1)S(1)}, bf16[1024,128]{1,0:T(8,128)(2,1)S(1)}, u32[]{:S(2)}, u32[]{:S(2)}) collective-permute-start(bf16[1024,128]{1,0:T(8,128)(2,1)S(1)} %get-tuple-element.43.features_ref), channel_id=1, source_target_pairs={{0,1},{1,0},{2,3},{3,2},{4,5},{5,4},{6,7},{7,6},{8,9},{9,8},{10,11... | collective-permute-start | bytes 786440 | tf_op jit(solution)/shard_map/ppermute | solution.py:438
  86.1 5.4 %collective-permute-start.7 = (bf16[512,1024]{1,0:T(8,128)(2,1)S(1)}, bf16[512,1024]{1,0:T(8,128)(2,1)S(1)}, u32[]{:S(2)}, u32[]{:S(2)}) collective-permute-start(bf16[512,1024]{1,0:T(8,128)(2,1)S(1)} %bitcast.15), channel_id=1, source_target_pairs={{0,1},{1,0},{2,3},{3,2},{4,5},{5,4},{6,7},{7,6},{8,9},{9,8},{10,11... | collective-permute-start | bytes 3145736 | tf_op jit(solution)/shard_map/ppermute | solution.py:438

commit v6 on v4

--- a/solution.py
+++ b/solution.py
@@ -84,8 +84,9 @@
     return raw * lax.rsqrt(head_sums(raw * raw, ones) + 1e-06)
 
 
-def rows_kernel(own_ref, c_ref, d_ref):
+def rows_kernel(own_ref, c_ref, d_ref, copy_ref):
     even = lax.axis_index("rows") % 2 == 0
+    copy_ref[...] = own_ref[...]
     for ref, take_last in ((c_ref, even), (d_ref, jnp.logical_not(even))):
 
         @pl.when(take_last)
@@ -223,8 +224,8 @@
 def main_kernel(
     gain_ref, own_ref, far_ref, kn_ref, vn_ref, qn_ref, don_ref, kraw_ref, qraw_ref, normed_ref,
     row_ref, bias_ref, win_ref, wo_ref, scale_ref,
-    out_ref, dx_ref, features_ref, send_ref, keep_ref,
-    kf_s, vf_s, qf_s, dof_s, att_s, dq_s, dk_s, dv_s, gp_s,
+    out_ref, dx_ref, send_ref, keep_ref,
+    out_s, dx_s, sems, kf_s, vf_s, qf_s, dof_s, att_s, dq_s, dk_s, dv_s, gp_s,
 ):
     my_row, my_col = lax.axis_index("rows"), lax.axis_index("cols")
     even = my_row % 2 == 0
@@ -309,7 +310,11 @@
     att = att_s[...]
     normed = normed_ref[...]
     x = own_ref[0:128, :].astype(F32)
-    out_ref[...] = (x + mm(att, wo_ref[...])).astype(BF16)
+    out_s[...] = (x + mm(att, wo_ref[...])).astype(BF16)
+    copies = [pltpu.make_async_copy(out_s, out_ref, sems.at[0]), pltpu.make_async_copy(dx_s, dx_ref, sems.at[1])]
+    copies[0].start()
+    send_ref[0:512, :] = jnp.transpose(normed)
+    send_ref[512:1024, :] = jnp.transpose(att)
 
     def norm_back(raw, grad):
         inv = lax.rsqrt(head_sums(raw * raw, ones) + 1e-06)
@@ -324,22 +329,32 @@
     r = lax.rsqrt(jnp.mean(x * x, axis=-1, keepdims=True) + 1e-06)
     along = jnp.mean(dnormed * x, axis=-1, keepdims=True)
     dx = r * dnormed - x * (r * r * r * along)
-    dx_ref[...] = (own_ref[128:256, :].astype(F32) + dx).astype(BF16)
-
-    features_ref[0:512, :] = jnp.transpose(normed)
-    features_ref[512:1024, :] = jnp.transpose(att)
+    dx_s[...] = (own_ref[128:256, :].astype(F32) + dx).astype(BF16)
+    copies[1].start()
+
     for core in range(2):
 
         @pl.when(my_col % 2 == core)
         def _():
-            for ref, half in ((keep_ref, core), (send_ref, 1 - core)):
-                ref[:, 0:768] = gp_s[:, 768 * half : 768 * half + 768]
-                ref[:, 768:1024] = own_ref[128:256, 256 * half : 256 * half + 256]
-
-
-def grads_kernel(factor, features_ref, keep_ref, got_features_ref, got_ref, out_ref):
-    features = jnp.concatenate([features_ref[...], got_features_ref[...]], axis=1)
-    grads = jnp.concatenate([keep_ref[...], got_ref[...]], axis=0)
+            keep_ref[:, 0:768] = gp_s[:, 768 * core : 768 * core + 768]
+            keep_ref[:, 768:1024] = own_ref[128:256, 256 * core : 256 * core + 256]
+            for j in range(8):
+                at = slice(1024 + 128 * j, 1152 + 128 * j)
+                if j < 6:
+                    lane = 768 * (1 - core) + 128 * j
+                    send_ref[at, :] = gp_s[:, lane : lane + 128]
+                else:
+                    lane = 256 * (1 - core) + 128 * (j - 6)
+                    send_ref[at, :] = own_ref[128:256, lane : lane + 128]
+
+    for copy in copies:
+        copy.wait()
+
+
+def grads_kernel(factor, sent_ref, keep_ref, got_ref, out_ref):
+    features = jnp.concatenate([sent_ref[0:1024, :], got_ref[0:1024, :]], axis=1)
+    got = jnp.concatenate([got_ref[1024 + 128 * j : 1152 + 128 * j, :] for j in range(8)], axis=1)
+    grads = jnp.concatenate([keep_ref[...], got], axis=0)
     out_ref[:, 0:768] = (mm(features[:512], grads[:, :768]) * factor).astype(BF16)
     out_ref[:, 768:1024] = (mm(features[512:], grads[:, 768:]) * factor).astype(BF16)
 
@@ -401,14 +416,18 @@
     )(half_grads, *whole)
 
 
-def call(kernel, outs, scratch=(), flops=0, scalars=0, inputs=0, limit=VMEM_LIMIT):
+def call(kernel, outs, scratch=(), flops=0, scalars=0, inputs=0, unplaced_outs=0, limit=VMEM_LIMIT):
     whole = pl.BlockSpec(memory_space=pltpu.VMEM)
     return pl.pallas_call(
         kernel,
         out_shape=outs,
         in_specs=[pl.BlockSpec(memory_space=pltpu.SMEM)] * scalars
         + [whole] * inputs,
-        out_specs=jax.tree.map(lambda _: whole, outs),
+        out_specs=tuple(
+            pl.BlockSpec(memory_space=pl.ANY) if i < unplaced_outs else whole for i in range(len(outs))
+        )
+        if isinstance(outs, tuple)
+        else whole,
         scratch_shapes=list(scratch),
         compiler_params=pltpu.CompilerParams(vmem_limit_bytes=limit),
         cost_estimate=pl.CostEstimate(flops=flops, bytes_accessed=4 << 20, transcendentals=0),
@@ -461,8 +480,8 @@
     bf = lambda *shape: jax.ShapeDtypeStruct(shape, BF16)
     vm = pltpu.VMEM
     own = jnp.concatenate([x, du], axis=0).reshape(2 * tokens, width)
-    to_c, to_d = call(
-        rows_kernel, (bf(144, width), bf(144, width)), inputs=1, limit=SMALL_LIMIT
+    to_c, to_d, own = call(
+        rows_kernel, (bf(144, width), bf(144, width), bf(256, width)), inputs=1, limit=SMALL_LIMIT
     )(own)
     from_c = swapped(to_c, paired, same)
     from_d = swapped(to_d, across, same)
@@ -488,23 +507,23 @@
         flops=1 << 20, scalars=1, inputs=7,
     )(cosine_logit_gain, own, mate, rows, mate_rows, *weights)
 
-    output, grad_latent, features, send, keep = call(
+    output, grad_latent, send, keep = call(
         main_kernel,
-        (bf(tokens, width), bf(tokens, width), bf(1024, tokens), bf(tokens, 1024), bf(tokens, 1024)),
+        (bf(tokens, width), bf(tokens, width), bf(2048, tokens), bf(tokens, 1024)),
         scratch=[
+            vm((128, 512), BF16), vm((128, 512), BF16), pltpu.SemaphoreType.DMA((2,)),
             vm((160, 512), BF16), vm((160, 512), BF16), vm((112, 512), BF16), vm((112, 512), BF16),
             vm((128, 512), BF16), vm((128, 512), BF16), vm((128, 512), F32), vm((128, 512), F32),
             vm((128, 1536), BF16),
         ],
-        flops=8 << 30, scalars=1, inputs=14,
+        flops=8 << 30, scalars=1, inputs=14, unplaced_outs=2,
     )(cosine_logit_gain, own, far, k, v, q, do, kraw, qraw, normed, *mask, *weights)
 
-    got_features = swapped(features, same, paired)
     got = swapped(send, same, paired)
     factor = 1.0 / math.sqrt(tokens * n_rows * n_cols)
     partial = call(
-        functools.partial(grads_kernel, factor), bf(512, 1024), flops=1 << 29, inputs=4, limit=SMALL_LIMIT
-    )(features, keep, got_features, got)
+        functools.partial(grads_kernel, factor), bf(512, 1024), flops=1 << 29, inputs=3, limit=SMALL_LIMIT
+    )(send, keep, got)
 
     groups = [
         [r * n_cols + 2 * c + core_ for r in range(n_rows) for c in range(n_cols // 2)]

time: 91.6 us -> 90.9 us (level)
    ppermute x8 -> x7, waiting for transfers between devices: 3.91 us -> 3.43 us  [swapped(): return lax.ppermute(value, AXES, pairs)]
    ppermute x8 -> x7, starting transfers between devices: 14.6 us -> 14.3 us  [swapped(): return lax.ppermute(value, AXES, pairs)]
  transfers between devices with their start and end apart: 8 -> 7, of which waited for: 5 -> 3; matrix products, arithmetic and copies ran while one was open for 1% -> 1% of each run, Pallas kernels for 6% -> 7%
where the time goes in v6:
time: 90.9 us; the launch traced here: 90.6 us
  blocking collectives  51.8 us (57%)
  Pallas kernels  16.7 us (18%)
  starting transfers between devices  14.3 us (16%)
  waiting for transfers between devices  3.43 us (4%)
  between operations  2.29 us (3%)
  other arithmetic  1.09 us (1%)
    all_to_all x2, blocking collectives, exchange(): lax.all_to_all(value.reshape(members, each, 1024), AXES, 0, 0, axis_index...  51.8 us
    ppermute x7, starting transfers between devices, swapped(): return lax.ppermute(value, AXES, pairs)  14.3 us
    pallas_call x1, Pallas kernels, per_device(): call(main_kernel, (bf(tokens, width), bf(tokens, width), bf(2048, tokens)...  8.45 us
    pallas_call x1, Pallas kernels, per_device(): call(near_kernel, (bf(480, width), bf(480, width), bf(336, width), bf(336...  4.14 us
    ppermute x7, waiting for transfers between devices, swapped(): return lax.ppermute(value, AXES, pairs)  3.43 us
    pallas_call x2, Pallas kernels, write_half(): pl.pallas_call(functools.partial(final_kernel, mine), in_specs=[pl.BlockS...  2.89 us
  transfers between devices with their start and end apart: 7, of which 3 were waited for; matrix products, arithmetic and copies ran while one was open for 1% of the time, Pallas kernels for 7%

profile of v6, /device:TPU:1, one launch (start us, length us, event | category | flops | bytes accessed | tf_op | source)
XLA Modules:
  0.0 90.6 jit_solution(18033529880271851897)
XLA Ops:
  0.6 0.0 copy-start
  0.6 1.0 %pad_maximum_fusion = bf16[16,16,512]{2,1,0:T(8,128)(2,1)S(1)} fusion(bf16[8,16,512]{2,1,0:T(8,128)(2,1)} %param.10, bf16[8,16,512]{2,1,0:T(8,128)(2,1)} %param.9), kind=kLoop, calls=%fused_computation.1 | loop fusion | flops 131072 | bytes 524288 | tf_op jit(solution)/shard_map/concatenate | solution.py:482
  1.7 4.5 %collective-permute-start = (bf16[144,512]{1,0:T(8,128)(2,1)S(1)}, bf16[144,512]{1,0:T(8,128)(2,1)S(1)}, u32[]{:S(2)}, u32[]{:S(2)}) collective-permute-start(bf16[144,512]{1,0:T(8,128)(2,1)S(1)} %get-tuple-element.27), channel_id=1, source_target_pairs={{0,16},{1,17},{2,18},{3,19},{4,20},{5,21},{6,22},{7,23},{8,24},{9,... | collective-permute-start | bytes 442376 | tf_op jit(solution)/shard_map/ppermute | solution.py:456
  6.2 0.7 collective-permute-start.1
  6.9 1.0 %collective-permute-start.2 = (bf16[256,512]{1,0:T(8,128)(2,1)S(1)}, bf16[256,512]{1,0:T(8,128)(2,1)S(1)}, u32[]{:S(2)}, u32[]{:S(2)}) collective-permute-start(bf16[256,512]{1,0:T(8,128)(2,1)S(1)} %get-tuple-element.26.own_ref), channel_id=1, source_target_pairs={{0,1},{1,0},{2,3},{3,2},{4,5},{5,4},{6,7},{7,6},{8,9},{9,8},{10,11... | collective-permute-start | bytes 786440 | tf_op jit(solution)/shard_map/ppermute | solution.py:456
  8.6 0.1 sine_convert_fusion
  8.7 0.3 shard_map.121
  9.6 0.0 copy-done
  9.7 0.8 convolution_add_fusion._scale.scale_ref
  10.5 0.0 collective-permute-done.c_ref
  10.5 0.0 collective-permute-done.1.d_ref
  10.5 0.0 collective-permute-done.2._mate.mate_ref
  10.5 0.0 copy-start.1
  10.5 0.0 copy-start.2
  10.5 0.0 copy-start.3
  10.6 0.2 shard_map.122
  10.8 3.1 %collective-permute-start.4 = (bf16[288,512]{1,0:T(8,128)(2,1)S(1)}, bf16[288,512]{1,0:T(8,128)(2,1)S(1)}, u32[]{:S(2)}, u32[]{:S(2)}) collective-permute-start(bf16[288,512]{1,0:T(8,128)(2,1)S(1)} %get-tuple-element.32.rows_ref), channel_id=1, source_target_pairs={{0,1},{1,0},{2,3},{3,2},{4,5},{5,4},{6,7},{7,6},{8,9},{9,8},{10,11... | collective-permute-start | bytes 884744 | tf_op jit(solution)/shard_map/ppermute | solution.py:456
  13.8 1.9 %collective-permute-start.3 = (bf16[176,512]{1,0:T(8,128)(2,1)S(1)}, bf16[176,512]{1,0:T(8,128)(2,1)S(1)}, u32[]{:S(2)}, u32[]{:S(2)}) collective-permute-start(bf16[176,512]{1,0:T(8,128)(2,1)S(1)} %get-tuple-element.31), channel_id=1, source_target_pairs={{1,2},{2,1},{3,4},{4,3},{5,6},{6,5},{7,8},{8,7},{9,10},{10,9},{11,... | collective-permute-start | bytes 540680 | tf_op jit(solution)/shard_map/ppermute | solution.py:456
  15.7 0.0 collective-permute-done.4.mate_rows_ref
  15.7 0.0 copy-done.1
  15.7 0.0 copy-done.2
  15.8 0.0 copy-done.3
  15.8 4.1 %shard_map.123 = (bf16[480,512]{1,0:T(8,128)(2,1)S(1)}, bf16[480,512]{1,0:T(8,128)(2,1)S(1)}, bf16[336,512]{1,0:T(8,128)(2,1)S(1)}, bf16[336,512]{1,0:T(8,128)(2...) custom-call(f32[8]{0:T(128)S(1)} %copy-done.3, ...), custom_call_target="tpu_custom_call" | custom-call | flops 1048576 | bytes 4194304 | tf_op jit(solution)/shard_map/pallas_call | solution.py:503
  19.9 0.7 collective-permute-done.3.far_ref
  20.6 8.4 %shard_map.124 = (bf16[128,512]{1,0:T(8,128)(2,1)}, bf16[128,512]{1,0:T(8,128)(2,1)}, bf16[2048,128]{1,0:T(8,128)(2,1)S(1)}, bf16[128,1024]{1,0:T(8,128)(2,1)S(1)}) custom-call(f32[8]{0:T(128)S(1)} %copy-done.3, bf16[256,512]{1,0:T(8,128)(2,1)S(1)} %get-tuple-element.26.own_ref, bf16[176,512]{1,0:T(8,128)(2,1)S(1)} %collective-permute-done.3.far_ref, ...), custom_call_target="tpu_custom_call" | custom-call | flops 8589934592 | bytes 4194304 | tf_op jit(solution)/shard_map/pallas_call | solution.py:510
  29.1 0.1 collective-permute-start.5
  29.2 1.9 %collective-permute-done.5.got_ref = bf16[2048,128]{1,0:T(8,128)(2,1)S(1)} collective-permute-done((bf16[2048,128]{1,0:T(8,128)(2,1)S(1)}, bf16[2048,128]{1,0:T(8,128)(2,1)S(1)}, u32[]{:S(2)}, u32[]{:S(2)}) %collective-permute-start.5) | collective-permute-done | bytes 524320 | tf_op jit(solution)/shard_map/ppermute | solution.py:456
  31.1 0.4 shard_map.125
  31.5 30.7 %all_to_all.10 = bf16[64,8,1024]{2,1,0:T(8,128)(2,1)S(1)} all-to-all(bf16[64,8,1024]{2,1,0:T(8,128)(2,1)S(1)} %bitcast.17), channel_id=1, replica_groups={{0,2,4,6,8,10,12,14,16,18,20,22,24,26,28,30,32,34,36,38,40,42,44,46,48,..., dimensions={0} | all-to-all | bytes 2097152 | tf_op jit(solution)/shard_map/all_to_all | solution.py:536
  62.2 0.2 shard_map.126
  62.4 21.2 %all_to_all.11 = bf16[64,8,1024]{2,1,0:T(8,128)(2,1)S(1)} all-to-all(bf16[64,8,1024]{2,1,0:T(8,128)(2,1)S(1)} %bitcast.19), channel_id=1, replica_groups={{0,2,4,6,8,10,12,14,16,18,20,22,24,26,28,30,32,34,36,38,40,42,44,46,48,..., dimensions={0} | all-to-all | bytes 2097152 | tf_op jit(solution)/shard_map/all_to_all | solution.py:536
  83.6 3.1 %collective-permute-start.6 = (bf16[512,1024]{1,0:T(8,128)(2,1)S(1)}, bf16[512,1024]{1,0:T(8,128)(2,1)S(1)}, u32[]{:S(2)}, u32[]{:S(2)}) collective-permute-start(bf16[512,1024]{1,0:T(8,128)(2,1)S(1)} %bitcast.15), channel_id=1, source_target_pairs={{0,1},{1,0},{2,3},{3,2},{4,5},{5,4},{6,7},{7,6},{8,9},{9,8},{10,11... | collective-permute-start | bytes 3145736 | tf_op jit(solution)/shard_map/ppermute | solution.py:456
  86.7 1.4 %shard_map.127 = (f32[512,1536]{1,0:T(8,128)}, f32[512,512]{1,0:T(8,128)}) custom-call(bf16[512,1024]{1,0:T(8,128)(2,1)S(1)} %bitcast.16), custom_call_target="tpu_custom_call" | custom-call | flops 1048576 | bytes 3145728 | tf_op jit(solution)/shard_map/pallas_call | solution.py:402
  88.1 0.8 collective-permute-done.6.grads_ref
  89.0 1.4 %shard_map.128 = (f32[512,1536]{1,0:T(8,128)}, f32[512,512]{1,0:T(8,128)}) custom-call(bf16[512,1024]{1,0:T(8,128)(2,1)S(1)} %collective-permute-done.6.grads_ref, f32[512,1536]{1,0:T(8,128)} %get-tuple-element.44.refs_0_, f32[512,512]{1,0:T(8,128)} %get-tuple-element.45.refs_1_), custom_call_target="tpu_custom_call", output_to_operand_aliasing={{0}: (1, {}), {1}: (2, {})} | custom-call | flops 1048576 | bytes 3145728 | tf_op jit(solution)/shard_map/pallas_call | solution.py:402
  (3 shorter events, 0.1 us)
Async XLA Ops:
  0.6 9.0 %copy-start = (bf16[256,512]{1,0:T(8,128)(2,1)S(1)}, bf16[256,512]{1,0:T(8,128)(2,1)}, u32[]{:S(2)}) copy-start(bf16[256,512]{1,0:T(8,128)(2,1)} %param.14) | copy-start | bytes 786436
  1.7 8.8 %collective-permute-start = (bf16[144,512]{1,0:T(8,128)(2,1)S(1)}, bf16[144,512]{1,0:T(8,128)(2,1)S(1)}, u32[]{:S(2)}, u32[]{:S(2)}) collective-permute-start(bf16[144,512]{1,0:T(8,128)(2,1)S(1)} %get-tuple-element.27), channel_id=1, source_target_pairs={{0,16},{1,17},{2,18},{3,19},{4,20},{5,21},{6,22},{7,23},{8,24},{9,... | collective-permute-start | bytes 442376 | tf_op jit(solution)/shard_map/ppermute | solution.py:456
  6.2 4.3 %collective-permute-start.1 = (bf16[144,512]{1,0:T(8,128)(2,1)S(1)}, bf16[144,512]{1,0:T(8,128)(2,1)S(1)}, u32[]{:S(2)}, u32[]{:S(2)}) collective-permute-start(bf16[144,512]{1,0:T(8,128)(2,1)S(1)} %get-tuple-element.28), channel_id=1, source_target_pairs={{16,32},{17,33},{18,34},{19,35},{20,36},{21,37},{22,38},{23,39},{2... | collective-permute-start | bytes 442376 | tf_op jit(solution)/shard_map/ppermute | solution.py:456
  6.9 3.6 %collective-permute-start.2 = (bf16[256,512]{1,0:T(8,128)(2,1)S(1)}, bf16[256,512]{1,0:T(8,128)(2,1)S(1)}, u32[]{:S(2)}, u32[]{:S(2)}) collective-permute-start(bf16[256,512]{1,0:T(8,128)(2,1)S(1)} %get-tuple-element.26.own_ref), channel_id=1, source_target_pairs={{0,1},{1,0},{2,3},{3,2},{4,5},{5,4},{6,7},{7,6},{8,9},{9,8},{10,11... | collective-permute-start | bytes 786440 | tf_op jit(solution)/shard_map/ppermute | solution.py:456
  10.5 5.2 %copy-start.1 = (bf16[512,1536]{1,0:T(8,128)(2,1)S(1)}, bf16[512,1536]{1,0:T(8,128)(2,1)}, u32[]{:S(2)}) copy-start(bf16[512,1536]{1,0:T(8,128)(2,1)} %win_ref.3) | copy-start | bytes 4718596
  10.5 5.2 %copy-start.2 = (bf16[512,512]{1,0:T(8,128)(2,1)S(1)}, bf16[512,512]{1,0:T(8,128)(2,1)}, u32[]{:S(2)}) copy-start(bf16[512,512]{1,0:T(8,128)(2,1)} %wo_ref.3) | copy-start | bytes 1572868
  10.5 5.2 %copy-start.3 = (f32[8]{0:T(128)S(1)}, f32[8]{0:T(128)}, u32[]{:S(2)}) copy-start(f32[8]{0:T(128)} %gain_ref.3) | copy-start | bytes 100
  10.8 5.0 %collective-permute-start.4 = (bf16[288,512]{1,0:T(8,128)(2,1)S(1)}, bf16[288,512]{1,0:T(8,128)(2,1)S(1)}, u32[]{:S(2)}, u32[]{:S(2)}) collective-permute-start(bf16[288,512]{1,0:T(8,128)(2,1)S(1)} %get-tuple-element.32.rows_ref), channel_id=1, source_target_pairs={{0,1},{1,0},{2,3},{3,2},{4,5},{5,4},{6,7},{7,6},{8,9},{9,8},{10,11... | collective-permute-start | bytes 884744 | tf_op jit(solution)/shard_map/ppermute | solution.py:456
  13.8 6.8 %collective-permute-start.3 = (bf16[176,512]{1,0:T(8,128)(2,1)S(1)}, bf16[176,512]{1,0:T(8,128)(2,1)S(1)}, u32[]{:S(2)}, u32[]{:S(2)}) collective-permute-start(bf16[176,512]{1,0:T(8,128)(2,1)S(1)} %get-tuple-element.31), channel_id=1, source_target_pairs={{1,2},{2,1},{3,4},{4,3},{5,6},{6,5},{7,8},{8,7},{9,10},{10,9},{11,... | collective-permute-start | bytes 540680 | tf_op jit(solution)/shard_map/ppermute | solution.py:456
  29.1 2.0 %collective-permute-start.5 = (bf16[2048,128]{1,0:T(8,128)(2,1)S(1)}, bf16[2048,128]{1,0:T(8,128)(2,1)S(1)}, u32[]{:S(2)}, u32[]{:S(2)}) collective-permute-start(bf16[2048,128]{1,0:T(8,128)(2,1)S(1)} %get-tuple-element.42.sent_ref), channel_id=1, source_target_pairs={{0,1},{1,0},{2,3},{3,2},{4,5},{5,4},{6,7},{7,6},{8,9},{9,8},{10,11... | collective-permute-start | bytes 1572872 | tf_op jit(solution)/shard_map/ppermute | solution.py:456
  83.6 5.4 %collective-permute-start.6 = (bf16[512,1024]{1,0:T(8,128)(2,1)S(1)}, bf16[512,1024]{1,0:T(8,128)(2,1)S(1)}, u32[]{:S(2)}, u32[]{:S(2)}) collective-permute-start(bf16[512,1024]{1,0:T(8,128)(2,1)S(1)} %bitcast.15), channel_id=1, source_target_pairs={{0,1},{1,0},{2,3},{3,2},{4,5},{5,4},{6,7},{7,6},{8,9},{9,8},{10,11... | collective-permute-start | bytes 3145736 | tf_op jit(solution)/shard_map/ppermute | solution.py:456

commit v7 on v6

--- a/solution.py
+++ b/solution.py
@@ -373,7 +373,7 @@
         out_ref[step * i : step * (i + 1), :] = block
 
 
-def final_kernel(mine, grads_ref, *refs):
+def final_kernel(mine, first, grads_ref, *refs):
     qkv_ref, out_ref, qkv_s, out_s, sems = refs[-5:]
     steps = sems.shape[1]
     rows = grads_ref.shape[0] // steps
@@ -387,20 +387,21 @@
                 part = slice(rows * i, rows * (i + 1))
                 qkv_s[part, :] = grads_ref[part, 0:768].astype(F32)
                 out_s[part, :] = grads_ref[part, 768:1024].astype(F32)
+                there = slice(first + rows * i, first + rows * (i + 1))
                 lanes = slice(768 * half, 768 * half + 768)
-                copies.append(pltpu.make_async_copy(qkv_s.at[part], qkv_ref.at[part, lanes], sems.at[0, i]))
+                copies.append(pltpu.make_async_copy(qkv_s.at[part], qkv_ref.at[there, lanes], sems.at[0, i]))
                 lanes = slice(256 * half, 256 * half + 256)
-                copies.append(pltpu.make_async_copy(out_s.at[part], out_ref.at[part, lanes], sems.at[1, i]))
+                copies.append(pltpu.make_async_copy(out_s.at[part], out_ref.at[there, lanes], sems.at[1, i]))
                 copies[-2].start()
                 copies[-1].start()
             for copy in copies:
                 copy.wait()
 
 
-def write_half(mine, half_grads, *whole):
+def write_half(mine, first, half_grads, *whole):
     unplaced = pl.BlockSpec(memory_space=pl.ANY)
     return pl.pallas_call(
-        functools.partial(final_kernel, mine),
+        functools.partial(final_kernel, mine, first),
         in_specs=[pl.BlockSpec(memory_space=pltpu.VMEM)] + [unplaced] * len(whole),
         out_specs=[unplaced, unplaced],
         out_shape=[
@@ -541,8 +542,10 @@
         functools.partial(sum_kernel, each), bf(512, 1024), inputs=1, limit=SMALL_LIMIT
     )(exchange(partial))
     mine = exchange(summed)
-    other = swapped(mine, same, paired)
-    qkv_grad, out_grad = write_half(False, other, *write_half(True, mine))
+    upper, lower = swapped(mine[:256], same, paired), swapped(mine[256:], same, paired)
+    grads = write_half(True, 0, mine)
+    grads = write_half(False, 0, upper, *grads)
+    qkv_grad, out_grad = write_half(False, 256, lower, *grads)
     return output.reshape(x.shape), grad_latent.reshape(x.shape), qkv_grad, out_grad
 
 

time: 90.9 us -> 91.1 us (level)
    ppermute x7 -> x8, waiting for transfers between devices: 3.43 us -> 2.61 us  [swapped(): return lax.ppermute(value, AXES, pairs)]
    pallas_call x2 -> x3, Pallas kernels: 2.89 us -> 3.68 us  [write_half(): pl.pallas_call(functools.partial(final_kernel, mine, first), in_specs=[pl...]
    ppermute x7 -> x8, starting transfers between devices: 14.3 us -> 14.5 us  [swapped(): return lax.ppermute(value, AXES, pairs)]
  transfers between devices with their start and end apart: 7 -> 8, of which waited for: 3 -> 2; matrix products, arithmetic and copies ran while one was open for 1% -> 1% of each run, Pallas kernels for 7% -> 8%
where the time goes in v7:
time: 91.1 us; the launch traced here: 90.8 us
  blocking collectives  51.8 us (57%)
  Pallas kernels  17.5 us (19%)
  starting transfers between devices  14.5 us (16%)
  waiting for transfers between devices  2.61 us (3%)
  between operations  2.32 us (3%)
  other arithmetic  1.09 us (1%)
    all_to_all x2, blocking collectives, exchange(): lax.all_to_all(value.reshape(members, each, 1024), AXES, 0, 0, axis_index...  51.8 us
    ppermute x8, starting transfers between devices, swapped(): return lax.ppermute(value, AXES, pairs)  14.5 us
    pallas_call x1, Pallas kernels, per_device(): call(main_kernel, (bf(tokens, width), bf(tokens, width), bf(2048, tokens)...  8.45 us
    pallas_call x1, Pallas kernels, per_device(): call(near_kernel, (bf(480, width), bf(480, width), bf(336, width), bf(336...  4.14 us
    pallas_call x3, Pallas kernels, write_half(): pl.pallas_call(functools.partial(final_kernel, mine, first), in_specs=[pl...  3.68 us
    ppermute x8, waiting for transfers between devices, swapped(): return lax.ppermute(value, AXES, pairs)  2.61 us
  transfers between devices with their start and end apart: 8, of which 2 were waited for; matrix products, arithmetic and copies ran while one was open for 1% of the time, Pallas kernels for 8%

profile of v7, /device:TPU:1, one launch (start us, length us, event | category | flops | bytes accessed | tf_op | source)
XLA Modules:
  0.0 90.8 jit_solution(2825720774598506636)
XLA Ops:
  0.6 0.0 copy-start
  0.6 1.0 %pad_maximum_fusion = bf16[16,16,512]{2,1,0:T(8,128)(2,1)S(1)} fusion(bf16[8,16,512]{2,1,0:T(8,128)(2,1)} %param.10, bf16[8,16,512]{2,1,0:T(8,128)(2,1)} %param.9), kind=kLoop, calls=%fused_computation.3 | loop fusion | flops 131072 | bytes 524288 | tf_op jit(solution)/shard_map/concatenate | solution.py:483
  1.7 4.5 %collective-permute-start = (bf16[144,512]{1,0:T(8,128)(2,1)S(1)}, bf16[144,512]{1,0:T(8,128)(2,1)S(1)}, u32[]{:S(2)}, u32[]{:S(2)}) collective-permute-start(bf16[144,512]{1,0:T(8,128)(2,1)S(1)} %get-tuple-element.29), channel_id=1, source_target_pairs={{0,16},{1,17},{2,18},{3,19},{4,20},{5,21},{6,22},{7,23},{8,24},{9,... | collective-permute-start | bytes 442376 | tf_op jit(solution)/shard_map/ppermute | solution.py:457
  6.2 0.7 collective-permute-start.1
  6.9 1.0 %collective-permute-start.2 = (bf16[256,512]{1,0:T(8,128)(2,1)S(1)}, bf16[256,512]{1,0:T(8,128)(2,1)S(1)}, u32[]{:S(2)}, u32[]{:S(2)}) collective-permute-start(bf16[256,512]{1,0:T(8,128)(2,1)S(1)} %get-tuple-element.28.own_ref), channel_id=1, source_target_pairs={{0,1},{1,0},{2,3},{3,2},{4,5},{5,4},{6,7},{7,6},{8,9},{9,8},{10,11... | collective-permute-start | bytes 786440 | tf_op jit(solution)/shard_map/ppermute | solution.py:457
  8.6 0.1 sine_convert_fusion
  8.7 0.3 shard_map.121
  9.6 0.0 copy-done
  9.7 0.8 convolution_add_fusion._scale.scale_ref
  10.5 0.0 collective-permute-done.c_ref
  10.5 0.0 collective-permute-done.1.d_ref
  10.5 0.0 collective-permute-done.2._mate.mate_ref
  10.5 0.0 copy-start.1
  10.5 0.0 copy-start.2
  10.5 0.0 copy-start.3
  10.6 0.2 shard_map.122
  10.8 3.1 %collective-permute-start.4 = (bf16[288,512]{1,0:T(8,128)(2,1)S(1)}, bf16[288,512]{1,0:T(8,128)(2,1)S(1)}, u32[]{:S(2)}, u32[]{:S(2)}) collective-permute-start(bf16[288,512]{1,0:T(8,128)(2,1)S(1)} %get-tuple-element.34.rows_ref), channel_id=1, source_target_pairs={{0,1},{1,0},{2,3},{3,2},{4,5},{5,4},{6,7},{7,6},{8,9},{9,8},{10,11... | collective-permute-start | bytes 884744 | tf_op jit(solution)/shard_map/ppermute | solution.py:457
  13.8 1.9 %collective-permute-start.3 = (bf16[176,512]{1,0:T(8,128)(2,1)S(1)}, bf16[176,512]{1,0:T(8,128)(2,1)S(1)}, u32[]{:S(2)}, u32[]{:S(2)}) collective-permute-start(bf16[176,512]{1,0:T(8,128)(2,1)S(1)} %get-tuple-element.33), channel_id=1, source_target_pairs={{1,2},{2,1},{3,4},{4,3},{5,6},{6,5},{7,8},{8,7},{9,10},{10,9},{11,... | collective-permute-start | bytes 540680 | tf_op jit(solution)/shard_map/ppermute | solution.py:457
  15.7 0.0 collective-permute-done.4.mate_rows_ref
  15.7 0.0 copy-done.1
  15.7 0.0 copy-done.2
  15.8 0.0 copy-done.3
  15.8 4.1 %shard_map.123 = (bf16[480,512]{1,0:T(8,128)(2,1)S(1)}, bf16[480,512]{1,0:T(8,128)(2,1)S(1)}, bf16[336,512]{1,0:T(8,128)(2,1)S(1)}, bf16[336,512]{1,0:T(8,128)(2...) custom-call(f32[8]{0:T(128)S(1)} %copy-done.3, ...), custom_call_target="tpu_custom_call" | custom-call | flops 1048576 | bytes 4194304 | tf_op jit(solution)/shard_map/pallas_call | solution.py:504
  19.9 0.7 collective-permute-done.3.far_ref
  20.6 8.4 %shard_map.124 = (bf16[128,512]{1,0:T(8,128)(2,1)}, bf16[128,512]{1,0:T(8,128)(2,1)}, bf16[2048,128]{1,0:T(8,128)(2,1)S(1)}, bf16[128,1024]{1,0:T(8,128)(2,1)S(1)}) custom-call(f32[8]{0:T(128)S(1)} %copy-done.3, bf16[256,512]{1,0:T(8,128)(2,1)S(1)} %get-tuple-element.28.own_ref, bf16[176,512]{1,0:T(8,128)(2,1)S(1)} %collective-permute-done.3.far_ref, ...), custom_call_target="tpu_custom_call" | custom-call | flops 8589934592 | bytes 4194304 | tf_op jit(solution)/shard_map/pallas_call | solution.py:511
  29.1 0.1 collective-permute-start.5
  29.2 1.9 %collective-permute-done.5.got_ref = bf16[2048,128]{1,0:T(8,128)(2,1)S(1)} collective-permute-done((bf16[2048,128]{1,0:T(8,128)(2,1)S(1)}, bf16[2048,128]{1,0:T(8,128)(2,1)S(1)}, u32[]{:S(2)}, u32[]{:S(2)}) %collective-permute-start.5) | collective-permute-done | bytes 524320 | tf_op jit(solution)/shard_map/ppermute | solution.py:457
  31.1 0.4 shard_map.125
  31.5 30.7 %all_to_all.10 = bf16[64,8,1024]{2,1,0:T(8,128)(2,1)S(1)} all-to-all(bf16[64,8,1024]{2,1,0:T(8,128)(2,1)S(1)} %bitcast.20), channel_id=1, replica_groups={{0,2,4,6,8,10,12,14,16,18,20,22,24,26,28,30,32,34,36,38,40,42,44,46,48,..., dimensions={0} | all-to-all | bytes 2097152 | tf_op jit(solution)/shard_map/all_to_all | solution.py:537
  62.2 0.2 shard_map.126
  62.4 21.2 %all_to_all.11 = bf16[64,8,1024]{2,1,0:T(8,128)(2,1)S(1)} all-to-all(bf16[64,8,1024]{2,1,0:T(8,128)(2,1)S(1)} %bitcast.22), channel_id=1, replica_groups={{0,2,4,6,8,10,12,14,16,18,20,22,24,26,28,30,32,34,36,38,40,42,44,46,48,..., dimensions={0} | all-to-all | bytes 2097152 | tf_op jit(solution)/shard_map/all_to_all | solution.py:537
  83.6 0.1 slice_bitcast_fusion
  83.6 3.2 %collective-permute-start.7 = (bf16[256,1024]{1,0:T(8,128)(2,1)S(1)}, bf16[256,1024]{1,0:T(8,128)(2,1)S(1)}, u32[]{:S(2)}, u32[]{:S(2)}) collective-permute-start(bf16[256,1024]{1,0:T(8,128)(2,1)S(1)} %get-tuple-element.52), channel_id=1, source_target_pairs={{0,1},{1,0},{2,3},{3,2},{4,5},{5,4},{6,7},{7,6},{8,9},{9,8},{10,11... | collective-permute-start | bytes 1572872 | tf_op jit(solution)/shard_map/ppermute | solution.py:457
  86.8 0.1 collective-permute-start.6
  86.9 1.4 %shard_map.127 = (f32[512,1536]{1,0:T(8,128)}, f32[512,512]{1,0:T(8,128)}) custom-call(bf16[512,1024]{1,0:T(8,128)(2,1)S(1)} %bitcast.19), custom_call_target="tpu_custom_call" | custom-call | flops 1048576 | bytes 3145728 | tf_op jit(solution)/shard_map/pallas_call | solution.py:403
  88.4 0.0 collective-permute-done.7.grads_ref
  88.4 1.1 %shard_map.128 = (f32[512,1536]{1,0:T(8,128)}, f32[512,512]{1,0:T(8,128)}) custom-call(bf16[256,1024]{1,0:T(8,128)(2,1)S(1)} %collective-permute-done.7.grads_ref, f32[512,1536]{1,0:T(8,128)} %get-tuple-element.46.refs_0_, f32[512,512]{1,0:T(8,128)} %get-tuple-element.47.refs_1_), custom_call_target="tpu_custom_call", output_to_operand_aliasing={{0}: (1, {}), {1}: (2, {})} | custom-call | flops 1048576 | bytes 3145728 | tf_op jit(solution)/shard_map/pallas_call | solution.py:403
  89.5 0.0 collective-permute-done.6.grads_ref
  89.5 1.1 %shard_map.129 = (f32[512,1536]{1,0:T(8,128)}, f32[512,512]{1,0:T(8,128)}) custom-call(bf16[256,1024]{1,0:T(8,128)(2,1)S(1)} %collective-permute-done.6.grads_ref, f32[512,1536]{1,0:T(8,128)} %get-tuple-element.48.refs_0_, f32[512,512]{1,0:T(8,128)} %get-tuple-element.49.refs_1_), custom_call_target="tpu_custom_call", output_to_operand_aliasing={{0}: (1, {}), {1}: (2, {})} | custom-call | flops 1048576 | bytes 3145728 | tf_op jit(solution)/shard_map/pallas_call | solution.py:403
  (3 shorter events, 0.1 us)
Async XLA Ops:
  0.6 9.0 %copy-start = (bf16[256,512]{1,0:T(8,128)(2,1)S(1)}, bf16[256,512]{1,0:T(8,128)(2,1)}, u32[]{:S(2)}) copy-start(bf16[256,512]{1,0:T(8,128)(2,1)} %param.14) | copy-start | bytes 786436
  1.7 8.8 %collective-permute-start = (bf16[144,512]{1,0:T(8,128)(2,1)S(1)}, bf16[144,512]{1,0:T(8,128)(2,1)S(1)}, u32[]{:S(2)}, u32[]{:S(2)}) collective-permute-start(bf16[144,512]{1,0:T(8,128)(2,1)S(1)} %get-tuple-element.29), channel_id=1, source_target_pairs={{0,16},{1,17},{2,18},{3,19},{4,20},{5,21},{6,22},{7,23},{8,24},{9,... | collective-permute-start | bytes 442376 | tf_op jit(solution)/shard_map/ppermute | solution.py:457
  6.2 4.3 %collective-permute-start.1 = (bf16[144,512]{1,0:T(8,128)(2,1)S(1)}, bf16[144,512]{1,0:T(8,128)(2,1)S(1)}, u32[]{:S(2)}, u32[]{:S(2)}) collective-permute-start(bf16[144,512]{1,0:T(8,128)(2,1)S(1)} %get-tuple-element.30), channel_id=1, source_target_pairs={{16,32},{17,33},{18,34},{19,35},{20,36},{21,37},{22,38},{23,39},{2... | collective-permute-start | bytes 442376 | tf_op jit(solution)/shard_map/ppermute | solution.py:457
  6.9 3.6 %collective-permute-start.2 = (bf16[256,512]{1,0:T(8,128)(2,1)S(1)}, bf16[256,512]{1,0:T(8,128)(2,1)S(1)}, u32[]{:S(2)}, u32[]{:S(2)}) collective-permute-start(bf16[256,512]{1,0:T(8,128)(2,1)S(1)} %get-tuple-element.28.own_ref), channel_id=1, source_target_pairs={{0,1},{1,0},{2,3},{3,2},{4,5},{5,4},{6,7},{7,6},{8,9},{9,8},{10,11... | collective-permute-start | bytes 786440 | tf_op jit(solution)/shard_map/ppermute | solution.py:457
  10.5 5.2 %copy-start.1 = (bf16[512,1536]{1,0:T(8,128)(2,1)S(1)}, bf16[512,1536]{1,0:T(8,128)(2,1)}, u32[]{:S(2)}) copy-start(bf16[512,1536]{1,0:T(8,128)(2,1)} %win_ref.3) | copy-start | bytes 4718596
  10.5 5.2 %copy-start.2 = (bf16[512,512]{1,0:T(8,128)(2,1)S(1)}, bf16[512,512]{1,0:T(8,128)(2,1)}, u32[]{:S(2)}) copy-start(bf16[512,512]{1,0:T(8,128)(2,1)} %wo_ref.3) | copy-start | bytes 1572868
  10.5 5.2 %copy-start.3 = (f32[8]{0:T(128)S(1)}, f32[8]{0:T(128)}, u32[]{:S(2)}) copy-start(f32[8]{0:T(128)} %gain_ref.3) | copy-start | bytes 100
  10.8 5.0 %collective-permute-start.4 = (bf16[288,512]{1,0:T(8,128)(2,1)S(1)}, bf16[288,512]{1,0:T(8,128)(2,1)S(1)}, u32[]{:S(2)}, u32[]{:S(2)}) collective-permute-start(bf16[288,512]{1,0:T(8,128)(2,1)S(1)} %get-tuple-element.34.rows_ref), channel_id=1, source_target_pairs={{0,1},{1,0},{2,3},{3,2},{4,5},{5,4},{6,7},{7,6},{8,9},{9,8},{10,11... | collective-permute-start | bytes 884744 | tf_op jit(solution)/shard_map/ppermute | solution.py:457
  13.8 6.8 %collective-permute-start.3 = (bf16[176,512]{1,0:T(8,128)(2,1)S(1)}, bf16[176,512]{1,0:T(8,128)(2,1)S(1)}, u32[]{:S(2)}, u32[]{:S(2)}) collective-permute-start(bf16[176,512]{1,0:T(8,128)(2,1)S(1)} %get-tuple-element.33), channel_id=1, source_target_pairs={{1,2},{2,1},{3,4},{4,3},{5,6},{6,5},{7,8},{8,7},{9,10},{10,9},{11,... | collective-permute-start | bytes 540680 | tf_op jit(solution)/shard_map/ppermute | solution.py:457
  29.1 2.0 %collective-permute-start.5 = (bf16[2048,128]{1,0:T(8,128)(2,1)S(1)}, bf16[2048,128]{1,0:T(8,128)(2,1)S(1)}, u32[]{:S(2)}, u32[]{:S(2)}) collective-permute-start(bf16[2048,128]{1,0:T(8,128)(2,1)S(1)} %get-tuple-element.44.sent_ref), channel_id=1, source_target_pairs={{0,1},{1,0},{2,3},{3,2},{4,5},{5,4},{6,7},{7,6},{8,9},{9,8},{10,11... | collective-permute-start | bytes 1572872 | tf_op jit(solution)/shard_map/ppermute | solution.py:457
  83.6 4.7 %collective-permute-start.7 = (bf16[256,1024]{1,0:T(8,128)(2,1)S(1)}, bf16[256,1024]{1,0:T(8,128)(2,1)S(1)}, u32[]{:S(2)}, u32[]{:S(2)}) collective-permute-start(bf16[256,1024]{1,0:T(8,128)(2,1)S(1)} %get-tuple-element.52), channel_id=1, source_target_pairs={{0,1},{1,0},{2,3},{3,2},{4,5},{5,4},{6,7},{7,6},{8,9},{9,8},{10,11... | collective-permute-start | bytes 1572872 | tf_op jit(solution)/shard_map/ppermute | solution.py:457
  86.8 2.7 %collective-permute-start.6 = (bf16[256,1024]{1,0:T(8,128)(2,1)S(1)}, bf16[256,1024]{1,0:T(8,128)(2,1)S(1)}, u32[]{:S(2)}, u32[]{:S(2)}) collective-permute-start(bf16[256,1024]{1,0:T(8,128)(2,1)S(1)} %get-tuple-element.53), channel_id=1, source_target_pairs={{0,1},{1,0},{2,3},{3,2},{4,5},{5,4},{6,7},{7,6},{8,9},{9,8},{10,11... | collective-permute-start | bytes 1572872 | tf_op jit(solution)/shard_map/ppermute | solution.py:457
